TPU v7x, 32 devices: a whole 2x2x4 slice. The times are simulated.
32 devices in a mesh: rep: 4 (over y, core), grp: 8 (over z, x).
Axes of the slice: x: 2, y: 2, z: 4, core: 2. Of those that a mesh axis runs over, the one named last changes fastest.
Arguments:
- tokens: bfloat16 [4096, 1536], P(('rep', 'grp')), may hold values from -6 to 6
- attn_gain: bfloat16 [1536], P('grp'), may hold values from 0.5 to 1.5
- w_qkv: bfloat16 [1536, 2560], P('grp'), may hold values from -0.15625 to 0.15625
- q_gain: bfloat16 [64], replicated, may hold values from 0.5 to 1.5
- k_gain: bfloat16 [64], replicated, may hold values from 0.5 to 1.5
- w_out: bfloat16 [1536, 1536], P('grp'), may hold values from -0.875 to 0.875
- ffn_gain: bfloat16 [1536], P('grp'), may hold values from 0.5 to 1.5
- w_gate_up: bfloat16 [1536, 9216], P('grp'), may hold values from -0.15625 to 0.15625
- w_down: bfloat16 [4608, 1536], P('grp'), may hold values from -0.09375 to 0.09375
- cotangent: bfloat16 [4096, 1536], P(('rep', 'grp')), may hold values from -6 to 6
- segment_ids: int32 [4096], P(('rep', 'grp')), may hold values from 0 to 7, as said below
Outputs:
- mixed: bfloat16 [4096, 1536], P(('rep', 'grp'))
- input_grad: float32 [4096, 1536], P(('rep', 'grp'))
- attn_gain_grad: float32 [1536], P('grp')
- w_qkv_grad: float32 [1536, 2560], P('grp')
- q_gain_grad: float32 [64], replicated
- k_gain_grad: float32 [64], replicated
- w_out_grad: float32 [1536, 1536], P('grp')
- ffn_gain_grad: float32 [1536], P('grp')
- w_gate_up_grad: float32 [1536, 9216], P('grp')
- w_down_grad: float32 [4608, 1536], P('grp')
Inputs may be any that keep to these rules, and one draw needn't show every extreme that they name: `segment_ids`: Non-decreasing within each sequence of 1024 tokens and 0 at its first token; every document number appears in every sequence.
All inputs are finite; a program needn't handle non-finite values.
Results may differ from a plain program's by a relative error of at most 0.02.
Values may be sent and summed in bfloat16 or wider, within the bound.
A program may use at most 320 MiB of HBM per device.

v0:
```python
import jax
import jax.numpy as jnp
from jax import lax
from jax.sharding import PartitionSpec as P

HEADS = 24
KV_HEADS = 8
HEAD_DIM = 64
FF = 4608


EPS = 1e-05
THETA = 1000000.0


def dot_last(left, right):
    return lax.dot_general(
        left, right, (((1,), (1,)), ((), ())), preferred_element_type=jnp.float32
    )


def dot_first(left, right):
    return lax.dot_general(
        left, right, (((0,), (0,)), ((), ())), preferred_element_type=jnp.float32
    )


def rope_tables(positions):
    half = HEAD_DIM // 2
    freq = jnp.exp(-jnp.log(THETA) * jnp.arange(half, dtype=jnp.float32) * 2.0 / HEAD_DIM)
    angle = positions.astype(jnp.float32)[:, None] * freq[None, :]
    return (jnp.cos(angle), jnp.sin(angle))


def rotate(values, cosine, sine):
    half = values.shape[-1] // 2
    first = values[..., :half]
    second = values[..., half:]
    cos_b = cosine[:, None, :]
    sin_b = sine[:, None, :]
    return jnp.concatenate(
        [first * cos_b - second * sin_b, second * cos_b + first * sin_b], axis=-1
    )


def rotate_back(grads, cosine, sine):
    half = grads.shape[-1] // 2
    first = grads[..., :half]
    second = grads[..., half:]
    cos_b = cosine[:, None, :]
    sin_b = sine[:, None, :]
    return jnp.concatenate(
        [first * cos_b + second * sin_b, second * cos_b - first * sin_b], axis=-1
    )


def norm_back(grad_out, values, inverse, gain):
    scaled = grad_out * gain
    gain_grad = jnp.sum((grad_out * values * inverse).reshape(-1, values.shape[-1]), axis=0)
    inner = jnp.mean(scaled * values, axis=-1, keepdims=True)
    return (inverse * scaled - values * inverse * inverse * inverse * inner, gain_grad)


def to_heads(array, rows, group):
    return (
        array.reshape(rows, KV_HEADS, group, HEAD_DIM)
        .transpose(1, 2, 0, 3)
        .reshape(KV_HEADS, group * rows, HEAD_DIM)
    )


def from_heads(array, rows, group):
    return array.reshape(KV_HEADS, group, rows, HEAD_DIM).transpose(2, 0, 1, 3)


def swiglu_back(grad_hidden, gate, up):
    sigma = jax.nn.sigmoid(gate)
    active = gate * sigma
    grad_gate = grad_hidden * up * sigma * (1.0 + gate * (1.0 - sigma))
    grad_up = grad_hidden * active
    return jnp.concatenate([grad_gate, grad_up], axis=1).astype(jnp.bfloat16)


def local(
    tokens,
    attn_gain,
    w_qkv,
    q_gain,
    k_gain,
    w_out,
    ffn_gain,
    w_gate_up,
    w_down,
    cotangent,
    segment_ids,
):
    rows, width = tokens.shape
    groups = lax.axis_size("grp")
    place = lax.axis_index("grp")
    q_width = HEADS * HEAD_DIM
    kv_width = KV_HEADS * HEAD_DIM
    group = HEADS // KV_HEADS
    scale = HEAD_DIM ** (-0.5)
    xs = tokens.astype(jnp.float32)
    w_qkv_all, w_out_all, attn_gain_all, ffn_gain_all = (
        lax.all_gather(w_qkv, "grp", axis=0, tiled=True),
        lax.all_gather(w_out, "grp", axis=0, tiled=True),
        lax.all_gather(attn_gain, "grp", axis=0, tiled=True),
        lax.all_gather(ffn_gain, "grp", axis=0, tiled=True),
    )
    gain_one = attn_gain_all.astype(jnp.float32)
    inv_one = lax.rsqrt(jnp.mean(xs * xs, axis=-1, keepdims=True) + EPS)
    normed = (xs * inv_one * gain_one).astype(jnp.bfloat16)
    qkv = jnp.dot(normed, w_qkv_all, preferred_element_type=jnp.float32)
    q_raw = qkv[:, :q_width].reshape(rows, HEADS, HEAD_DIM)
    k_raw = qkv[:, q_width : q_width + kv_width].reshape(rows, KV_HEADS, HEAD_DIM)
    values_low = qkv[:, q_width + kv_width :].astype(jnp.bfloat16)
    q_scale = q_gain.astype(jnp.float32)
    k_scale = k_gain.astype(jnp.float32)
    q_inv = lax.rsqrt(jnp.mean(q_raw * q_raw, axis=-1, keepdims=True) + EPS)
    k_inv = lax.rsqrt(jnp.mean(k_raw * k_raw, axis=-1, keepdims=True) + EPS)
    seq_pos = place * rows + jnp.arange(rows, dtype=jnp.int32)
    cosine, sine = rope_tables(seq_pos)
    queries_low = rotate(q_raw * q_inv * q_scale, cosine, sine).astype(jnp.bfloat16)
    keys_low = (
        rotate(k_raw * k_inv * k_scale, cosine, sine).astype(jnp.bfloat16).reshape(rows, kv_width)
    )
    seg_low = segment_ids.astype(jnp.bfloat16)
    keys_all, values_all, seg_all = (
        lax.all_gather(keys_low, "grp", axis=0, tiled=True),
        lax.all_gather(values_low, "grp", axis=0, tiled=True),
        lax.all_gather(seg_low, "grp", axis=0, tiled=True),
    )
    length = keys_all.shape[0]
    key_pos = jnp.arange(length, dtype=jnp.int32)
    key_seg = seg_all.astype(jnp.int32)
    query_seg = jnp.tile(segment_ids, group)
    query_pos = jnp.tile(seq_pos, group)
    allowed = (query_seg[:, None] == key_seg[None, :]) & (key_pos[None, :] <= query_pos[:, None])
    query_heads = to_heads(queries_low, rows, group)
    key_heads = keys_all.reshape(length, KV_HEADS, HEAD_DIM).transpose(1, 0, 2)
    value_heads = values_all.reshape(length, KV_HEADS, HEAD_DIM).transpose(1, 0, 2)

    def attend(item):
        query, key, value = item
        scores = jnp.where(allowed, dot_last(query, key) * scale, -1e30)
        top = jnp.max(scores, axis=-1, keepdims=True)
        expo = jnp.exp(scores - top)
        total = jnp.sum(expo, axis=-1, keepdims=True)
        probs = (expo / total).astype(jnp.bfloat16)
        return (jnp.dot(probs, value, preferred_element_type=jnp.float32), top + jnp.log(total))

    head_out, log_total = lax.map(attend, (query_heads, key_heads, value_heads))
    attended = from_heads(head_out, rows, group).reshape(rows, q_width).astype(jnp.bfloat16)
    mid = xs + jnp.dot(attended, w_out_all, preferred_element_type=jnp.float32)
    gain_two = ffn_gain_all.astype(jnp.float32)
    inv_two = lax.rsqrt(jnp.mean(mid * mid, axis=-1, keepdims=True) + EPS)
    normed_two = (mid * inv_two * gain_two).astype(jnp.bfloat16)
    w_gu_all, w_down_all = (
        lax.all_gather(w_gate_up, "grp", axis=0, tiled=True),
        lax.all_gather(w_down, "grp", axis=0, tiled=True),
    )
    gate_up = jnp.dot(normed_two, w_gu_all, preferred_element_type=jnp.float32)
    gate = gate_up[:, :FF]
    up = gate_up[:, FF:]
    hidden = (jax.nn.silu(gate) * up).astype(jnp.bfloat16)
    mixed = (mid + jnp.dot(hidden, w_down_all, preferred_element_type=jnp.float32)).astype(
        jnp.bfloat16
    )
    grad_gu = swiglu_back(dot_last(cotangent, w_down_all), gate, up)
    down_grad = lax.psum_scatter(
        dot_first(hidden, cotangent).astype(jnp.bfloat16), "grp", scatter_dimension=0, tiled=True
    )
    up_grad = lax.psum_scatter(
        dot_first(normed_two, grad_gu).astype(jnp.bfloat16), "grp", scatter_dimension=0, tiled=True
    )
    grad_normed_two = dot_last(grad_gu, w_gu_all)
    grad_mid_part, gain_two_grad = norm_back(grad_normed_two, mid, inv_two, gain_two)
    grad_mid = cotangent.astype(jnp.float32) + grad_mid_part
    grad_branch = grad_mid.astype(jnp.bfloat16)
    out_grad_full = dot_first(attended, grad_branch)
    w_qkv_back, w_out_back = (
        lax.all_gather(w_qkv, "grp", axis=0, tiled=True),
        lax.all_gather(w_out, "grp", axis=0, tiled=True),
    )
    grad_attended = dot_last(grad_branch, w_out_back).astype(jnp.bfloat16)
    grad_heads = to_heads(grad_attended, rows, group)

    def attend_back(item):
        query, key, value, grad_o, log_sum = item
        scores = dot_last(query, key) * scale
        probs = jnp.where(allowed, jnp.exp(scores - log_sum), 0.0)
        grad_p = dot_last(grad_o, value)
        delta = jnp.sum(probs * grad_p, axis=-1, keepdims=True)
        grad_s = (probs * (grad_p - delta)).astype(jnp.bfloat16)
        grad_q = jnp.dot(grad_s, key, preferred_element_type=jnp.float32) * scale
        grad_k = dot_first(grad_s, query) * scale
        grad_v = dot_first(probs.astype(jnp.bfloat16), grad_o)
        return (grad_q, grad_k, grad_v)

    head_dq, head_dk, head_dv = lax.map(
        attend_back, (query_heads, key_heads, value_heads, grad_heads, log_total)
    )
    keys_grad_all = head_dk.transpose(1, 0, 2).reshape(length, kv_width)
    values_grad_all = head_dv.transpose(1, 0, 2).reshape(length, kv_width)
    key_grad, value_grad = (
        lax.psum_scatter(
            keys_grad_all.astype(jnp.bfloat16), "grp", scatter_dimension=0, tiled=True
        ).astype(jnp.float32),
        lax.psum_scatter(
            values_grad_all.astype(jnp.bfloat16), "grp", scatter_dimension=0, tiled=True
        ).astype(jnp.float32),
    )
    grad_q = from_heads(head_dq, rows, group).reshape(rows, HEADS, HEAD_DIM)
    grad_q_raw, q_gain_part = norm_back(rotate_back(grad_q, cosine, sine), q_raw, q_inv, q_scale)
    grad_k = key_grad.reshape(rows, KV_HEADS, HEAD_DIM)
    grad_k_raw, k_gain_part = norm_back(rotate_back(grad_k, cosine, sine), k_raw, k_inv, k_scale)
    grad_qkv = jnp.concatenate(
        [grad_q_raw.reshape(rows, q_width), grad_k_raw.reshape(rows, kv_width), value_grad], axis=1
    ).astype(jnp.bfloat16)
    qkv_grad_full = dot_first(normed, grad_qkv)
    grad_normed = dot_last(grad_qkv, w_qkv_back)
    grad_x_part, gain_one_grad = norm_back(grad_normed, xs, inv_one, gain_one)
    input_grad = grad_mid + grad_x_part
    head_gains = jnp.broadcast_to(
        jnp.concatenate([q_gain_part, k_gain_part])[None, :], (groups, 2 * HEAD_DIM)
    )
    qkv_owned, out_owned, gain_one_owned, gain_two_owned, head_owned = (
        lax.psum_scatter(qkv_grad_full, "grp", scatter_dimension=0, tiled=True),
        lax.psum_scatter(out_grad_full, "grp", scatter_dimension=0, tiled=True),
        lax.psum_scatter(gain_one_grad, "grp", scatter_dimension=0, tiled=True),
        lax.psum_scatter(gain_two_grad, "grp", scatter_dimension=0, tiled=True),
        lax.psum_scatter(head_gains, "grp", scatter_dimension=0, tiled=True),
    )
    qkv_total, out_total, gain_one_total, gain_two_total, up_total, down_total, head_total = (
        lax.psum(qkv_owned.astype(jnp.bfloat16), "rep").astype(jnp.float32),
        lax.psum(out_owned.astype(jnp.bfloat16), "rep").astype(jnp.float32),
        lax.psum(gain_one_owned.astype(jnp.bfloat16), "rep").astype(jnp.float32),
        lax.psum(gain_two_owned.astype(jnp.bfloat16), "rep").astype(jnp.float32),
        lax.psum(up_grad, "rep").astype(jnp.float32),
        lax.psum(down_grad, "rep").astype(jnp.float32),
        lax.psum(head_owned.astype(jnp.bfloat16), "rep").astype(jnp.float32),
    )
    q_gain_total = head_total[0, :HEAD_DIM]
    k_gain_total = head_total[0, HEAD_DIM:]
    return (
        mixed,
        input_grad,
        gain_one_total,
        qkv_total,
        q_gain_total,
        k_gain_total,
        out_total,
        gain_two_total,
        up_total,
        down_total,
    )


def solution(mesh):
    placed = (
        P(("rep", "grp"), None),
        P("grp"),
        P("grp", None),
        P(),
        P(),
        P("grp", None),
        P("grp"),
        P("grp", None),
        P("grp", None),
        P(("rep", "grp"), None),
        P(("rep", "grp")),
    )
    return jax.shard_map(
        local,
        mesh=mesh,
        in_specs=placed,
        out_specs=(
            P(("rep", "grp"), None),
            P(("rep", "grp"), None),
            P("grp"),
            P("grp", None),
            P(),
            P(),
            P("grp", None),
            P("grp"),
            P("grp", None),
            P("grp", None),
        ),
        check_vma=False,
    )
```

profile of v0, /device:TPU:0, one launch (start us, length us, event | category | flops | bytes accessed | tf_op | source)
XLA Modules:
  0.0 2533.0 jit_solution(14811746248613135315)
XLA Ops:
  11.7 23.9 all-reduce.6
  37.6 93.9 %all-gather.8.cloned.1.call-done = bf16[1536,2560]{1,0:T(8,128)(2,1)} async-done(((bf16[192,2560]{1,0:T(8,128)(2,1)}), bf16[1536,2560]{1,0:T(8,128)(2,1)}) %all-gather.8.cloned.1.call-update) | async-done | bytes 7864336 | tf_op jit(solution)/shard_map/all_gather | solution.py:106
  131.5 4.7 fusion.73
  141.1 18.0 all-gather
  162.9 13.0 all-gather.10.cloned.1.call-done
  178.7 39.1 %all-gather.12.cloned.1.call-done = bf16[1024,512]{1,0:T(8,128)(2,1)} async-done(((bf16[128,512]{1,0:T(8,128)(2,1)}), bf16[1024,512]{1,0:T(8,128)(2,1)}) %all-gather.12.cloned.1.call-update) | async-done | bytes 1048592 | tf_op jit(solution)/shard_map/all_gather | solution.py:131
  221.1 37.0 %while.30 = (s32[]{:T(128)}, bf16[8,384,64]{1,2,0:T(8,128)(2,1)}, f32[8,384,1]{1,2,0:T(1,128)}, bf16[8,384,64]{2,1,0:T(8,128)(2,1)S(1)}, bf16[8,1024,64]{2,1,0:T...) while((s32[]{:T(128)}, bf16[8,384,64]{1,2,0:T(8,128)(2,1)}, ...), condition=%wide.region_6.7_spmd.clone.clone, body=%wide.region_3.6_spmd.clone.sunk.clone | while | flops 104988288 | bytes 5465193 | solution.py:153
  259.9 38.6 %all-gather.14.cloned.1.call-done = bf16[1536,1536]{1,0:T(8,128)(2,1)} async-done(((bf16[192,1536]{1,0:T(8,128)(2,1)}), bf16[1536,1536]{1,0:T(8,128)(2,1)}) %all-gather.14.cloned.1.call-update) | async-done | bytes 4718608 | tf_op jit(solution)/shard_map/all_gather | solution.py:107
  298.4 3.2 multiply_reduce_fusion.4
  301.7 535.7 %all-gather.16.cloned.1.call-done = bf16[1536,9216]{1,0:T(8,128)(2,1)} async-done(((bf16[192,9216]{1,0:T(8,128)(2,1)}), bf16[1536,9216]{1,0:T(8,128)(2,1)}) %all-gather.16.cloned.1.call-update) | async-done | bytes 28311568 | tf_op jit(solution)/shard_map/all_gather | solution.py:160
  837.4 15.2 fusion.80
  852.7 182.4 %all-gather.18.cloned.1.call-done = bf16[4608,1536]{1,0:T(8,128)(2,1)} async-done(((bf16[576,1536]{1,0:T(8,128)(2,1)}), bf16[4608,1536]{1,0:T(8,128)(2,1)}) %all-gather.18.cloned.1.call-update) | async-done | bytes 14155792 | tf_op jit(solution)/shard_map/all_gather | solution.py:161
  1035.1 13.0 multiply_convert_fusion.2
  1048.1 15.7 multiply_reduce_fusion.1
  1071.3 78.3 %while.31 = (s32[]{:T(128)}, f32[8,384,64]{1,2,0:T(8,128)}, bf16[8,1024,64]{1,2,0:T(8,128)(2,1)}, bf16[8,1024,64]{1,2,0:T(8,128)(2,1)}, bf16[8,384,64]{2,1,0:T(8...) while((s32[]{:T(128)}, f32[8,384,64]{1,2,0:T(8,128)}, ...), condition=%wide.region_11.12_spmd.clone.clone, body=%wide.region_9.11_spmd.clone.sunk.clone | while | flops 256466560 | bytes 13619841 | solution.py:201
  1154.3 6.1 fusion.69
  1184.3 29.4 %reduce-scatter.19.cloned.1.call-done = bf16[128,512]{1,0:T(8,128)(2,1)} async-done(((bf16[1024,512]{1,0:T(8,128)(2,1)}), bf16[128,512]{1,0:T(8,128)(2,1)}) %reduce-scatter.19.cloned.1.call-update) | async-done | bytes 131088
  1220.8 59.7 %reduce-scatter.9.cloned.1.call-done = bf16[128,512]{1,0:T(8,128)(2,1)} async-done(((bf16[1024,512]{1,0:T(8,128)(2,1)}), bf16[128,512]{1,0:T(8,128)(2,1)}) %reduce-scatter.9.cloned.1.call-update) | async-done | bytes 131088 | tf_op jit(solution)/shard_map/reduce_scatter | solution.py:210
  1280.4 8.8 fusion.64
  1290.3 8.5 convolution_convert_fusion.1
  1299.4 14.4 convolution_convert_fusion
  1314.1 132.5 %reduce-scatter.13.cloned.1.call-done = f32[192,1536]{1,0:T(8,128)} async-done(((f32[1536,1536]{1,0:T(8,128)}), f32[192,1536]{1,0:T(8,128)}) %reduce-scatter.13.cloned.1.call-update) | async-done | bytes 1179664 | tf_op jit(solution)/shard_map/reduce_scatter | solution.py:230
  1448.7 251.5 %reduce-scatter.11.cloned.1.call-done = f32[192,2560]{1,0:T(8,128)} async-done(((f32[1536,2560]{1,0:T(8,128)}), f32[192,2560]{1,0:T(8,128)}) %reduce-scatter.11.cloned.1.call-update) | async-done | bytes 1966096 | tf_op jit(solution)/shard_map/reduce_scatter | solution.py:229
  1702.8 229.4 %reduce-scatter.17.cloned.1.call-done = bf16[576,1536]{1,0:T(8,128)(2,1)} async-done(((bf16[4608,1536]{1,0:T(8,128)(2,1)}), bf16[576,1536]{1,0:T(8,128)(2,1)}) %reduce-scatter.17.cloned.1.call-update) | async-done | bytes 1769488 | tf_op jit(solution)/shard_map/reduce_scatter | solution.py:171
  1932.2 451.7 %reduce-scatter.15.cloned.1.call-done = bf16[192,9216]{1,0:T(8,128)(2,1)} async-done(((bf16[1536,9216]{1,0:T(8,128)(2,1)}), bf16[192,9216]{1,0:T(8,128)(2,1)}) %reduce-scatter.15.cloned.1.call-update) | async-done | bytes 3538960 | tf_op jit(solution)/shard_map/reduce_scatter | solution.py:174
  2402.8 8.0 fusion.43
  2411.8 6.1 fusion.59
  2418.0 35.2 %all-reduce.5 = (bf16[1536]{0:T(1024)(128)(2,1)S(1)}, bf16[8,128]{1,0:T(8,128)(2,1)S(1)}, bf16[1536]{0:T(1024)(128)(2,1)S(1)}) all-reduce(f32[1536]{0:T(1024)S(1)} %get-tuple-element.224, f32[8,128]{1,0:T(8,128)S(1)} %broadcast_in_dim.29, f32[1536]{0:T(1024)S(1)} %copy-done.39), channel_id=4, replica_groups=mesh['rep'=4,'grp'=8] {'grp'}, use_global_device_ids=true, to_apply=%region_18.19.clone | all-reduce | flops 4096 | bytes 24576
  2454.0 5.7 all-reduce.7
  2462.6 53.6 %all-reduce.11.cloned.1.call-done = (bf16[192,2560]{1,0:T(8,128)(2,1)}, bf16[192,1536]{1,0:T(8,128)(2,1)}, bf16[192,9216]{1,0:T(8,128)(2,1)}, bf16[576,1536]{1,0:T(8,128)(2,1)}) async-done(((bf16[192,2560]{1,0:T(8,128)(2,1)}, bf16[192,1536]{1,0:T(8,128)(2,1)}, bf16[192,9216]{1,0:T(8,128)(2,1)}, bf16[576,1536]{1,0:T(8,128)(2,1)}), (bf16[192,2560]{1,0:T(8,128)(2,1)}, bf16[192,1536]{1,0:T(8,128)(2,1)}, ...) | async-done | bytes 6881296 | tf_op jit(solution)/shard_map/psum | solution.py:236
  2516.2 2.8 convert_element_type.171
  2520.2 3.7 convert_element_type.179
  (331 shorter events, 213.0 us)
Async XLA Ops:
  7.2 124.4 %all-gather.8.cloned.1.call-start = ((), (), s32[]{:S(2)}) async-start(), calls=%async_computation.6 | async-start | bytes 8847360 | tf_op jit(solution)/shard_map/all_gather | solution.py:106
  7.9 168.0 %all-gather.10.cloned.1.call-start = ((), (), s32[]{:S(2)}) async-start(), calls=%async_computation.7 | async-start | bytes 1179648 | tf_op jit(solution)/shard_map/all_gather | solution.py:130
  36.2 100.2 %copy-start.43 = (f32[64]{0:T(128)}, f32[64]{0:T(128)S(1)}, u32[]{:S(2)}) copy-start(f32[64]{0:T(128)S(1)} %convert_element_type.147) | copy-start | bytes 772
  37.4 98.8 %copy-start.37 = (f32[128]{0:T(128)}, f32[128]{0:T(128)S(1)}, u32[]{:S(2)}) copy-start(f32[128]{0:T(128)S(1)} %add_rsqrt_fusion.3) | copy-start | bytes 1540
  37.6 99.7 %copy-start.26 = (f32[128,32]{0,1:T(8,128)}, f32[128,32]{0,1:T(8,128)S(1)}, u32[]{:S(2)}) copy-start(f32[128,32]{0,1:T(8,128)S(1)} %get-tuple-element.299) | copy-start | bytes 49156
  37.6 99.6 %copy-start.28 = (f32[128,32]{0,1:T(8,128)}, f32[128,32]{0,1:T(8,128)S(1)}, u32[]{:S(2)}) copy-start(f32[128,32]{0,1:T(8,128)S(1)} %get-tuple-element.300) | copy-start | bytes 49156
  136.2 24.9 copy-start.1
  138.0 79.8 %all-gather.12.cloned.1.call-start = ((), (), s32[]{:S(2)}) async-start(), calls=%async_computation.8 | async-start | bytes 1179648 | tf_op jit(solution)/shard_map/all_gather | solution.py:131
  138.7 159.7 %all-gather.14.cloned.1.call-start = ((), (), s32[]{:S(2)}) async-start(), calls=%async_computation.9 | async-start | bytes 5308416 | tf_op jit(solution)/shard_map/all_gather | solution.py:107
  139.3 698.1 %all-gather.16.cloned.1.call-start = ((), (), s32[]{:S(2)}) async-start(), calls=%async_computation.10 | async-start | bytes 31850496 | tf_op jit(solution)/shard_map/all_gather | solution.py:160
  139.9 895.2 %all-gather.18.cloned.1.call-start = ((), (), s32[]{:S(2)}) async-start(), calls=%async_computation.11 | async-start | bytes 15925248 | tf_op jit(solution)/shard_map/all_gather | solution.py:161
  140.5 1073.2 %reduce-scatter.19.cloned.1.call-start = ((), (), s32[]{:S(2)}) async-start(), calls=%async_computation.17 | async-start | bytes 1179648
  258.1 40.4 %copy-start = (bf16[128,1536]{1,0:T(8,128)(2,1)S(1)}, bf16[128,1536]{1,0:T(8,128)(2,1)}, u32[]{:S(2)}) copy-start(bf16[128,1536]{1,0:T(8,128)(2,1)} %param.15) | copy-start | bytes 1179652
  259.9 41.8 %copy-start.3 = (bf16[128,8,3,64]{0,3,2,1:T(8,128)(2,1)}, bf16[128,8,3,64]{0,3,2,1:T(8,128)(2,1)S(1)}, u32[]{:S(2)}) copy-start(bf16[128,8,3,64]{0,3,2,1:T(8,128)(2,1)S(1)} %copy.99) | copy-start | bytes 1179652
  301.7 746.4 %copy-start.35 = (f32[128]{0:T(128)}, f32[128]{0:T(128)S(1)}, u32[]{:S(2)}) copy-start(f32[128]{0:T(128)S(1)} %add_rsqrt_fusion.2) | copy-start | bytes 1540
  837.4 197.7 %copy-start.16 = (bf16[128,1536]{1,0:T(8,128)(2,1)S(1)}, bf16[128,1536]{1,0:T(8,128)(2,1)}, u32[]{:S(2)}) copy-start(bf16[128,1536]{1,0:T(8,128)(2,1)} %param.24) | copy-start | bytes 1179652
  1048.1 16.7 slice-start
  1048.1 15.7 copy-start.17
  1048.1 16.7 slice-start.1
  1151.9 128.5 %reduce-scatter.9.cloned.1.call-start = ((), (), s32[]{:S(2)}) async-start(), calls=%async_computation.12 | async-start | bytes 1179648 | tf_op jit(solution)/shard_map/reduce_scatter | solution.py:210
  1154.3 292.3 %reduce-scatter.13.cloned.1.call-start = ((), (), s32[]{:S(2)}) async-start(), calls=%async_computation.14 | async-start | bytes 10616832 | tf_op jit(solution)/shard_map/reduce_scatter | solution.py:230
  1160.4 539.9 %reduce-scatter.11.cloned.1.call-start = ((), (), s32[]{:S(2)}) async-start(), calls=%async_computation.13 | async-start | bytes 17694720 | tf_op jit(solution)/shard_map/reduce_scatter | solution.py:229
  1182.2 33.4 %copy-start.5 = (f32[128,512]{0,1:T(8,128)S(1)}, f32[128,512]{0,1:T(8,128)}, u32[]{:S(2)}) copy-start(f32[128,512]{0,1:T(8,128)} %copy-done.4) | copy-start | bytes 786436
  1184.3 96.1 %copy-start.19 = (bf16[128,1536]{1,0:T(8,128)(2,1)}, bf16[128,1536]{1,0:T(8,128)(2,1)S(1)}, u32[]{:S(2)}) copy-start(bf16[128,1536]{1,0:T(8,128)(2,1)S(1)} %fusion.55) | copy-start | bytes 1179652
  1215.6 73.7 %copy-start.20 = (f32[128,8,32]{0,2,1:T(8,128)}, f32[128,8,32]{0,2,1:T(8,128)S(1)}, u32[]{:S(2)}) copy-start(f32[128,8,32]{0,2,1:T(8,128)S(1)} %get-tuple-element.293) | copy-start | bytes 393220
  1289.3 643.0 %reduce-scatter.17.cloned.1.call-start = ((), (), s32[]{:S(2)}) async-start(), calls=%async_computation.16 | async-start | bytes 15925248 | tf_op jit(solution)/shard_map/reduce_scatter | solution.py:171
  1298.8 1085.2 %reduce-scatter.15.cloned.1.call-start = ((), (), s32[]{:S(2)}) async-start(), calls=%async_computation.15 | async-start | bytes 31850496 | tf_op jit(solution)/shard_map/reduce_scatter | solution.py:174
  1313.8 1202.4 %all-reduce.11.cloned.1.call-start = ((), (), s32[]{:S(2)}) async-start(), calls=%async_computation.18 | async-start | bytes 13762560 | tf_op jit(solution)/shard_map/psum | solution.py:236
  2402.8 8.0 copy-start.23
  2402.8 8.3 copy-start.21
  2402.8 8.5 copy-start.13
  2411.8 6.2 copy-start.39
  (31 other events, 62.7 us)
Sparse Core Ops, SparseCore 0:
  10.2 121.2 all-gather.7
  138.1 37.8 all-gather.9
  178.7 39.0 all-gather.11
  219.8 78.6 all-gather.13
  299.8 537.5 all-gather.15
  839.5 195.5 all-gather.17
  1152.0 61.6 reduce-scatter.18
  1218.1 62.3 reduce-scatter.8
  1284.0 162.4 reduce-scatter.12
  1450.0 250.1 reduce-scatter.10
  1703.9 228.2 reduce-scatter.16
  1936.0 447.8 reduce-scatter.14
  2387.3 128.8 all-reduce.10
where the time goes:
time: 2540 us; the launch traced here: 2530 us
  waiting for transfers between devices  2110 us (83%)
  matrix products  206 us (8%)
  blocking collectives  82.8 us (3%)
  local copies, waits for them, and re-layouts  75.1 us (3%)
  other arithmetic  38.7 us (2%)
    all_gather x1, waiting for transfers between devices, local(): lax.all_gather(w_gate_up, 'grp', axis=0, tiled=True)  536 us
    reduce_scatter x1, waiting for transfers between devices, local(): lax.psum_scatter(dot_first(normed_two, grad_gu).astype(jnp.bfloat16), 'gr...  452 us
    reduce_scatter x1, waiting for transfers between devices, local(): lax.psum_scatter(qkv_grad_full, 'grp', scatter_dimension=0, tiled=True)  252 us
    reduce_scatter x1, waiting for transfers between devices, local(): lax.psum_scatter(dot_first(hidden, cotangent).astype(jnp.bfloat16), 'grp'...  229 us
    all_gather x1, waiting for transfers between devices, local(): lax.all_gather(w_down, 'grp', axis=0, tiled=True)  182 us
    reduce_scatter x1, waiting for transfers between devices, local(): lax.psum_scatter(out_grad_full, 'grp', scatter_dimension=0, tiled=True)  132 us
    all_gather x1, waiting for transfers between devices, local(): lax.all_gather(w_qkv, 'grp', axis=0, tiled=True)  93.9 us
    dot_general x28, matrix products, dot_last(): lax.dot_general(left, right, (((1,), (1,)), ((), ())), preferred_element_...  75.4 us
  transfers between devices with their start and end apart: 13, of which 13 were waited for; matrix products, arithmetic and copies ran while one was open for 7% of the time, Pallas kernels for 0%

commit v1 on v0

v1 whole, which is shorter than its diff:
```python
import functools

import jax
import jax.numpy as jnp
from jax import lax
from jax.experimental import pallas as pl
from jax.experimental.pallas import tpu as pltpu
from jax.sharding import PartitionSpec as P

HEADS = 24
KV_HEADS = 8
HEAD_DIM = 64
GROUP = HEADS // KV_HEADS
Q_COLS = GROUP * HEAD_DIM
HEAD_COLS = Q_COLS + 2 * HEAD_DIM

EPS = 1e-05
THETA = 1000000.0
MESH = pl.DeviceIdType.MESH
F32 = jnp.float32
BF16 = jnp.bfloat16

VMEM = pl.BlockSpec(memory_space=pltpu.VMEM)
ANY = pl.BlockSpec(memory_space=pl.ANY)


def here():
    rep = lax.axis_index("rep")
    grp = lax.axis_index("grp")
    r = rep % 4
    return rep - r, r // 2, r % 2, grp // 2, grp % 2


def device(base, y, c, z, x):
    return {"rep": base + 2 * y + c, "grp": 2 * z + x}


def remote(src, dst, send, recv, to):
    return pltpu.make_async_remote_copy(
        src_ref=src, dst_ref=dst, send_sem=send, recv_sem=recv, device_id=to, device_id_type=MESH
    )


def greet(targets):
    barrier = pltpu.get_barrier_semaphore()
    for to in targets:
        pl.semaphore_signal(barrier, inc=1, device_id=to, device_id_type=MESH)
    pl.semaphore_wait(barrier, len(targets))


def neighbours():
    base, y, c, z, x = here()
    to_c = device(base, y, 1 - c, z, x)
    to_x = device(base, y, c, z, 1 - x)
    to_y = device(base, 1 - y, c, z, x)
    return to_c, to_x, to_y


GATHER_SEMS = 8


class Gather:
    def __init__(self, src, out, send, recv, local):
        self.src, self.out, self.send, self.recv, self.local = src, out, send, recv, local
        _, y, c, _, x = here()
        self.to_c, self.to_x, self.to_y = neighbours()
        slot = lambda a, b, d: 4 * a + 2 * b + d
        self.own = slot(y, c, x)
        self.at_c, self.at_x, self.at_y = slot(y, 1 - c, x), slot(y, c, 1 - x), slot(1 - y, c, x)
        self.at_xc, self.at_yc = slot(y, 1 - c, 1 - x), slot(1 - y, 1 - c, x)
        self.at_xy, self.at_xyc = slot(1 - y, c, 1 - x), slot(1 - y, 1 - c, 1 - x)
        self.half = src.shape[0] // 2

    def part(self, ref, k):
        return ref.at[pl.ds(k * self.half, self.half)]

    def copy(self, k, src, dst, to):
        return remote(src, dst, self.send.at[k], self.recv.at[k], to)

    def start(self):
        out, src = self.out, self.src
        self.keep = pltpu.make_async_copy(src, out.at[self.own], self.local)
        self.keep.start()
        self.sent = [
            self.copy(0, src, out.at[self.own], self.to_x),
            self.copy(1, src, out.at[self.own], self.to_y),
            self.copy(2, src, out.at[self.own], self.to_c),
        ]
        for copy in self.sent:
            copy.start()

    def forward(self):
        out = self.out
        self.copy(0, self.src, out.at[self.at_x], self.to_x).wait_recv()
        first = self.part(out.at[self.at_x], 0)
        self.go(3, first, first, self.to_y)
        self.go(4, out.at[self.at_x], out.at[self.at_x], self.to_c)
        self.copy(1, self.src, out.at[self.at_y], self.to_y).wait_recv()
        second = self.part(out.at[self.at_y], 1)
        self.go(5, second, second, self.to_x)
        self.go(6, out.at[self.at_y], out.at[self.at_y], self.to_c)

    def go(self, k, src, dst, to):
        copy = self.copy(k, src, dst, to)
        copy.start()
        self.sent.append(copy)

    def finish(self):
        out = self.out
        first = self.part(out.at[self.at_xy], 0)
        second = self.part(out.at[self.at_xy], 1)
        self.copy(3, first, first, self.to_y).wait_recv()
        self.copy(5, second, second, self.to_x).wait_recv()
        self.go(7, out.at[self.at_xy], out.at[self.at_xy], self.to_c)
        for k, at in ((2, self.at_c), (4, self.at_xc), (6, self.at_yc), (7, self.at_xyc)):
            self.copy(k, out.at[at], out.at[at], self.to_c).wait_recv()
        for copy in self.sent:
            copy.wait_send()
        self.keep.wait()


SUM_SEMS = 10


def sum_scratch(width):
    return [
        pltpu.VMEM((4, 128, width), BF16),
        pltpu.VMEM((4, 128, width), BF16),
        pltpu.VMEM((2, 64, width), BF16),
        pltpu.VMEM((2, 64, width), BF16),
        pltpu.VMEM((2, 64, width), BF16),
        pltpu.VMEM((2, 64, width), BF16),
        pltpu.VMEM((128, width), F32),
        pltpu.SemaphoreType.DMA((SUM_SEMS,)),
        pltpu.SemaphoreType.DMA((SUM_SEMS,)),
    ]


class Summed:
    def __init__(self, part, scratch):
        self.part = part
        (self.r1, self.chip, self.rx, self.ry, self.mine, self.late, self.out,
         self.send, self.recv) = scratch
        _, self.y, self.c, _, self.x = here()
        self.to_c, self.to_x, self.to_y = neighbours()
        y, x = self.y, self.x
        self.order = ((1 - y, 1 - x), (y, 1 - x), (1 - y, x), (y, x))
        self.sent = []

    def copy(self, k, src, dst, to):
        return remote(src, dst, self.send.at[k], self.recv.at[k], to)

    def go(self, k, src, dst, to):
        copy = self.copy(k, src, dst, to)
        copy.start()
        self.sent.append(copy)

    def start(self):
        for k, (y, x) in enumerate(self.order):
            self.go(k, self.part.at[4 * y + 2 * (1 - self.c) + x], self.r1.at[2 * y + x], self.to_c)

    def middle(self):
        x, y, c = self.x, self.y, self.c
        top, low = pl.ds(0, 64), pl.ds(64, 64)
        for k, (b, a) in enumerate(self.order):
            at = 2 * b + a
            self.copy(k, self.r1.at[at], self.r1.at[at], self.to_c).wait_recv()
            total = self.part[4 * b + 2 * c + a].astype(F32) + self.r1[at].astype(F32)
            if k == 3:
                self.out[...] = total
                continue
            self.chip[at] = total.astype(BF16)
            if k in (0, 1):
                self.go(4 + k, self.chip.at[at, top], self.rx.at[b], self.to_x)
            if k in (0, 2):
                self.go(6 + k // 2, self.chip.at[at, low], self.ry.at[a], self.to_y)
        self.copy(4, self.rx.at[1 - y], self.rx.at[1 - y], self.to_x).wait_recv()
        self.mine[0] = (
            self.chip[2 * (1 - y) + x, 0:64].astype(F32) + self.rx[1 - y].astype(F32)
        ).astype(BF16)
        self.go(8, self.mine.at[0], self.late.at[0], self.to_y)
        self.copy(6, self.ry.at[1 - x], self.ry.at[1 - x], self.to_y).wait_recv()
        self.mine[1] = (
            self.chip[2 * y + 1 - x, 64:128].astype(F32) + self.ry[1 - x].astype(F32)
        ).astype(BF16)
        self.go(9, self.mine.at[1], self.late.at[1], self.to_x)

    def finish(self):
        x, y = self.x, self.y
        self.copy(5, self.rx.at[y], self.rx.at[y], self.to_x).wait_recv()
        self.copy(7, self.ry.at[x], self.ry.at[x], self.to_y).wait_recv()
        self.copy(8, self.late.at[0], self.late.at[0], self.to_y).wait_recv()
        self.copy(9, self.late.at[1], self.late.at[1], self.to_x).wait_recv()
        self.out[0:64] += self.rx[y].astype(F32) + self.late[0].astype(F32)
        self.out[64:128] += self.ry[x].astype(F32) + self.late[1].astype(F32)
        for copy in self.sent:
            copy.wait_send()


def dma(n):
    return pltpu.SemaphoreType.DMA((n,))


def params(cid, limit=60):
    return pltpu.CompilerParams(
        collective_id=cid, has_side_effects=True, vmem_limit_bytes=limit * 2**20
    )


def local_params(limit=60):
    return pltpu.CompilerParams(vmem_limit_bytes=limit * 2**20)


def gather_kernel(zs, tok, cot, seg, wq, gains, tok_o, cot_o, seg_o, wq_o, gains_o,
                  sa, ra, sb, rb, sc, rc, sw, rw, sg, rg, keep):
    base, y, c, z, x = here()
    to_c, to_x, to_y = neighbours()
    far = []
    for k in range(1, 2 * zs):
        zk, xk = (z + k // 2) % zs, (x + k % 2) % 2
        far.append((device(base, y, c, zk, xk), xk))
    greet([to_c, to_y] + [d for d, _ in far])
    a = Gather(tok, tok_o, sa, ra, keep.at[0])
    b = Gather(cot, cot_o, sb, rb, keep.at[1])
    s = Gather(seg, seg_o, sc, rc, keep.at[2])
    own = 2 * z + x
    s.start()
    a.start()
    sent = []
    for k, (to, xk) in enumerate(far):
        sent.append(remote(wq.at[xk], wq_o.at[own], sw.at[k], rw.at[k], to))
        sent.append(remote(gains, gains_o.at[own], sg.at[k], rg.at[k], to))
    for copy in sent:
        copy.start()
    mine = [
        pltpu.make_async_copy(wq.at[x], wq_o.at[own], keep.at[3]),
        pltpu.make_async_copy(gains, gains_o.at[own], keep.at[4]),
    ]
    for copy in mine:
        copy.start()
    b.start()
    s.forward()
    a.forward()
    s.finish()
    a.finish()
    b.forward()
    b.finish()
    for copy in sent:
        copy.wait_send()
    for k in range(1, 2 * zs):
        zk, xk = (z + zs - k // 2) % zs, (x + k % 2) % 2
        at = 2 * zk + xk
        remote(wq.at[0], wq_o.at[at], sw.at[k - 1], rw.at[k - 1], to_c).wait_recv()
        remote(gains, gains_o.at[at], sg.at[k - 1], rg.at[k - 1], to_c).wait_recv()
    for copy in mine:
        copy.wait()


def first_gather(zs, tok, cot, seg, wq, gains):
    shape = jax.ShapeDtypeStruct
    n = 2 * zs - 1
    return pl.pallas_call(
        functools.partial(gather_kernel, zs),
        name="gather_first",
        out_shape=(
            shape((8,) + tok.shape, BF16),
            shape((8,) + cot.shape, BF16),
            shape((8,) + seg.shape, seg.dtype),
            shape((2 * zs,) + wq.shape[1:], BF16),
            shape((2 * zs,) + gains.shape, BF16),
        ),
        in_specs=[ANY] * 5,
        out_specs=(ANY,) * 5,
        scratch_shapes=[dma(8)] * 6 + [dma(n)] * 4 + [dma(5)],
        compiler_params=params(0),
    )(tok, cot, seg, wq, gains)


def up_kernel(zs, kv, seg, kv_o, seg_o, sk, rk, ss, rs, keep):
    base, y, c, z, x = here()
    others = [device(base, y, c, (z + k) % zs, x) for k in range(1, zs)]
    greet(others)
    mine = [
        pltpu.make_async_copy(kv, kv_o.at[z], keep.at[0]),
        pltpu.make_async_copy(seg, seg_o.at[z], keep.at[1]),
    ]
    for copy in mine:
        copy.start()
    for k in range(1, zs):
        @pl.when(z + k < zs)
        def _():
            to = device(base, y, c, (z + k) % zs, x)
            remote(seg, seg_o.at[z], ss.at[k - 1], rs.at[k - 1], to).start()
            remote(kv, kv_o.at[z], sk.at[k - 1], rk.at[k - 1], to).start()
    for k in range(1, zs):
        @pl.when(z - k >= 0)
        def _():
            at = (z + zs - k) % zs
            to = device(base, y, c, at, x)
            remote(seg, seg_o.at[at], ss.at[k - 1], rs.at[k - 1], to).wait_recv()
            remote(kv, kv_o.at[at], sk.at[k - 1], rk.at[k - 1], to).wait_recv()
    for k in range(1, zs):
        @pl.when(z + k < zs)
        def _():
            to = device(base, y, c, (z + k) % zs, x)
            remote(seg, seg_o.at[z], ss.at[k - 1], rs.at[k - 1], to).wait_send()
            remote(kv, kv_o.at[z], sk.at[k - 1], rk.at[k - 1], to).wait_send()
    for copy in mine:
        copy.wait()


def send_up(zs, kv, seg):
    shape = jax.ShapeDtypeStruct
    n = zs - 1
    return pl.pallas_call(
        functools.partial(up_kernel, zs),
        name="send_up",
        out_shape=(shape((zs,) + kv.shape, BF16), shape((zs,) + seg.shape, seg.dtype)),
        in_specs=[ANY] * 2,
        out_specs=(ANY,) * 2,
        scratch_shapes=[dma(n)] * 4 + [dma(2)],
        compiler_params=params(1),
    )(kv, seg)


def scores_of(q, k, q_seg, k_seg, diagonal, span):
    s = lax.dot_general(q, k, (((1,), (1,)), ((), ())), preferred_element_type=F32)
    allowed = q_seg == k_seg
    if diagonal:
        row = lax.broadcasted_iota(jnp.int32, s.shape, 0) % span
        col = lax.broadcasted_iota(jnp.int32, s.shape, 1)
        allowed = allowed & (col <= row)
    return jnp.where(allowed, jnp.exp(s), 0.0)


def attend_kernel(q_ref, kv_ref, qseg_ref, kseg_ref, o_ref, inv_ref, acc, tot):
    _, _, _, z, _ = here()
    span = kv_ref.shape[2]

    def sequence(s, carry):
        q = q_ref[s]
        q_seg = qseg_ref[s]

        def block(at, diagonal):
            kv = kv_ref[at, s]
            p = scores_of(q, kv[:, :HEAD_DIM], q_seg, kseg_ref[at, s], diagonal, span)
            tot[...] += jnp.sum(p, axis=1, keepdims=True)
            acc[...] += jnp.dot(p.astype(BF16), kv[:, HEAD_DIM:], preferred_element_type=F32)

        acc[...] = jnp.zeros_like(acc)
        tot[...] = jnp.zeros_like(tot)

        def step(at, inner):
            block(at, False)
            return inner

        lax.fori_loop(0, z, step, 0)
        block(z, True)
        inv = 1.0 / tot[...]
        inv_ref[s] = inv
        o_ref[s] = acc[...] * inv
        return carry

    lax.fori_loop(0, q_ref.shape[0], sequence, 0)


def attend(q, kv, q_seg, k_seg):
    shape = jax.ShapeDtypeStruct
    seqs, rows, _ = q.shape
    return pl.pallas_call(
        attend_kernel,
        name="attend",
        out_shape=(shape(q.shape, F32), shape((seqs, rows, 1), F32)),
        in_specs=[VMEM] * 4,
        out_specs=(VMEM,) * 2,
        scratch_shapes=[pltpu.VMEM((rows, HEAD_DIM), F32), pltpu.VMEM((rows, 1), F32)],
        compiler_params=local_params(),
        cost_estimate=pl.CostEstimate(
            flops=4 * seqs * rows * 1024 * HEAD_DIM, bytes_accessed=8 * 2**20,
            transcendentals=seqs * rows * 1024),
    )(q, kv, q_seg, k_seg)


def attend_back_kernel(q_ref, kv_ref, qseg_ref, kseg_ref, inv_ref, o_ref, do_ref,
                       dq_ref, dkv_ref, acc):
    _, _, _, z, _ = here()
    span = kv_ref.shape[2]
    first = (((0,), (0,)), ((), ()))
    last = (((1,), (1,)), ((), ()))

    def sequence(s, carry):
        q = q_ref[s]
        q_seg = qseg_ref[s]
        inv = inv_ref[s]
        do = do_ref[s]
        delta = jnp.sum(do.astype(F32) * o_ref[s], axis=1, keepdims=True)
        acc[...] = jnp.zeros_like(acc)

        def block(at, diagonal):
            kv = kv_ref[at, s]
            key = kv[:, :HEAD_DIM]
            p = scores_of(q, key, q_seg, kseg_ref[at, s], diagonal, span) * inv
            dp = lax.dot_general(do, kv[:, HEAD_DIM:], last, preferred_element_type=F32)
            ds = (p * (dp - delta)).astype(BF16)
            acc[...] += jnp.dot(ds, key, preferred_element_type=F32)
            dk = lax.dot_general(ds, q, first, preferred_element_type=F32)
            dv = lax.dot_general(p.astype(BF16), do, first, preferred_element_type=F32)
            dkv_ref[at, s] = jnp.concatenate([dk, dv], axis=1).astype(BF16)

        def step(at, inner):
            block(at, False)
            return inner

        lax.fori_loop(0, z, step, 0)
        block(z, True)
        dq_ref[s] = acc[...] * HEAD_DIM ** (-0.5)
        return carry

    lax.fori_loop(0, q_ref.shape[0], sequence, 0)


def attend_back(q, kv, q_seg, k_seg, inv, o, do):
    shape = jax.ShapeDtypeStruct
    seqs, rows, _ = q.shape
    return pl.pallas_call(
        attend_back_kernel,
        name="attend_back",
        out_shape=(shape(q.shape, F32), shape(kv.shape, BF16)),
        in_specs=[VMEM] * 7,
        out_specs=(VMEM,) * 2,
        scratch_shapes=[pltpu.VMEM((rows, HEAD_DIM), F32)],
        compiler_params=local_params(),
        cost_estimate=pl.CostEstimate(
            flops=10 * seqs * rows * 1024 * HEAD_DIM, bytes_accessed=12 * 2**20,
            transcendentals=seqs * rows * 1024),
    )(q, kv, q_seg, k_seg, inv, o, do)


def down_kernel(zs, dkv, total, got, sk, rk):
    base, y, c, z, x = here()
    others = [device(base, y, c, (z + k) % zs, x) for k in range(1, zs)]
    greet(others)
    for k in range(1, zs):
        @pl.when(z - k >= 0)
        def _():
            at = (z + zs - k) % zs
            remote(dkv.at[at], got.at[k - 1], sk.at[k - 1], rk.at[k - 1],
                   device(base, y, c, at, x)).start()
    total[...] = dkv[z].astype(F32)
    for k in range(1, zs):
        @pl.when(z + k < zs)
        def _():
            remote(dkv.at[0], got.at[k - 1], sk.at[k - 1], rk.at[k - 1], others[0]).wait_recv()
            total[...] += got[k - 1].astype(F32)
    for k in range(1, zs):
        @pl.when(z - k >= 0)
        def _():
            at = (z + zs - k) % zs
            remote(dkv.at[at], got.at[k - 1], sk.at[k - 1], rk.at[k - 1], others[0]).wait_send()


def send_down(zs, dkv):
    n = zs - 1
    return pl.pallas_call(
        functools.partial(down_kernel, zs),
        name="send_down",
        out_shape=jax.ShapeDtypeStruct(dkv.shape[1:], F32),
        in_specs=[VMEM],
        out_specs=VMEM,
        scratch_shapes=[pltpu.VMEM((n,) + dkv.shape[1:], BF16), dma(n), dma(n)],
        compiler_params=params(2),
    )(dkv)


def inverse_rms(v):
    return lax.rsqrt(jnp.mean(v * v, axis=-1, keepdims=True) + EPS)


def norm_back(dy, v, inv, gain):
    scaled = dy * gain
    gain_grad = jnp.sum(dy * v * inv, axis=0, keepdims=True)
    inner = jnp.mean(scaled * v, axis=-1, keepdims=True)
    return inv * scaled - v * inv * inv * inv * inner, gain_grad


def mid_kernel(part, tok, gain, mid_o, all_o, *rest):
    scratch, (low, sg, rg, keep) = rest[:9], rest[9:]
    greet(neighbours())
    summed = Summed(part, scratch)
    summed.start()
    summed.middle()
    summed.finish()
    mid = tok[...].astype(F32) + summed.out[...]
    mid_o[...] = mid
    low[...] = (mid * inverse_rms(mid) * gain[...]).astype(BF16)
    gather = Gather(low, all_o, sg, rg, keep.at[0])
    gather.start()
    gather.forward()
    gather.finish()


def mid_call(part, tok, gain):
    shape = jax.ShapeDtypeStruct
    return pl.pallas_call(
        mid_kernel,
        name="sum_mid",
        out_shape=(shape(tok.shape, F32), shape((8,) + tok.shape, BF16)),
        in_specs=[VMEM] * 3,
        out_specs=(VMEM, ANY),
        scratch_shapes=sum_scratch(tok.shape[1])
        + [pltpu.VMEM(tok.shape, BF16), dma(8), dma(8), dma(1)],
        compiler_params=params(3),
    )(part, tok, gain)


def dmid_kernel(part, part_mixed, mid, cot, gain, dmid_o, gain_o, mixed_o, all_o, *rest):
    sa, sb, (low, sg, rg, keep) = rest[:9], rest[9:18], rest[18:]
    greet(neighbours())
    first = Summed(part, sa)
    second = Summed(part_mixed, sb)
    first.start()
    first.middle()
    second.start()
    first.finish()
    v = mid[...]
    dv, gain_grad = norm_back(first.out[...], v, inverse_rms(v), gain[...])
    gain_o[...] = gain_grad
    dmid = cot[...].astype(F32) + dv
    dmid_o[...] = dmid
    low[...] = dmid.astype(BF16)
    gather = Gather(low, all_o, sg, rg, keep.at[0])
    gather.start()
    second.middle()
    gather.forward()
    gather.finish()
    second.finish()
    mixed_o[...] = (v + second.out[...]).astype(BF16)


def dmid_call(part, part_mixed, mid, cot, gain):
    shape = jax.ShapeDtypeStruct
    width = mid.shape[1]
    return pl.pallas_call(
        dmid_kernel,
        name="sum_dmid",
        out_shape=(shape(mid.shape, F32), shape((1, width), F32), shape(mid.shape, BF16),
                   shape((8,) + mid.shape, BF16)),
        in_specs=[VMEM] * 5,
        out_specs=(VMEM, VMEM, VMEM, ANY),
        scratch_shapes=sum_scratch(width) + sum_scratch(width)
        + [pltpu.VMEM(mid.shape, BF16), dma(8), dma(8), dma(1)],
        compiler_params=params(4),
    )(part, part_mixed, mid, cot, gain)


def input_kernel(part, tok, dmid, gain, out_o, gain_o, *scratch):
    greet(neighbours())
    summed = Summed(part, scratch)
    summed.start()
    summed.middle()
    summed.finish()
    v = tok[...].astype(F32)
    dv, gain_grad = norm_back(summed.out[...], v, inverse_rms(v), gain[...])
    gain_o[...] = gain_grad
    out_o[...] = dmid[...] + dv


def input_call(part, tok, dmid, gain):
    shape = jax.ShapeDtypeStruct
    return pl.pallas_call(
        input_kernel,
        name="sum_input",
        out_shape=(shape(dmid.shape, F32), shape((1, dmid.shape[1]), F32)),
        in_specs=[VMEM] * 4,
        out_specs=(VMEM, VMEM),
        scratch_shapes=sum_scratch(dmid.shape[1]),
        compiler_params=params(5),
    )(part, tok, dmid, gain)


def z_turn(array, k, zs):
    pairs = [(2 * z + x, 2 * ((z + k) % zs) + x) for z in range(zs) for x in range(2)]
    return lax.ppermute(array, "grp", pairs)


def x_swap(array, zs):
    pairs = [(2 * z + x, 2 * z + 1 - x) for z in range(zs) for x in range(2)]
    return lax.ppermute(array, "grp", pairs)


def r_swap(array, k):
    reps = lax.axis_size("rep")
    return lax.ppermute(array, "rep", [(i, i ^ k) for i in range(reps)])


def pick(stack, at):
    return lax.dynamic_index_in_dim(stack, at, 0, keepdims=False)


def z_gather(own, z, zs):
    turned = jnp.stack([own] + [z_turn(own, k, zs) for k in range(1, zs)])
    return turned[(z - jnp.arange(zs)) % zs]


def z_sum(blocks, z, zs):
    total = pick(blocks, z).astype(F32)
    for k in range(1, zs):
        total = total + z_turn(pick(blocks, (z + k) % zs), k, zs).astype(F32)
    return total.astype(BF16)


def over_quads(array):
    reps = lax.axis_size("rep")
    if reps == 4:
        return array
    rows = [[j + 4 * q for q in range(reps // 4)] for j in range(4)]
    return lax.psum(array, "rep", axis_index_groups=rows)


def r_gather(own, r):
    core = r_swap(own, 1)
    other = r_swap(own, 2)
    both = r_swap(other, 1)
    turned = jnp.stack([own, core, other, both])
    return turned[r ^ jnp.arange(4)]


def scatter_rows(grad, z, x, r, zs):
    rows = grad.shape[0] // (2 * zs)
    cols = grad.shape[1]
    mine = over_quads(z_sum(grad.reshape(zs, 2, rows, cols), z, zs))
    keep, give = pick(mine, x), pick(mine, 1 - x)
    got = x_swap(give, zs)
    pair = jnp.where(x == 0, jnp.stack([keep, got], 1), jnp.stack([got, keep], 1))
    whole = r_gather(pair, r)
    return whole.transpose(1, 0, 2, 3).reshape(rows, 8, cols).astype(F32)


def scatter_head(grad, z, r, zs):
    rows, cols = grad.shape
    quarter = grad.reshape(4, rows // 4, cols)
    got = [pick(quarter, r)] + [r_swap(pick(quarter, r ^ k), k) for k in range(1, 4)]
    heads = jnp.stack(got)[r ^ jnp.arange(4)]
    mine = over_quads(z_sum(heads, z, zs))
    return r_gather(mine, r).reshape(rows, cols).astype(F32)


def rope_tables(positions):
    half = HEAD_DIM // 2
    freq = jnp.exp(-jnp.log(THETA) * jnp.arange(half, dtype=F32) * 2.0 / HEAD_DIM)
    angle = positions.astype(F32)[:, None] * freq[None, :]
    return jnp.cos(angle), jnp.sin(angle)


def rotate(values, cosine, sine):
    half = HEAD_DIM // 2
    first, second = values[..., :half], values[..., half:]
    return jnp.concatenate(
        [first * cosine - second * sine, second * cosine + first * sine], axis=-1
    )


def head_norm_back(dy, v, inv, gain):
    scaled = dy * gain
    gain_grad = jnp.sum((dy * v * inv).reshape(-1, HEAD_DIM), axis=0)
    inner = jnp.mean(scaled * v, axis=-1, keepdims=True)
    return inv * scaled - v * inv * inv * inv * inner, gain_grad


def dot_last(left, right):
    return lax.dot_general(left, right, (((1,), (1,)), ((), ())), preferred_element_type=F32)


def dot_first(left, right):
    return lax.dot_general(left, right, (((0,), (0,)), ((), ())), preferred_element_type=F32)


def dot(left, right):
    return jnp.dot(left, right, preferred_element_type=F32)


def local(tokens, attn_gain, w_qkv, q_gain, k_gain, w_out, ffn_gain, w_gate_up, w_down,
          cotangent, segment_ids):
    rows, width = tokens.shape
    zs = lax.axis_size("grp") // 2
    _, y, c, z, x = here()
    r = 2 * y + c
    q_width, kv_width = HEADS * HEAD_DIM, KV_HEADS * HEAD_DIM
    ff = w_gate_up.shape[1] // 2
    part = ff // 8
    own_rows = w_qkv.shape[0]
    span = 2 * rows
    cut = lax.dynamic_slice_in_dim

    q_pair = cut(w_qkv, 2 * Q_COLS * r, 2 * Q_COLS, 1)
    k_pair = cut(w_qkv, q_width + 2 * HEAD_DIM * r, 2 * HEAD_DIM, 1)
    v_pair = cut(w_qkv, q_width + kv_width + 2 * HEAD_DIM * r, 2 * HEAD_DIM, 1)
    wq = jnp.stack([
        jnp.concatenate([
            q_pair[:, i * Q_COLS:(i + 1) * Q_COLS],
            k_pair[:, i * HEAD_DIM:(i + 1) * HEAD_DIM],
            v_pair[:, i * HEAD_DIM:(i + 1) * HEAD_DIM]], 1)
        for i in range(2)])
    gains = jnp.zeros((16, 256), BF16)
    gains = gains.at[0, :own_rows].set(attn_gain).at[1, :own_rows].set(ffn_gain)
    seg = jnp.broadcast_to(segment_ids[None, :], (16, rows))

    tok_all, cot_all, seg_all, wq_all, gains_all = first_gather(
        zs, tokens, cotangent, seg, wq, gains)
    w_qkv_t = wq_all.reshape(width, HEAD_COLS)
    gain_one = gains_all[:, 0, :own_rows].reshape(1, width).astype(F32)
    gain_two = gains_all[:, 1, :own_rows].reshape(1, width).astype(F32)

    quarter = jnp.concatenate([
        cut(w_down, r * (part // 4), part // 4, 0), cut(w_out, r * (own_rows // 4), own_rows // 4, 0)], 0)
    heads = z_gather(quarter, z, zs)
    got = [pick(heads, r)] + [r_swap(pick(heads, r ^ k), k) for k in range(1, 4)]
    whole = jnp.stack(got)[r ^ jnp.arange(4)]
    w_down_t = whole[:, :part // 4].reshape(part, width)
    w_out_t = whole[:, part // 4:].reshape(own_rows, width)
    pair = cut(w_gate_up.reshape(own_rows, 2, ff), 2 * part * r, 2 * part, 2)
    pair = jnp.stack([pair[:, :, :part], pair[:, :, part:]]).reshape(2, own_rows, 2 * part)
    keep, give = pick(pair, x), pick(pair, 1 - x)
    got = x_swap(give, zs)
    unit = jnp.where(x == 0, jnp.stack([keep, got]), jnp.stack([got, keep]))
    w_gu_t = z_gather(unit, z, zs).reshape(width, 2 * part)

    xs = tok_all.reshape(8 * rows, width).astype(F32)
    normed = (xs * inverse_rms(xs) * gain_one).astype(BF16)
    qkv = dot(normed, w_qkv_t)
    q_raw = qkv[:, :Q_COLS].reshape(4, span, GROUP, HEAD_DIM).transpose(0, 2, 1, 3)
    k_raw = qkv[:, Q_COLS:Q_COLS + HEAD_DIM].reshape(4, span, HEAD_DIM)
    values = qkv[:, Q_COLS + HEAD_DIM:].astype(BF16)
    q_scale, k_scale = q_gain.astype(F32), k_gain.astype(F32)
    q_inv, k_inv = inverse_rms(q_raw), inverse_rms(k_raw)
    cosine, sine = rope_tables(span * z + jnp.arange(span, dtype=jnp.int32))
    queries = rotate(q_raw * q_inv * q_scale, cosine, sine) * HEAD_DIM ** (-0.5)
    queries = queries.astype(BF16).reshape(4, GROUP * span, HEAD_DIM)
    keys = rotate(k_raw * k_inv * k_scale, cosine, sine).astype(BF16)
    kv = jnp.concatenate([keys.reshape(4 * span, HEAD_DIM), values], 1)
    kv_all, segs = send_up(zs, kv, seg_all[:, 0].reshape(8, rows))
    kv_all = kv_all.reshape(zs, 4, span, 2 * HEAD_DIM)
    k_seg = segs.reshape(zs, 4, 1, span)
    q_seg = jnp.tile(seg_all[:, 0].reshape(4, span), (1, GROUP))[:, :, None]
    attended_full, inv_total = attend(queries, kv_all, q_seg, k_seg)
    attended = (
        attended_full.reshape(4, GROUP, span, HEAD_DIM).transpose(0, 2, 1, 3)
        .reshape(8 * rows, Q_COLS).astype(BF16))
    out_part = dot(attended, w_out_t).astype(BF16).reshape(8, rows, width)
    mid, normed_two = mid_call(out_part, tokens, gain_two)

    n2 = normed_two.reshape(8 * rows, width)
    cot = cot_all.reshape(8 * rows, width)
    gate_up = dot(n2, w_gu_t)
    gate, up = gate_up[:, :part], gate_up[:, part:]
    sigma = jax.nn.sigmoid(gate)
    active = gate * sigma
    hidden = (active * up).astype(BF16)
    mixed_part = dot(hidden, w_down_t).astype(BF16).reshape(8, rows, width)
    dh = dot_last(cot, w_down_t)
    dgu = jnp.concatenate(
        [dh * up * sigma * (1.0 + gate * (1.0 - sigma)), dh * active], axis=1).astype(BF16)
    dn2_part = dot_last(dgu, w_gu_t).astype(BF16).reshape(8, rows, width)
    down_grad = scatter_head(dot_first(hidden, cot).astype(BF16), z, r, zs)
    gu_grad = scatter_rows(dot_first(n2, dgu).astype(BF16), z, x, r, zs)
    gu_grad = gu_grad.reshape(own_rows, 8, 2, part).transpose(0, 2, 1, 3).reshape(own_rows, 2 * ff)

    dmid, gain_two_grad, mixed, dbranch = dmid_call(dn2_part, mixed_part, mid, cotangent, gain_two)
    dbranch = dbranch.reshape(8 * rows, width)
    dattended = dot_last(dbranch, w_out_t).astype(BF16)
    dattended = (
        dattended.reshape(4, span, GROUP, HEAD_DIM).transpose(0, 2, 1, 3)
        .reshape(4, GROUP * span, HEAD_DIM))
    out_grad = scatter_head(dot_first(attended, dbranch).astype(BF16), z, r, zs)
    dq, dkv = attend_back(queries, kv_all, q_seg, k_seg, inv_total, attended_full, dattended)
    dkv = send_down(zs, dkv.reshape(zs, 4 * span, 2 * HEAD_DIM))
    dq = rotate(dq.reshape(4, GROUP, span, HEAD_DIM), cosine, -sine)
    dk = rotate(dkv[:, :HEAD_DIM].reshape(4, span, HEAD_DIM), cosine, -sine)
    dq_raw, q_gain_part = head_norm_back(dq, q_raw, q_inv, q_scale)
    dk_raw, k_gain_part = head_norm_back(dk, k_raw, k_inv, k_scale)
    dqkv = jnp.concatenate([
        dq_raw.transpose(0, 2, 1, 3).reshape(8 * rows, Q_COLS),
        dk_raw.reshape(8 * rows, HEAD_DIM), dkv[:, HEAD_DIM:]], 1).astype(BF16)
    in_part = dot_last(dqkv, w_qkv_t).astype(BF16).reshape(8, rows, width)
    qkv_grad = scatter_rows(dot_first(normed, dqkv).astype(BF16), z, x, r, zs)
    qkv_grad = jnp.concatenate([
        qkv_grad[:, :, :Q_COLS].reshape(own_rows, q_width),
        qkv_grad[:, :, Q_COLS:Q_COLS + HEAD_DIM].reshape(own_rows, kv_width),
        qkv_grad[:, :, Q_COLS + HEAD_DIM:].reshape(own_rows, kv_width)], 1)
    input_grad, gain_one_grad = input_call(in_part, tokens, dmid, gain_one)

    head_gains = jnp.concatenate([q_gain_part, k_gain_part])
    pad = jnp.zeros((1, width), F32).at[0, :2 * HEAD_DIM].set(head_gains)
    gains_sum = lax.psum(jnp.concatenate([gain_one_grad, gain_two_grad, pad], 0), ("rep", "grp"))
    place = 2 * z + x
    gain_one_out = cut(gains_sum[0], place * own_rows, own_rows, 0)
    gain_two_out = cut(gains_sum[1], place * own_rows, own_rows, 0)
    return (mixed, input_grad, gain_one_out, qkv_grad, gains_sum[2, :HEAD_DIM],
            gains_sum[2, HEAD_DIM:2 * HEAD_DIM], out_grad, gain_two_out, gu_grad, down_grad)


def solution(mesh):
    rows, split = P(("rep", "grp"), None), P("grp", None)
    return jax.shard_map(
        local,
        mesh=mesh,
        in_specs=(rows, P("grp"), split, P(), P(), split, P("grp"), split, split, rows,
                  P(("rep", "grp"))),
        out_specs=(rows, rows, P("grp"), split, P(), P(), split, P("grp"), split, split),
        check_vma=False,
    )
```

time: 2540 us -> 753 us (0.30)
  waiting for transfers between devices: 2110 us -> 161 us
  Pallas kernels: 0 us -> 250 us
  matrix products: 206 us -> 42.4 us
  starting transfers between devices: 0.78 us -> 52.4 us
  blocking collectives: 82.8 us -> 37.1 us
  local copies, waits for them, and re-layouts: 75.1 us -> 118 us
  other arithmetic: 38.7 us -> 76.1 us
    reduce_scatter x5 -> x0, waiting for transfers between devices: 1120 us -> none  [the longest x1 452 us: local(): lax.psum_scatter(dot_first(normed_two, grad_gu).astype(jnp.bfloat16), 'gr...]
    all_gather x6 -> x0, waiting for transfers between devices: 903 us -> none  [the longest x1 536 us: local(): lax.all_gather(w_gate_up, 'grp', axis=0, tiled=True)]
    pallas_call x0 -> x8, Pallas kernels: none -> 250 us  [the longest x1 53.6 us: first_gather(): pl.pallas_call(functools.partial(gather_kernel, zs), name='gather_first',...]
    ppermute x0 -> x42, waiting for transfers between devices: none -> 161 us  [the longest x18 118 us: z_turn(): return lax.ppermute(array, 'grp', pairs)]
    dot_general x28 -> x4, matrix products: 75.4 us -> 15.3 us  [dot_last(): lax.dot_general(left, right, (((1,), (1,)), ((), ())), preferred_element_...]
    unnamed x2 -> x0, blocking collectives: 59.1 us -> none
    dot_general x20 -> x4, matrix products: 67.3 us -> 11.9 us  [dot_first(): lax.dot_general(left, right, (((0,), (0,)), ((), ())), preferred_element_...]
    psum x1 -> x0, waiting for transfers between devices: 53.6 us -> none  [local(): lax.psum(qkv_owned.astype(jnp.bfloat16), 'rep').astype(jnp.float32)]
  transfers between devices with their start and end apart: 13 -> 42, of which waited for: 13 -> 18; matrix products, arithmetic and copies ran while one was open for 7% -> 16% of each run, Pallas kernels for 0% -> 17%
where the time goes in v1:
time: 753 us; the launch traced here: 739 us
  Pallas kernels  250 us (33%)
  waiting for transfers between devices  161 us (21%)
  local copies, waits for them, and re-layouts  118 us (16%)
  other arithmetic  76.1 us (10%)
  starting transfers between devices  52.4 us (7%)
  matrix products  42.4 us (6%)
  blocking collectives  37.1 us (5%)
    ppermute x18, waiting for transfers between devices, z_turn(): return lax.ppermute(array, 'grp', pairs)  118 us
    pallas_call x1, Pallas kernels, first_gather(): pl.pallas_call(functools.partial(gather_kernel, zs), name='gather_first',...  53.6 us
    pallas_call x1, Pallas kernels, dmid_call(): pl.pallas_call(dmid_kernel, name='sum_dmid', out_shape=(shape(mid.shape,...  51.4 us
    pallas_call x1, Pallas kernels, send_down(): pl.pallas_call(functools.partial(down_kernel, zs), name='send_down', out_...  40.3 us
    ppermute x18, starting transfers between devices, z_turn(): return lax.ppermute(array, 'grp', pairs)  40.1 us
    pallas_call x1, Pallas kernels, mid_call(): pl.pallas_call(mid_kernel, name='sum_mid', out_shape=(shape(tok.shape, F3...  39.1 us
    psum x1, blocking collectives, local(): lax.psum(jnp.concatenate([gain_one_grad, gain_two_grad, pad], 0), ('rep',...  37.1 us
    ppermute x21, waiting for transfers between devices, r_swap(): return lax.ppermute(array, 'rep', [(i, i ^ k) for i in range(reps)])  36.1 us
  transfers between devices with their start and end apart: 42, of which 18 were waited for; matrix products, arithmetic and copies ran while one was open for 16% of the time, Pallas kernels for 17%

profile of v1, /device:TPU:0, one launch (start us, length us, event | category | flops | bytes accessed | tf_op | source)
XLA Modules:
  0.0 739.4 jit_solution(3063906598531935612)
XLA Ops:
  3.3 4.0 collective-permute-start.1
  11.2 6.4 reshape.815
  28.2 53.6 %gather_first.1 = (bf16[8,128,1536]{2,1,0:T(8,128)(2,1)}, bf16[8,128,1536]{2,1,0:T(8,128)(2,1)}, s32[8,16,128]{2,1,0:T(8,128)}, bf16[8,192,320]{2,1,0:T(8,128)(2,1)}, bf16[8,16,256]{2,1,0:T(8,128)(2,1)}) custom-call(bf16[128,1536]{1,0:T(8,128)(2,1)} %tok.5, bf16[128,1536]{1,0:T(8,128)(2,1)} %cot.3, s32[16,128]{1,0:T(8,128)} %broadcast_in_dim.2.seg, ...), custom_call_target="tpu_custom_call" | custom-call | tf_op jit(solution)/shard_map/gather_first/pallas_call | solution.py:262
  111.4 3.9 gather_fusion
  124.5 26.5 %send_up.1 = (bf16[4,1024,128]{2,1,0:T(8,128)(2,1)}, s32[4,8,128]{2,1,0:T(8,128)}) custom-call(bf16[1024,128]{1,0:T(8,128)(2,1)} %pad_maximum_fusion.19.kv, s32[8,128]{1,0:T(8,128)} %get-tuple-element.150.seg), custom_call_target="tpu_custom_call" | custom-call | tf_op jit(solution)/shard_map/send_up/pallas_call | solution.py:315
  151.0 8.8 %attend.1 = (f32[4,768,64]{2,1,0:T(8,128)}, f32[4,768,1]{2,1,0:T(8,128)}) custom-call(bf16[4,768,64]{2,1,0:T(8,128)(2,1)} %fusion.6.q_ref, bf16[4,4,256,128]{3,2,1,0:T(8,128)(2,1)} %bitcast.308, s32[4,768,1]{2,1,0:T(8,128)} %copy.89.qseg_ref, s32[4,4,1,256]{3,2,1,0:T(1,128)} %bitcast.310), custom_call_target="tpu_custom_call" | custom-call | flops 805306368 | bytes 8388608 | tf_op jit(solution)/shard_map/attend/pallas_call | solution.py:370
  167.0 14.8 %collective-permute-start.9 = (bf16[2,192,1152]{2,1,0:T(8,128)(2,1)}, bf16[2,192,1152]{2,1,0:T(8,128)(2,1)}, u32[]{:S(2)}, u32[]{:S(2)}) collective-permute-start(bf16[2,192,1152]{2,1,0:T(8,128)(2,1)} %maximum_select_fusion.1), channel_id=1, source_target_pairs={{0,6},{1,7},{2,0},{3,1},{4,2},{5,3},{6,4},{7,5},{8,14},{9,15},{10,... | collective-permute-start | bytes 2654216 | tf_op jit(solution)/shard_map/ppermute | solution.py:583
  186.9 3.8 gather_fusion.1
  197.2 39.1 %sum_mid.1 = (f32[128,1536]{1,0:T(8,128)}, bf16[8,128,1536]{2,1,0:T(8,128)(2,1)}) custom-call(bf16[8,128,1536]{2,1,0:T(8,128)(2,1)} %bitcast.242, bf16[128,1536]{1,0:T(8,128)(2,1)} %tok.5, f32[1,1536]{1,0:T(1,128)} %reshape.837.gain), custom_call_target="tpu_custom_call" | custom-call | tf_op jit(solution)/shard_map/sum_mid/pallas_call | solution.py:504
  236.4 17.1 %collective-permute-done.8 = bf16[2,192,1152]{2,1,0:T(8,128)(2,1)} collective-permute-done((bf16[2,192,1152]{2,1,0:T(8,128)(2,1)}, bf16[2,192,1152]{2,1,0:T(8,128)(2,1)}, u32[]{:S(2)}, u32[]{:S(2)}) %collective-permute-start.8) | collective-permute-done | bytes 884768 | tf_op jit(solution)/shard_map/ppermute | solution.py:583
  256.8 4.9 gather_fusion.2
  261.6 7.1 fusion.36
  271.7 5.7 convolution_convert_fusion.4
  277.4 5.9 convolution_convert_fusion
  286.5 4.1 convolution_convert_fusion.1
  290.6 51.4 %sum_dmid.1 = (f32[128,1536]{1,0:T(8,128)}, f32[1,1536]{1,0:T(1,128)}, bf16[128,1536]{1,0:T(8,128)(2,1)}, bf16[8,128,1536]{2,1,0:T(8,128)(2,1)}) custom-call(bf16[8,128,1536]{2,1,0:T(8,128)(2,1)} %bitcast.262, bf16[8,128,1536]{2,1,0:T(8,128)(2,1)} %bitcast.263, f32[128,1536]{1,0:T(8,128)} %get-tuple-element.74.mid, bf16[128,1536]{1,0:T(8,128)(2,1)} %cot.3, ...), custom_call_target="tpu_custom_call" | custom-call | tf_op jit(solution)/shard_map/sum_dmid/pallas_call | solution.py:543
  348.5 9.1 %attend_back.1 = (f32[4,768,64]{2,1,0:T(8,128)}, bf16[4,4,256,128]{3,2,1,0:T(8,128)(2,1)}) custom-call(bf16[4,768,64]{2,1,0:T(8,128)(2,1)} %fusion.6.q_ref, bf16[4,4,256,128]{3,2,1,0:T(8,128)(2,1)} %bitcast.309, s32[4,768,1]{2,1,0:T(8,128)} %copy.89.qseg_ref, s32[4,4,1,256]{3,2,1,0:T(1,128)} %bitcast.311, f32[4,768,1]{2,1,0:T(8,128)} %get-tuple-element.76.inv_ref, ...), custom_call_target="tpu_custom_call" | custom-call | flops 2013265920 | bytes 12582912 | tf_op jit(solution)/shard_map/attend_back/pallas_call | solution.py:425
  357.6 40.3 %send_down.1 = f32[1024,128]{1,0:T(8,128)} custom-call(bf16[4,1024,128]{2,1,0:T(8,128)(2,1)} %bitcast.280), custom_call_target="tpu_custom_call" | custom-call | tf_op jit(solution)/shard_map/send_down/pallas_call | solution.py:464
  418.8 21.4 %sum_input.1 = (f32[128,1536]{1,0:T(8,128)}, f32[1,1536]{1,0:T(1,128)}) custom-call(bf16[8,128,1536]{2,1,0:T(8,128)(2,1)} %bitcast.258, bf16[128,1536]{1,0:T(8,128)(2,1)} %tok.5, f32[128,1536]{1,0:T(8,128)} %get-tuple-element.80.dmid, f32[1,1536]{1,0:T(1,128)} %reshape.838.gain), custom_call_target="tpu_custom_call" | custom-call | tf_op jit(solution)/shard_map/sum_input/pallas_call | solution.py:570
  441.1 37.1 %psum.7 = f32[3,1536]{1,0:T(4,128)S(1)} all-reduce(f32[3,1536]{1,0:T(4,128)S(1)} %select_maximum_fusion), channel_id=1, replica_groups=mesh['rep'=4,'grp'=8] {'rep','grp'}, use_global_device_ids=true, to_apply=%region_8.9 | all-reduce | flops 4608 | bytes 36864 | tf_op jit(solution)/shard_map/psum | solution.py:794
  490.6 14.0 %collective-permute-done.19 = bf16[48,1536]{1,0:T(8,128)(2,1)} collective-permute-done((bf16[48,1536]{1,0:T(8,128)(2,1)}, bf16[48,1536]{1,0:T(8,128)(2,1)}, u32[]{:S(2)}, u32[]{:S(2)}) %collective-permute-start.19) | collective-permute-done | bytes 147488 | tf_op jit(solution)/shard_map/ppermute | solution.py:593
  517.3 5.7 collective-permute-done.12
  523.1 18.9 %collective-permute-done.11 = bf16[2,192,320]{2,1,0:T(8,128)(2,1)} collective-permute-done((bf16[2,192,320]{2,1,0:T(8,128)(2,1)S(1)}, bf16[2,192,320]{2,1,0:T(8,128)(2,1)}, u32[]{:S(2)}, u32[]{:S(2)}) %collective-permute-start.11) | collective-permute-done | bytes 245792 | tf_op jit(solution)/shard_map/ppermute | solution.py:583
  581.1 7.7 %collective-permute-done.28 = bf16[2,192,1152]{2,1,0:T(8,128)(2,1)} collective-permute-done((bf16[2,192,1152]{2,1,0:T(8,128)(2,1)}, bf16[2,192,1152]{2,1,0:T(8,128)(2,1)}, u32[]{:S(2)}, u32[]{:S(2)}) %collective-permute-start.28) | collective-permute-done | bytes 884768 | tf_op jit(solution)/shard_map/ppermute | solution.py:583
  588.8 56.9 %collective-permute-done.27 = bf16[2,192,1152]{2,1,0:T(8,128)(2,1)} collective-permute-done((bf16[2,192,1152]{2,1,0:T(8,128)(2,1)}, bf16[2,192,1152]{2,1,0:T(8,128)(2,1)}, u32[]{:S(2)}, u32[]{:S(2)}) %collective-permute-start.27) | collective-permute-done | bytes 884768 | tf_op jit(solution)/shard_map/ppermute | solution.py:583
  649.2 5.9 collective-permute-done.37
  674.6 13.9 %collective-permute-done.31 = bf16[192,2,1152]{2,0,1:T(8,128)(2,1)} collective-permute-done((bf16[192,2,1152]{2,0,1:T(8,128)(2,1)}, bf16[192,2,1152]{2,0,1:T(8,128)(2,1)}, u32[]{:S(2)}, u32[]{:S(2)}) %collective-permute-start.31) | collective-permute-done | bytes 884768 | tf_op jit(solution)/shard_map/ppermute | solution.py:593
  696.7 4.7 gather_fusion.6
  701.4 5.4 convert_bitcast_fusion
  706.9 10.7 %reshape.851 = f32[192,8,2,576]{3,2,0,1:T(2,128)} reshape(f32[192,4,2,1152]{3,0,2,1:T(8,128)} %convert_bitcast_fusion) | data formatting | bytes 14155776 | tf_op jit(solution)/shard_map/reshape | solution.py:766
  717.5 10.9 %copy.107 = f32[192,2,8,576]{3,2,1,0:T(8,128)} copy(f32[192,2,8,576]{3,1,0,2:T(2,128)} %bitcast.241) | data formatting | bytes 14155776 | tf_op jit(solution)/shard_map/reshape | solution.py:766
  728.4 8.8 %reshape.846 = f32[192,9216]{1,0:T(8,128)} reshape(f32[192,2,8,576]{3,2,1,0:T(8,128)} %copy.107) | data formatting | bytes 14155776 | tf_op jit(solution)/shard_map/reshape | solution.py:766
  (327 shorter events, 208.5 us)
Async XLA Ops:
  3.3 105.0 %collective-permute-start.1 = (bf16[192,1536]{1,0:T(8,128)(2,1)}, bf16[192,1536]{1,0:T(8,128)(2,1)}, u32[]{:S(2)}, u32[]{:S(2)}) collective-permute-start(bf16[192,1536]{1,0:T(8,128)(2,1)} %get-tuple-element.145), channel_id=1, source_target_pairs={{0,4},{1,5},{2,6},{3,7},{4,0},{5,1},{6,2},{7,3},{8,12},{9,13},{10,... | collective-permute-start | bytes 1769480 | tf_op jit(solution)/shard_map/ppermute | solution.py:583
  7.4 100.9 %collective-permute-start = (bf16[192,1536]{1,0:T(8,128)(2,1)}, bf16[192,1536]{1,0:T(8,128)(2,1)}, u32[]{:S(2)}, u32[]{:S(2)}) collective-permute-start(bf16[192,1536]{1,0:T(8,128)(2,1)} %get-tuple-element.145), channel_id=1, source_target_pairs={{0,2},{1,3},{2,4},{3,5},{4,6},{5,7},{6,0},{7,1},{8,10},{9,11},{10,... | collective-permute-start | bytes 1769480 | tf_op jit(solution)/shard_map/ppermute | solution.py:583
  8.9 99.4 %collective-permute-start.2 = (bf16[192,1536]{1,0:T(8,128)(2,1)}, bf16[192,1536]{1,0:T(8,128)(2,1)}, u32[]{:S(2)}, u32[]{:S(2)}) collective-permute-start(bf16[192,1536]{1,0:T(8,128)(2,1)} %get-tuple-element.145), channel_id=1, source_target_pairs={{0,6},{1,7},{2,0},{3,1},{4,2},{5,3},{6,4},{7,5},{8,14},{9,15},{10,... | collective-permute-start | bytes 1769480 | tf_op jit(solution)/shard_map/ppermute | solution.py:583
  22.5 142.3 %collective-permute-start.6 = (bf16[192,1152]{1,0:T(8,128)(2,1)}, bf16[192,1152]{1,0:T(8,128)(2,1)}, u32[]{:S(2)}, u32[]{:S(2)}) collective-permute-start(bf16[192,1152]{1,0:T(8,128)(2,1)} %get-tuple-element.128), channel_id=1, source_target_pairs={{0,1},{1,0},{2,3},{3,2},{4,5},{5,4},{6,7},{7,6},{8,9},{9,8},{10,11... | collective-permute-start | bytes 1327112 | tf_op jit(solution)/shard_map/ppermute | solution.py:588
  118.3 63.6 %collective-permute-start.4 = (bf16[192,1536]{1,0:T(8,128)(2,1)}, bf16[192,1536]{1,0:T(8,128)(2,1)}, u32[]{:S(2)}, u32[]{:S(2)}) collective-permute-start(bf16[192,1536]{1,0:T(8,128)(2,1)} %get-tuple-element.101), channel_id=1, source_target_pairs={{0,16},{8,24},{16,0},{24,8},{1,17},{9,25},{17,1},{25,9},{2,18},{10... | collective-permute-start | bytes 1769480 | tf_op jit(solution)/shard_map/ppermute | solution.py:593
  164.2 19.9 %collective-permute-start.3 = (bf16[192,1536]{1,0:T(8,128)(2,1)}, bf16[192,1536]{1,0:T(8,128)(2,1)S(1)}, u32[]{:S(2)}, u32[]{:S(2)}) collective-permute-start(bf16[192,1536]{1,0:T(8,128)(2,1)} %get-tuple-element.102), channel_id=1, source_target_pairs={{0,8},{8,0},{16,24},{24,16},{1,9},{9,1},{17,25},{25,17},{2,10},{10... | collective-permute-start | bytes 1769480 | tf_op jit(solution)/shard_map/ppermute | solution.py:593
  164.2 19.9 %collective-permute-start.5 = (bf16[192,1536]{1,0:T(8,128)(2,1)}, bf16[192,1536]{1,0:T(8,128)(2,1)S(1)}, u32[]{:S(2)}, u32[]{:S(2)}) collective-permute-start(bf16[192,1536]{1,0:T(8,128)(2,1)} %get-tuple-element.103), channel_id=1, source_target_pairs={{0,24},{8,16},{16,8},{24,0},{1,25},{9,17},{17,9},{25,1},{2,26},{10... | collective-permute-start | bytes 1769480 | tf_op jit(solution)/shard_map/ppermute | solution.py:593
  167.0 69.3 %collective-permute-start.9 = (bf16[2,192,1152]{2,1,0:T(8,128)(2,1)}, bf16[2,192,1152]{2,1,0:T(8,128)(2,1)}, u32[]{:S(2)}, u32[]{:S(2)}) collective-permute-start(bf16[2,192,1152]{2,1,0:T(8,128)(2,1)} %maximum_select_fusion.1), channel_id=1, source_target_pairs={{0,6},{1,7},{2,0},{3,1},{4,2},{5,3},{6,4},{7,5},{8,14},{9,15},{10,... | collective-permute-start | bytes 2654216 | tf_op jit(solution)/shard_map/ppermute | solution.py:583
  181.8 71.6 %collective-permute-start.8 = (bf16[2,192,1152]{2,1,0:T(8,128)(2,1)}, bf16[2,192,1152]{2,1,0:T(8,128)(2,1)}, u32[]{:S(2)}, u32[]{:S(2)}) collective-permute-start(bf16[2,192,1152]{2,1,0:T(8,128)(2,1)} %maximum_select_fusion.1), channel_id=1, source_target_pairs={{0,4},{1,5},{2,6},{3,7},{4,0},{5,1},{6,2},{7,3},{8,12},{9,13},{10,... | collective-permute-start | bytes 2654216 | tf_op jit(solution)/shard_map/ppermute | solution.py:583
  181.8 71.6 %collective-permute-start.7 = (bf16[2,192,1152]{2,1,0:T(8,128)(2,1)}, bf16[2,192,1152]{2,1,0:T(8,128)(2,1)}, u32[]{:S(2)}, u32[]{:S(2)}) collective-permute-start(bf16[2,192,1152]{2,1,0:T(8,128)(2,1)} %maximum_select_fusion.1), channel_id=1, source_target_pairs={{0,2},{1,3},{2,4},{3,5},{4,6},{5,7},{6,0},{7,1},{8,10},{9,11},{10,... | collective-permute-start | bytes 2654216 | tf_op jit(solution)/shard_map/ppermute | solution.py:583
  480.0 78.0 %collective-permute-start.35 = (bf16[144,1536]{1,0:T(8,128)(2,1)}, bf16[144,1536]{1,0:T(8,128)(2,1)S(1)}, u32[]{:S(2)}, u32[]{:S(2)}) collective-permute-start(bf16[144,1536]{1,0:T(8,128)(2,1)} %get-tuple-element.108), channel_id=1, source_target_pairs={{0,24},{8,16},{16,8},{24,0},{1,25},{9,17},{17,9},{25,1},{2,26},{10... | collective-permute-start | bytes 1327112 | tf_op jit(solution)/shard_map/ppermute | solution.py:593
  480.5 77.5 %collective-permute-start.34 = (bf16[144,1536]{1,0:T(8,128)(2,1)}, bf16[144,1536]{1,0:T(8,128)(2,1)}, u32[]{:S(2)}, u32[]{:S(2)}) collective-permute-start(bf16[144,1536]{1,0:T(8,128)(2,1)} %get-tuple-element.109), channel_id=1, source_target_pairs={{0,16},{8,24},{16,0},{24,8},{1,17},{9,25},{17,1},{25,9},{2,18},{10... | collective-permute-start | bytes 1327112 | tf_op jit(solution)/shard_map/ppermute | solution.py:593
  483.1 21.5 %collective-permute-start.19 = (bf16[48,1536]{1,0:T(8,128)(2,1)}, bf16[48,1536]{1,0:T(8,128)(2,1)}, u32[]{:S(2)}, u32[]{:S(2)}) collective-permute-start(bf16[48,1536]{1,0:T(8,128)(2,1)} %get-tuple-element.141), channel_id=1, source_target_pairs={{0,24},{8,16},{16,8},{24,0},{1,25},{9,17},{17,9},{25,1},{2,26},{10... | collective-permute-start | bytes 442376 | tf_op jit(solution)/shard_map/ppermute | solution.py:593
  484.6 24.0 %collective-permute-start.18 = (bf16[48,1536]{1,0:T(8,128)(2,1)}, bf16[48,1536]{1,0:T(8,128)(2,1)}, u32[]{:S(2)}, u32[]{:S(2)}) collective-permute-start(bf16[48,1536]{1,0:T(8,128)(2,1)} %get-tuple-element.142), channel_id=1, source_target_pairs={{0,16},{8,24},{16,0},{24,8},{1,17},{9,25},{17,1},{25,9},{2,18},{10... | collective-permute-start | bytes 442376 | tf_op jit(solution)/shard_map/ppermute | solution.py:593
  484.9 26.0 %collective-permute-start.17 = (bf16[48,1536]{1,0:T(8,128)(2,1)}, bf16[48,1536]{1,0:T(8,128)(2,1)}, u32[]{:S(2)}, u32[]{:S(2)}) collective-permute-start(bf16[48,1536]{1,0:T(8,128)(2,1)} %get-tuple-element.143), channel_id=1, source_target_pairs={{0,8},{8,0},{16,24},{24,16},{1,9},{9,1},{17,25},{25,17},{2,10},{10... | collective-permute-start | bytes 442376 | tf_op jit(solution)/shard_map/ppermute | solution.py:593
  508.6 14.3 %collective-permute-start.12 = (bf16[2,192,320]{2,1,0:T(8,128)(2,1)S(1)}, bf16[2,192,320]{2,1,0:T(8,128)(2,1)}, u32[]{:S(2)}, u32[]{:S(2)}) collective-permute-start(bf16[2,192,320]{2,1,0:T(8,128)(2,1)S(1)} %get-tuple-element.116), channel_id=1, source_target_pairs={{0,6},{1,7},{2,0},{3,1},{4,2},{5,3},{6,4},{7,5},{8,14},{9,15},{10,... | collective-permute-start | bytes 737288 | tf_op jit(solution)/shard_map/ppermute | solution.py:583
  510.9 31.1 %collective-permute-start.11 = (bf16[2,192,320]{2,1,0:T(8,128)(2,1)S(1)}, bf16[2,192,320]{2,1,0:T(8,128)(2,1)}, u32[]{:S(2)}, u32[]{:S(2)}) collective-permute-start(bf16[2,192,320]{2,1,0:T(8,128)(2,1)S(1)} %get-tuple-element.117), channel_id=1, source_target_pairs={{0,4},{1,5},{2,6},{3,7},{4,0},{5,1},{6,2},{7,3},{8,12},{9,13},{10,... | collective-permute-start | bytes 737288 | tf_op jit(solution)/shard_map/ppermute | solution.py:583
  516.3 27.0 %collective-permute-start.20 = (bf16[48,1536]{1,0:T(8,128)(2,1)S(1)}, bf16[48,1536]{1,0:T(8,128)(2,1)S(1)}, u32[]{:S(2)}, u32[]{:S(2)}) collective-permute-start(bf16[48,1536]{1,0:T(8,128)(2,1)S(1)} %get-tuple-element.137), channel_id=1, source_target_pairs={{0,2},{1,3},{2,4},{3,5},{4,6},{5,7},{6,0},{7,1},{8,10},{9,11},{10,... | collective-permute-start | bytes 442376 | tf_op jit(solution)/shard_map/ppermute | solution.py:583
  523.0 22.1 %collective-permute-start.21 = (bf16[48,1536]{1,0:T(8,128)(2,1)S(1)}, bf16[48,1536]{1,0:T(8,128)(2,1)S(1)}, u32[]{:S(2)}, u32[]{:S(2)}) collective-permute-start(bf16[48,1536]{1,0:T(8,128)(2,1)S(1)} %get-tuple-element.138), channel_id=1, source_target_pairs={{0,4},{1,5},{2,6},{3,7},{4,0},{5,1},{6,2},{7,3},{8,12},{9,13},{10,... | collective-permute-start | bytes 442376 | tf_op jit(solution)/shard_map/ppermute | solution.py:583
  543.4 14.7 %collective-permute-start.33 = (bf16[144,1536]{1,0:T(8,128)(2,1)S(1)}, bf16[144,1536]{1,0:T(8,128)(2,1)S(1)}, u32[]{:S(2)}, u32[]{:S(2)}) collective-permute-start(bf16[144,1536]{1,0:T(8,128)(2,1)S(1)} %copy-done.26), channel_id=1, source_target_pairs={{0,8},{8,0},{16,24},{24,16},{1,9},{9,1},{17,25},{25,17},{2,10},{10... | collective-permute-start | bytes 1327112 | tf_op jit(solution)/shard_map/ppermute | solution.py:593
  545.1 33.0 %collective-permute-start.26 = (bf16[2,192,1152]{2,1,0:T(8,128)(2,1)}, bf16[2,192,1152]{2,1,0:T(8,128)(2,1)}, u32[]{:S(2)}, u32[]{:S(2)}) collective-permute-start(bf16[2,192,1152]{2,1,0:T(8,128)(2,1)} %get-tuple-element.93), channel_id=1, source_target_pairs={{0,2},{1,3},{2,4},{3,5},{4,6},{5,7},{6,0},{7,1},{8,10},{9,11},{10,... | collective-permute-start | bytes 2654216 | tf_op jit(solution)/shard_map/ppermute | solution.py:583
  553.4 35.4 %collective-permute-start.28 = (bf16[2,192,1152]{2,1,0:T(8,128)(2,1)}, bf16[2,192,1152]{2,1,0:T(8,128)(2,1)}, u32[]{:S(2)}, u32[]{:S(2)}) collective-permute-start(bf16[2,192,1152]{2,1,0:T(8,128)(2,1)} %get-tuple-element.94), channel_id=1, source_target_pairs={{0,6},{1,7},{2,0},{3,1},{4,2},{5,3},{6,4},{7,5},{8,14},{9,15},{10,... | collective-permute-start | bytes 2654216 | tf_op jit(solution)/shard_map/ppermute | solution.py:583
  566.2 79.5 %collective-permute-start.27 = (bf16[2,192,1152]{2,1,0:T(8,128)(2,1)}, bf16[2,192,1152]{2,1,0:T(8,128)(2,1)}, u32[]{:S(2)}, u32[]{:S(2)}) collective-permute-start(bf16[2,192,1152]{2,1,0:T(8,128)(2,1)} %get-tuple-element.95), channel_id=1, source_target_pairs={{0,4},{1,5},{2,6},{3,7},{4,0},{5,1},{6,2},{7,3},{8,12},{9,13},{10,... | collective-permute-start | bytes 2654216 | tf_op jit(solution)/shard_map/ppermute | solution.py:583
  571.2 78.0 %collective-permute-start.36 = (bf16[144,1536]{1,0:T(8,128)(2,1)}, bf16[144,1536]{1,0:T(8,128)(2,1)}, u32[]{:S(2)}, u32[]{:S(2)}) collective-permute-start(bf16[144,1536]{1,0:T(8,128)(2,1)} %get-tuple-element.104), channel_id=1, source_target_pairs={{0,2},{1,3},{2,4},{3,5},{4,6},{5,7},{6,0},{7,1},{8,10},{9,11},{10,... | collective-permute-start | bytes 1327112 | tf_op jit(solution)/shard_map/ppermute | solution.py:583
  572.0 83.1 %collective-permute-start.37 = (bf16[144,1536]{1,0:T(8,128)(2,1)}, bf16[144,1536]{1,0:T(8,128)(2,1)}, u32[]{:S(2)}, u32[]{:S(2)}) collective-permute-start(bf16[144,1536]{1,0:T(8,128)(2,1)} %get-tuple-element.105), channel_id=1, source_target_pairs={{0,4},{1,5},{2,6},{3,7},{4,0},{5,1},{6,2},{7,3},{8,12},{9,13},{10,... | collective-permute-start | bytes 1327112 | tf_op jit(solution)/shard_map/ppermute | solution.py:583
  579.0 76.2 %collective-permute-start.38 = (bf16[144,1536]{1,0:T(8,128)(2,1)S(1)}, bf16[144,1536]{1,0:T(8,128)(2,1)S(1)}, u32[]{:S(2)}, u32[]{:S(2)}) collective-permute-start(bf16[144,1536]{1,0:T(8,128)(2,1)S(1)} %copy-done.27), channel_id=1, source_target_pairs={{0,6},{1,7},{2,0},{3,1},{4,2},{5,3},{6,4},{7,5},{8,14},{9,15},{10,... | collective-permute-start | bytes 1327112 | tf_op jit(solution)/shard_map/ppermute | solution.py:583
  648.9 12.0 %collective-permute-start.29 = (bf16[192,1152]{1,0:T(8,128)(2,1)S(1)}, bf16[192,1152]{1,0:T(8,128)(2,1)S(1)}, u32[]{:S(2)}, u32[]{:S(2)}) collective-permute-start(bf16[192,1152]{1,0:T(8,128)(2,1)S(1)} %get-tuple-element.126), channel_id=1, source_target_pairs={{0,1},{1,0},{2,3},{3,2},{4,5},{5,4},{6,7},{7,6},{8,9},{9,8},{10,11... | collective-permute-start | bytes 1327112 | tf_op jit(solution)/shard_map/ppermute | solution.py:588
  657.3 13.4 %collective-permute-start.40 = (bf16[144,1536]{1,0:T(8,128)(2,1)}, bf16[144,1536]{1,0:T(8,128)(2,1)}, u32[]{:S(2)}, u32[]{:S(2)}) collective-permute-start(bf16[144,1536]{1,0:T(8,128)(2,1)} %fusion.9), channel_id=1, source_target_pairs={{0,16},{8,24},{16,0},{24,8},{1,17},{9,25},{17,1},{25,9},{2,18},{10... | collective-permute-start | bytes 1327112 | tf_op jit(solution)/shard_map/ppermute | solution.py:593
  662.0 26.6 %collective-permute-start.31 = (bf16[192,2,1152]{2,0,1:T(8,128)(2,1)}, bf16[192,2,1152]{2,0,1:T(8,128)(2,1)}, u32[]{:S(2)}, u32[]{:S(2)}) collective-permute-start(bf16[192,2,1152]{2,0,1:T(8,128)(2,1)} %maximum_select_fusion.3), channel_id=1, source_target_pairs={{0,16},{8,24},{16,0},{24,8},{1,17},{9,25},{17,1},{25,9},{2,18},{10... | collective-permute-start | bytes 2654216 | tf_op jit(solution)/shard_map/ppermute | solution.py:593
  668.3 20.3 %collective-permute-start.39 = (bf16[144,1536]{1,0:T(8,128)(2,1)}, bf16[144,1536]{1,0:T(8,128)(2,1)S(1)}, u32[]{:S(2)}, u32[]{:S(2)}) collective-permute-start(bf16[144,1536]{1,0:T(8,128)(2,1)} %fusion.9), channel_id=1, source_target_pairs={{0,8},{8,0},{16,24},{24,16},{1,9},{9,1},{17,25},{25,17},{2,10},{10... | collective-permute-start | bytes 1327112 | tf_op jit(solution)/shard_map/ppermute | solution.py:593
  670.7 17.9 %collective-permute-start.41 = (bf16[144,1536]{1,0:T(8,128)(2,1)}, bf16[144,1536]{1,0:T(8,128)(2,1)S(1)}, u32[]{:S(2)}, u32[]{:S(2)}) collective-permute-start(bf16[144,1536]{1,0:T(8,128)(2,1)} %collective-permute-done.40), channel_id=1, source_target_pairs={{0,8},{8,0},{16,24},{24,16},{1,9},{9,1},{17,25},{25,17},{2,10},{10... | collective-permute-start | bytes 1327112 | tf_op jit(solution)/shard_map/ppermute | solution.py:593
  673.1 20.0 %collective-permute-start.30 = (bf16[192,2,1152]{2,0,1:T(8,128)(2,1)}, bf16[192,2,1152]{2,0,1:T(8,128)(2,1)}, u32[]{:S(2)}, u32[]{:S(2)}) collective-permute-start(bf16[192,2,1152]{2,0,1:T(8,128)(2,1)} %maximum_select_fusion.3), channel_id=1, source_target_pairs={{0,8},{8,0},{16,24},{24,16},{1,9},{9,1},{17,25},{25,17},{2,10},{10... | collective-permute-start | bytes 2654216 | tf_op jit(solution)/shard_map/ppermute | solution.py:593
  (63 other events, 557.8 us)

commit v2 on v0

v2 whole, which is shorter than its diff:
```python
import functools

import jax
import jax.numpy as jnp
from jax import lax
from jax.experimental import pallas as pl
from jax.experimental.pallas import tpu as pltpu
from jax.sharding import PartitionSpec as P

HEADS = 24
KV_HEADS = 8
HEAD_DIM = 64
GROUP = HEADS // KV_HEADS
Q_COLS = GROUP * HEAD_DIM
HEAD_COLS = Q_COLS + 2 * HEAD_DIM

EPS = 1e-05
THETA = 1000000.0
MESH = pl.DeviceIdType.MESH
F32 = jnp.float32
BF16 = jnp.bfloat16

VMEM = pl.BlockSpec(memory_space=pltpu.VMEM)
ANY = pl.BlockSpec(memory_space=pl.ANY)


def here():
    rep = lax.axis_index("rep")
    grp = lax.axis_index("grp")
    r = rep % 4
    return rep - r, r // 2, r % 2, grp // 2, grp % 2


def device(base, y, c, z, x):
    return {"rep": base + 2 * y + c, "grp": 2 * z + x}


def remote(src, dst, send, recv, to):
    return pltpu.make_async_remote_copy(
        src_ref=src, dst_ref=dst, send_sem=send, recv_sem=recv, device_id=to, device_id_type=MESH
    )


def greet(targets):
    barrier = pltpu.get_barrier_semaphore()
    for to in targets:
        pl.semaphore_signal(barrier, inc=1, device_id=to, device_id_type=MESH)
    pl.semaphore_wait(barrier, len(targets))


def neighbours():
    base, y, c, z, x = here()
    to_c = device(base, y, 1 - c, z, x)
    to_x = device(base, y, c, z, 1 - x)
    to_y = device(base, 1 - y, c, z, x)
    return to_c, to_x, to_y


GATHER_SEMS = 8


class Gather:
    def __init__(self, src, out, send, recv, local):
        self.src, self.out, self.send, self.recv, self.local = src, out, send, recv, local
        _, y, c, _, x = here()
        self.to_c, self.to_x, self.to_y = neighbours()
        slot = lambda a, b, d: 4 * a + 2 * b + d
        self.own = slot(y, c, x)
        self.at_c, self.at_x, self.at_y = slot(y, 1 - c, x), slot(y, c, 1 - x), slot(1 - y, c, x)
        self.at_xc, self.at_yc = slot(y, 1 - c, 1 - x), slot(1 - y, 1 - c, x)
        self.at_xy, self.at_xyc = slot(1 - y, c, 1 - x), slot(1 - y, 1 - c, 1 - x)
        self.half = src.shape[0] // 2

    def part(self, ref, k):
        return ref.at[pl.ds(k * self.half, self.half)]

    def copy(self, k, src, dst, to):
        return remote(src, dst, self.send.at[k], self.recv.at[k], to)

    def start(self):
        out, src = self.out, self.src
        self.keep = pltpu.make_async_copy(src, out.at[self.own], self.local)
        self.keep.start()
        self.sent = [
            self.copy(0, src, out.at[self.own], self.to_x),
            self.copy(1, src, out.at[self.own], self.to_y),
            self.copy(2, src, out.at[self.own], self.to_c),
        ]
        for copy in self.sent:
            copy.start()

    def forward(self):
        out = self.out
        self.copy(0, self.src, out.at[self.at_x], self.to_x).wait_recv()
        first = self.part(out.at[self.at_x], 0)
        self.go(3, first, first, self.to_y)
        self.go(4, out.at[self.at_x], out.at[self.at_x], self.to_c)
        self.copy(1, self.src, out.at[self.at_y], self.to_y).wait_recv()
        second = self.part(out.at[self.at_y], 1)
        self.go(5, second, second, self.to_x)
        self.go(6, out.at[self.at_y], out.at[self.at_y], self.to_c)

    def go(self, k, src, dst, to):
        copy = self.copy(k, src, dst, to)
        copy.start()
        self.sent.append(copy)

    def finish(self):
        out = self.out
        first = self.part(out.at[self.at_xy], 0)
        second = self.part(out.at[self.at_xy], 1)
        self.copy(3, first, first, self.to_y).wait_recv()
        self.copy(5, second, second, self.to_x).wait_recv()
        self.go(7, out.at[self.at_xy], out.at[self.at_xy], self.to_c)
        for k, at in ((2, self.at_c), (4, self.at_xc), (6, self.at_yc), (7, self.at_xyc)):
            self.copy(k, out.at[at], out.at[at], self.to_c).wait_recv()
        for copy in self.sent:
            copy.wait_send()
        self.keep.wait()


def dma(n):
    return pltpu.SemaphoreType.DMA((n,))


def params(cid, limit=60):
    return pltpu.CompilerParams(
        collective_id=cid, has_side_effects=True, vmem_limit_bytes=limit * 2**20
    )


def inverse_rms(v):
    return lax.rsqrt(jnp.mean(v * v, axis=-1, keepdims=True) + EPS)


def norm_back(dy, v, inv, gain):
    scaled = dy * gain
    gain_grad = jnp.sum(dy * v * inv, axis=0, keepdims=True)
    inner = jnp.mean(scaled * v, axis=-1, keepdims=True)
    return inv * scaled - v * inv * inv * inv * inner, gain_grad


def when(cond):
    return pl.when(cond)


def lanes(shape):
    return lax.broadcasted_iota(jnp.int32, shape, len(shape) - 1)


def roll(v, by):
    return pltpu.roll(v, by % v.shape[-1], v.ndim - 1)


class Along:
    def __init__(self, src, slot, send, recv, flip=False, mate=None):
        self.src, self.slot, self.send, self.recv = src, slot, send, recv
        self.base, self.y, self.c, self.z, self.x = here()
        self.to = (1 - self.x) if flip else self.x
        self.got = mate if flip else slot
        self.flip = flip

    def at(self, zk, x):
        return device(self.base, self.y, self.c, zk, x)

    def copy(self, d):
        zk = (self.z + d + 4) % 4
        return remote(self.src, self.slot(self.z), self.send.at[d + 2], self.recv.at[self.z],
                      self.at(zk, self.to))

    def fits(self, d):
        return (self.z + d >= 0) & (self.z + d < 4)

    def start(self):
        if self.flip:
            self.copy(0).start()
        for d in (2, -2, 1, -1):
            pl.when(self.fits(d))(lambda d=d: self.copy(d).start())

    def arrival(self, zk):
        ref = self.got(zk)
        return remote(ref, ref, self.send.at[0], self.recv.at[zk], self.at(self.z, 1 - self.x))

    def passed(self, zk, to):
        ref = self.got(zk)
        return remote(ref, ref, self.send.at[5], self.recv.at[zk], self.at(to, self.x))

    def forward(self):
        @pl.when(self.z == 2)
        def _():
            self.arrival(0).wait_recv()
            self.passed(0, 3).start()

        @pl.when(self.z == 1)
        def _():
            self.arrival(3).wait_recv()
            self.passed(3, 0).start()

    def wait(self, zk):
        early = ((self.z == 2) & (zk == 0)) | ((self.z == 1) & (zk == 3))
        due = jnp.logical_not(early)
        if not self.flip:
            due = due & (self.z != zk)
        pl.when(due)(lambda: self.arrival(zk).wait_recv())

    def finish(self):
        for zk in range(4):
            self.wait(zk)

    def sent(self):
        if self.flip:
            self.copy(0).wait_send()
        for d in (2, -2, 1, -1):
            pl.when(self.fits(d))(lambda d=d: self.copy(d).wait_send())
        pl.when(self.z == 2)(lambda: self.passed(0, 3).wait_send())
        pl.when(self.z == 1)(lambda: self.passed(3, 0).wait_send())


def layer_mates():
    base, y, c, z, x = here()
    return [
        device(base, (y + k // 4) % 2, (c + k // 2) % 2, z, (x + k) % 2) for k in range(1, 8)
    ]


def z_mates():
    base, y, c, z, x = here()
    return [device(base, y, c, (z + k // 2) % 4, (x + k) % 2) for k in range(2, 8)]


def rotated(u, cos, sin):
    lane = lanes(u.shape)
    return u * cos + jnp.where(lane < 32, roll(u, -32), roll(u, 32)) * sin


def low_half(v):
    return jnp.where(lanes(v.shape) < HEAD_DIM, v, 0.0)


def high_half(v):
    return jnp.where(lanes(v.shape) >= HEAD_DIM, v, 0.0)


def split_heads(tile_a, tile_b):
    return [low_half(tile_a), low_half(roll(tile_a, 64)), low_half(tile_b),
            low_half(roll(tile_b, 64))]


def head_inverse(u):
    return lax.rsqrt(jnp.sum(u * u, axis=-1, keepdims=True) * (1.0 / HEAD_DIM) + EPS)


def exp_scores(q, kv, q_seg, k_seg, diagonal):
    s = lax.dot_general(q, kv, (((1,), (1,)), ((), ())), preferred_element_type=F32)
    allowed = q_seg == k_seg
    if diagonal:
        row = lax.broadcasted_iota(jnp.int32, allowed.shape, 0)
        col = lax.broadcasted_iota(jnp.int32, allowed.shape, 1)
        allowed = allowed & (col <= row)
    n = allowed.shape[0]
    return jnp.concatenate([
        jnp.where(allowed, jnp.exp(s[n * j:n * (j + 1)]), 0.0) for j in range(GROUP)], axis=0)


def segment_row(segs, zk, s):
    return jnp.concatenate([segs[zk, 2 * s, 0:1], segs[zk, 2 * s + 1, 0:1]], axis=1)


def segment_columns(segs, zk, s):
    parts = []
    for i in range(2):
        row = jnp.broadcast_to(segs[zk, 2 * s + i, 0:1], (128, 128))
        parts.append(jnp.transpose(row))
    col = jnp.concatenate(parts, axis=0)
    return jnp.concatenate([col, col], axis=1)


class SeqSum:
    def __init__(self, part, scratch):
        self.part = part
        (self.r1, self.chip, self.rx, self.ry, self.mine, self.late, self.out,
         self.send, self.recv) = scratch
        _, self.y, self.c, _, self.x = here()
        self.to_c, self.to_x, self.to_y = neighbours()

    def copy(self, k, src, dst, to):
        return remote(src, dst, self.send.at[k], self.recv.at[k], to)

    def swap(self, b, a):
        at = 2 * b + a
        return self.copy(at, self.part.at[4 * b + 2 * (1 - self.c) + a], self.r1.at[at], self.to_c)

    def give(self, b):
        for a in range(2):
            self.swap(b, a).start()

    def along_x(self, b):
        at = 2 * b + 1 - self.x
        return self.copy(4 + b, self.chip.at[at, pl.ds(0, 64)], self.rx.at[b], self.to_x)

    def along_y(self, a):
        at = 2 * (1 - self.y) + a
        return self.copy(6 + a, self.chip.at[at, pl.ds(64, 64)], self.ry.at[a], self.to_y)

    def last_y(self):
        return self.copy(8, self.mine.at[0], self.late.at[0], self.to_y)

    def last_x(self):
        return self.copy(9, self.mine.at[1], self.late.at[1], self.to_x)

    def total(self, b, a):
        self.swap(b, a).wait_recv()
        at = 2 * b + a
        return self.part[4 * b + 2 * self.c + a].astype(F32) + self.r1[at].astype(F32)

    def take_far(self):
        b = 1 - self.y
        for a in (1 - self.x, self.x):
            self.chip[2 * b + a] = self.total(b, a).astype(BF16)
            self.along_y(a).start()
            if a is not self.x:
                self.along_x(b).start()

    def take_near(self):
        b, x = self.y, self.x
        self.chip[2 * b + 1 - x] = self.total(b, 1 - x).astype(BF16)
        self.along_x(b).start()
        self.out[...] = self.total(b, x)

    def middle(self):
        x, y = self.x, self.y
        self.along_x(1 - y).wait_recv()
        self.mine[0] = (
            self.chip[2 * (1 - y) + x, 0:64].astype(F32) + self.rx[1 - y].astype(F32)
        ).astype(BF16)
        self.last_y().start()
        self.along_y(1 - x).wait_recv()
        self.mine[1] = (
            self.chip[2 * y + 1 - x, 64:128].astype(F32) + self.ry[1 - x].astype(F32)
        ).astype(BF16)
        self.last_x().start()

    def finish(self):
        x, y = self.x, self.y
        self.along_x(y).wait_recv()
        self.along_y(x).wait_recv()
        self.last_y().wait_recv()
        self.last_x().wait_recv()
        self.out[0:64] += self.rx[y].astype(F32) + self.late[0].astype(F32)
        self.out[64:128] += self.ry[x].astype(F32) + self.late[1].astype(F32)

    def sent(self):
        for b in range(2):
            for a in range(2):
                self.swap(b, a).wait_send()
            self.along_x(b).wait_send()
            self.along_y(b).wait_send()
        self.last_y().wait_send()
        self.last_x().wait_send()


def seq_scratch(width):
    return [
        pltpu.VMEM((4, 128, width), BF16),
        pltpu.VMEM((4, 128, width), BF16),
        pltpu.VMEM((2, 64, width), BF16),
        pltpu.VMEM((2, 64, width), BF16),
        pltpu.VMEM((2, 64, width), BF16),
        pltpu.VMEM((2, 64, width), BF16),
        pltpu.VMEM((128, width), F32),
        dma(10),
        dma(10),
    ]


FWD_IN = ("tok", "cot", "seg", "wq", "gains", "wgu", "wd", "wo", "qg", "kg", "cos", "sin")
FWD_OUT = ("normed", "cot_all", "n2_all", "wq_all", "wo_all", "wd_all", "wgu_all", "qkv", "q",
           "kv", "segs", "o", "att", "mid", "g_one", "g_two",
           "gains_all")


def forward_kernel(names, *refs):
    m = dict(zip(names, refs))
    base, y, c, z, x = here()
    r = 2 * y + c
    to_c, to_x, to_y = neighbours()
    greet(layer_mates() + z_mates())
    rows, width = m["tok"].shape
    quarter_d, quarter_o = m["wd"].shape[0] // 4, m["wo"].shape[0] // 4
    own_rows = m["wq"].shape[1]
    half_cols = m["wgu"].shape[1] // 2
    piece = m["raw"].shape[2]
    part = piece // 2
    keep = m["keep"]
    own = 2 * z + x
    t_own = 2 * r + x

    def local_copy(k, src, dst):
        return pltpu.make_async_copy(src, dst, keep.at[k])

    tok = Gather(m["tok"], m["tok_all"], m["ga_s"], m["ga_r"], keep.at[0])
    cot = Gather(m["cot"], m["cot_all"], m["gb_s"], m["gb_r"], keep.at[1])
    tok.start()
    segs = m["segs_v"]
    mates = layer_mates()

    def seg_copy(k):
        return remote(m["seg"], segs.at[z, t_own], m["sg_s"].at[k - 1], m["sg_r"].at[k - 1],
                      mates[k - 1])

    def gain_target(k):
        return device(base, y, c, (z + k // 2) % 4, (x + k) % 2)

    def gain_copy(k):
        return remote(m["gains"], m["gains_all"].at[own], m["gn_s"].at[k - 1],
                      m["gn_r"].at[k - 1], gain_target(k))

    for k in range(1, 8):
        seg_copy(k).start()
    wq = m["wq_v"]

    def wq_slot(zk, a):
        return wq.at[pl.ds((2 * zk + a) * own_rows, own_rows)]

    near = Along(m["wq"].at[x], lambda zk: wq_slot(zk, x), m["wa_s"], m["wa_r"])
    flip = Along(m["wq"].at[1 - x], lambda zk: wq_slot(zk, x), m["wb_s"], m["wb_r"],
                 flip=True, mate=lambda zk: wq_slot(zk, 1 - x))
    near.start()
    flip.start()
    for k in range(1, 8):
        gain_copy(k).start()
    local = [
        local_copy(2, m["wq"].at[x], wq_slot(z, x)),
        local_copy(3, m["gains"], m["gains_all"].at[own]),
        local_copy(4, m["seg"], segs.at[z, t_own]),
        local_copy(5, m["wgu"].at[:, pl.ds(piece * r, piece)], m["raw"].at[0]),
        local_copy(6, m["wgu"].at[:, pl.ds(half_cols + piece * r, piece)], m["raw"].at[1]),
    ]
    for copy in local:
        copy.start()
    out_q = Along(m["wo"].at[pl.ds(quarter_o * r, quarter_o)], lambda zk: m["zo"].at[zk],
                  m["wo_s"], m["wo_r"])
    down_q = Along(m["wd"].at[pl.ds(quarter_d * r, quarter_d)], lambda zk: m["zd"].at[zk],
                   m["wd_s"], m["wd_r"])
    out_q.start()
    quarters = [
        local_copy(7, m["wo"].at[pl.ds(quarter_o * r, quarter_o)], m["zo"].at[z]),
        local_copy(8, m["wd"].at[pl.ds(quarter_d * r, quarter_d)], m["zd"].at[z]),
    ]
    for copy in quarters:
        copy.start()

    local[3].wait()
    local[4].wait()
    gate, up = m["raw"].at[0], m["raw"].at[1]
    pair = m["pair"]
    main = (part // 128) * 128
    for a in range(2):
        at = a * (piece - main)
        pair[a, :, 0:main] = gate[:, at:at + main]
        pair[a, :, main:2 * main] = up[:, at:at + main]
    g_tile = gate[:, main:main + 128].astype(F32)
    u_tile = up[:, main:main + 128].astype(F32)
    low = lanes(g_tile.shape) < HEAD_DIM
    pair[0, :, 2 * main:] = jnp.where(low, g_tile, roll(u_tile, 64)).astype(BF16)
    pair[1, :, 2 * main:] = jnp.where(low, roll(g_tile, 64), u_tile).astype(BF16)
    wgu = m["wgu_all"]

    def gu_rows(zk, a):
        return wgu.at[pl.ds((2 * zk + a) * own_rows, own_rows)]

    def gu_unit(zk):
        return wgu.at[pl.ds(2 * zk * own_rows, 2 * own_rows)]

    cross = remote(pair.at[1 - x], gu_rows(z, x), m["xc_s"], m["xc_r"], to_x)
    cross_in = remote(pair.at[x], gu_rows(z, 1 - x), m["xc_s"], m["xc_r"], to_x)
    cross.start()
    mine = local_copy(5, pair.at[x], gu_rows(z, x))
    mine.start()

    tok.forward()
    near.forward()
    flip.forward()
    tok.finish()
    cot.start()
    near.finish()
    flip.finish()
    down_q.start()
    out_q.forward()
    for k in range(1, 8):
        at = 2 * ((z + 4 - k // 2) % 4) + (x + k) % 2
        remote(m["gains"], m["gains_all"].at[at], m["gn_s"].at[k - 1], m["gn_r"].at[k - 1],
               to_c).wait_recv()
        seg_copy(k).wait_recv()
    for k in (0, 1, 2):
        local[k].wait()
    gather_gains = pltpu.make_async_copy(m["gains_all"], m["gains_v"], keep.at[3])
    gather_gains.start()
    gather_gains.wait()
    gain_rows = []
    for i in range(2):
        gain_rows.append(jnp.concatenate(
            [m["gains_v"][k, 0:16].astype(F32)[i:i + 1, :own_rows] for k in range(8)], axis=1))
    m["g_one"][...], m["g_two"][...] = gain_rows
    kv = m["kv_v"]
    q_all, qkv_all = m["q_v"], m["qkv_v"]
    qg, kg, cos, sin = m["qg"][...], m["kg"][...], m["cos"][...], m["sin"][...]
    span = 2 * rows

    def order(k):
        return (y + 1 + k) % 2, (c + 1 + k // 2) % 2

    def kv_copy(d, s):
        return remote(kv.at[z, s], kv.at[z, s], m["kv_s"].at[d - 1, s], m["kv_r"].at[z, s],
                      device(base, y, c, (z + d) % 4, x))

    def kv_pass(s):
        return remote(kv.at[0, s], kv.at[0, s], m["kv_s"].at[2, s], m["kv_r"].at[0, s],
                      device(base, y, c, 3, x))

    def kv_arrival(zk, s):
        return remote(kv.at[zk, s], kv.at[zk, s], m["kv_s"].at[0, s], m["kv_r"].at[zk, s], to_x)

    def seg_up(k):
        return remote(segs.at[z], segs.at[z], m["su_s"].at[k - 1], m["su_r"].at[z],
                      device(base, y, c, (z + k) % 4, x))

    for k in range(1, 4):
        pl.when(z + k < 4)(lambda k=k: seg_up(k).start())

    def project(k, carry):
        b, e = order(k)
        s = 2 * b + e
        tokens = m["tok_all"][pl.ds(2 * s, 2)].reshape(span, width).astype(F32)
        normed = (tokens * inverse_rms(tokens) * m["g_one"][...]).astype(BF16)
        m["tok_all"][pl.ds(2 * s, 2)] = normed.reshape(2, rows, width)
        qkv = jnp.dot(normed, wq[...], preferred_element_type=F32)
        qkv_all[s] = qkv
        heads = split_heads(qkv[:, 0:128], qkv[:, 128:256])
        for j in range(GROUP):
            u = heads[j]
            u = rotated(u * head_inverse(u) * qg[0:1], cos, sin) * HEAD_DIM ** (-0.5)
            q_all[s, pl.ds(j * span, span)] = u.astype(BF16)
        u = heads[GROUP]
        u = rotated(u * head_inverse(u) * kg[0:1], cos, sin)
        v = jnp.concatenate([jnp.zeros((span, HEAD_DIM), F32), qkv[:, 256:320]], axis=1)
        kv[z, s] = (u + v).astype(BF16)
        for d in (2, 1):
            pl.when(z + d < 4)(lambda d=d: kv_copy(d, s).start())
        return carry

    lax.fori_loop(0, 4, project, 0)
    exports = [local_copy(9, m["tok_all"], m["normed"]), local_copy(10, wq, m["wq_all"]),
               local_copy(11, qkv_all, m["qkv"]), local_copy(12, q_all, m["q"])]
    for copy in exports:
        copy.start()

    mine.wait()
    cross_in.wait_recv()
    gu = Along(gu_unit(z), gu_unit, m["wg_s"], m["wg_r"])
    gu.start()
    cot.forward()

    def hand(k, zk, src, dst, sems, n):
        ss, rs = sems
        to = device(base, zk // 2, zk % 2, z, x)
        pl.when(r != zk)(lambda: remote(src.at[zk], dst.at[pl.ds(n * r, n)], ss.at[zk],
                                        rs.at[r], to).start())

        @pl.when(r == zk)
        def _():
            copy = local_copy(k, src.at[zk], dst.at[pl.ds(n * r, n)])
            copy.start()
            copy.wait()

    def handed(src, dst, sems, n):
        ss, rs = sems
        for rk in range(4):
            ref = dst.at[pl.ds(n * rk, n)]
            pl.when(r != rk)(lambda ref=ref, rk=rk: remote(
                src.at[0], ref, ss.at[0], rs.at[rk], to_x).wait_recv())

    def hand_sent(src, dst, sems, n):
        ss, rs = sems
        for zk in range(4):
            pl.when(r != zk)(lambda zk=zk: remote(
                src.at[zk], dst.at[pl.ds(0, n)], ss.at[zk], rs.at[0], to_x).wait_send())

    quarters[0].wait()
    out_q.finish()
    out_sems = (m["ho_s"], m["ho_r"])
    down_sems = (m["hd_s"], m["hd_r"])
    for zk in range(4):
        hand(13, zk, m["zo"], m["wo_v"], out_sems, quarter_o)

    for k in range(1, 4):
        pl.when(z - k >= 0)(lambda k=k: remote(
            segs.at[0], segs.at[(z + 4 - k) % 4], m["su_s"].at[k - 1],
            m["su_r"].at[(z + 4 - k) % 4], to_x).wait_recv())

    summed = SeqSum(m["part"], [m[n] for n in SUM_NAMES])
    o_all, att = m["o_v"], m["att_v"]
    acc, q_seg = m["acc"], m["q_seg"]

    def attend_one(k, carry):
        b, e = order(k)
        s = 2 * b + e
        q_seg[...] = segment_columns(segs, z, s)

        def block(zk, diagonal):
            tile = kv[zk, s]
            p = exp_scores(q_all[s], tile, q_seg[...], segment_row(segs, zk, s), diagonal)
            ones = jnp.where(lanes(tile.shape) < HEAD_DIM, 1.0, tile.astype(F32)).astype(BF16)
            add = jnp.dot(p.astype(BF16), ones, preferred_element_type=F32)
            if diagonal:
                acc[...] = add
            else:
                acc[...] += add

        block(z, True)

        @pl.when(z == 2)
        def _():
            kv_arrival(0, s).wait_recv()
            kv_pass(s).start()

        def step(i, inner):
            zk = z - 1 - i
            pl.when(jnp.logical_not((z == 2) & (zk == 0)))(
                lambda: kv_arrival(zk, s).wait_recv())
            block(zk, False)
            return inner

        lax.fori_loop(0, z, step, 0)
        total = acc[...]
        inv = 1.0 / jnp.where(lanes(total.shape) < HEAD_DIM, total, 1.0)
        inv = jnp.where(lanes(total.shape) < HEAD_DIM, inv, roll(inv, 64))
        o = total * inv
        o_all[s] = jnp.where(lanes(o.shape) < HEAD_DIM, inv, o)
        o = high_half(o)
        first, second, third = o[0:span], o[span:2 * span], o[2 * span:]
        att[s, :, 0:128] = (roll(first, 64) + second).astype(BF16)
        att[s, :, 128:192] = roll(third, 64)[:, 0:HEAD_DIM].astype(BF16)
        pl.when(k == 0)(lambda: handed(m["zo"], m["wo_v"], out_sems, quarter_o))
        out = jnp.dot(att[s], m["wo_v"][...], preferred_element_type=F32).astype(BF16)
        m["part"][pl.ds(2 * s, 2)] = out.reshape(2, rows, width)
        pl.when(k < 2)(lambda: summed.give(b))
        pl.when(k == 2)(summed.take_far)
        pl.when(k == 3)(summed.take_near)
        return carry

    lax.fori_loop(0, 4, attend_one, 0)
    more = [local_copy(14, o_all, m["o"]),
            local_copy(16, att, m["att"]), local_copy(17, kv, m["kv"]),
            local_copy(18, segs, m["segs"]), local_copy(19, m["wo_v"], m["wo_all"])]
    for copy in more:
        copy.start()
    down_q.forward()
    summed.middle()
    gu.forward()
    summed.finish()
    mid = m["tok"][...].astype(F32) + summed.out[...]
    m["mid"][...] = mid
    m["low"][...] = (mid * inverse_rms(mid) * m["g_two"][...]).astype(BF16)
    n2 = Gather(m["low"], m["n2_all"], m["gc_s"], m["gc_r"], keep.at[20])
    n2.start()
    quarters[1].wait()
    down_q.finish()
    for zk in range(4):
        hand(13, zk, m["zd"], m["wd_all"], down_sems, quarter_d)
    cot.finish()
    n2.forward()
    n2.finish()
    handed(m["zd"], m["wd_all"], down_sems, quarter_d)
    gu.finish()

    for along in (near, flip, out_q, down_q, gu):
        along.sent()
    summed.sent()
    cross.wait_send()
    for k in range(1, 8):
        seg_copy(k).wait_send()
        gain_copy(k).wait_send()
    for k in range(1, 4):
        pl.when(z + k < 4)(lambda k=k: seg_up(k).wait_send())

    def kv_sent(s, carry):
        for d in (1, 2):
            pl.when(z + d < 4)(lambda d=d: kv_copy(d, s).wait_send())
        pl.when(z == 2)(lambda: kv_pass(s).wait_send())
        return carry

    lax.fori_loop(0, 4, kv_sent, 0)
    hand_sent(m["zo"], m["wo_v"], out_sems, quarter_o)
    hand_sent(m["zd"], m["wd_all"], down_sems, quarter_d)
    for copy in exports + more:
        copy.wait()


SUM_NAMES = ("r1", "chip", "rx", "ry", "mine", "late", "sum_out", "sum_s", "sum_r")


def forward_call(tok, cot, seg, wq, gains, wgu, wd, wo, qg, kg, cos, sin):
    shape = jax.ShapeDtypeStruct
    rows, width = tok.shape
    span = 2 * rows
    own_rows = wq.shape[1]
    part = wgu.shape[1] // 16
    outs = {
        "normed": shape((8, rows, width), BF16),
        "cot_all": shape((8, rows, width), BF16),
        "n2_all": shape((8, rows, width), BF16),
        "wq_all": shape((width, HEAD_COLS), BF16),
        "wo_all": shape((Q_COLS, width), BF16),
        "wd_all": shape((part, width), BF16),
        "wgu_all": shape((width, 2 * part), BF16),
        "qkv": shape((4, span, HEAD_COLS), F32),
        "q": shape((4, GROUP * span, 128), BF16),
        "kv": shape((4, 4, span, 128), BF16),
        "segs": shape((4, 8) + seg.shape, seg.dtype),
        "o": shape((4, GROUP * span, 128), F32),
        "att": shape((4, span, Q_COLS), BF16),
        "mid": shape((rows, width), F32),
        "g_one": shape((1, width), F32),
        "g_two": shape((1, width), F32),
        "gains_all": shape((8,) + gains.shape, BF16),
    }
    sems = {
        "ga_s": dma(8), "ga_r": dma(8), "gb_s": dma(8), "gb_r": dma(8), "gc_s": dma(8),
        "gc_r": dma(8), "sg_s": dma(7), "sg_r": dma(7), "gn_s": dma(7), "gn_r": dma(7),
        "wa_s": dma(6), "wa_r": dma(4), "wb_s": dma(6), "wb_r": dma(4), "wo_s": dma(6),
        "wo_r": dma(4), "wd_s": dma(6), "wd_r": dma(4), "wg_s": dma(6), "wg_r": dma(4),
        "xc_s": pltpu.SemaphoreType.DMA, "xc_r": pltpu.SemaphoreType.DMA,
        "kv_s": pltpu.SemaphoreType.DMA((3, 4)), "kv_r": pltpu.SemaphoreType.DMA((4, 4)),
        "su_s": dma(3), "su_r": dma(4), "ho_s": dma(4), "ho_r": dma(4), "hd_s": dma(4),
        "hd_r": dma(4), "keep": dma(21),
    }
    buffers = {
        "tok_all": pltpu.VMEM((8, rows, width), BF16),
        "segs_v": pltpu.VMEM((4, 8) + seg.shape, seg.dtype),
        "wq_v": pltpu.VMEM((width, HEAD_COLS), BF16),
        "gains_v": pltpu.VMEM((8,) + gains.shape, BF16),
        "raw": pltpu.VMEM((2, own_rows, 2 * part), BF16),
        "pair": pltpu.VMEM((2, own_rows, 2 * part), BF16),
        "zo": pltpu.VMEM((4, wo.shape[0] // 4, width), BF16),
        "zd": pltpu.VMEM((4, wd.shape[0] // 4, width), BF16),
        "wo_v": pltpu.VMEM((Q_COLS, width), BF16),
        "qkv_v": pltpu.VMEM((4, span, HEAD_COLS), F32),
        "q_v": pltpu.VMEM((4, GROUP * span, 128), BF16),
        "kv_v": pltpu.VMEM((4, 4, span, 128), BF16),
        "o_v": pltpu.VMEM((4, GROUP * span, 128), F32),
        "att_v": pltpu.VMEM((4, span, Q_COLS), BF16),
        "acc": pltpu.VMEM((GROUP * span, 128), F32),
        "q_seg": pltpu.VMEM((span, span), jnp.int32),
        "part": pltpu.VMEM((8, rows, width), BF16),
        "low": pltpu.VMEM((rows, width), BF16),
    }
    buffers.update(zip(SUM_NAMES, seq_scratch(width)))
    names = FWD_IN + FWD_OUT + tuple(buffers) + tuple(sems)
    specs = {n: VMEM for n in ("tok", "seg", "gains", "wq", "qg", "kg", "cos", "sin")}
    outs_list = pl.pallas_call(
        functools.partial(forward_kernel, names),
        name="forward",
        out_shape=tuple(outs[n] for n in FWD_OUT),
        in_specs=[specs.get(n, ANY) for n in FWD_IN],
        out_specs=tuple(VMEM if n in ("mid", "g_one", "g_two") else ANY for n in FWD_OUT),
        scratch_shapes=list(buffers.values()) + list(sems.values()),
        compiler_params=params(0),
    )(tok, cot, seg, wq, gains, wgu, wd, wo, qg, kg, cos, sin)
    return dict(zip(FWD_OUT, outs_list))


class ZSum:
    def __init__(self, block, slot, send, recv):
        self.block, self.slot, self.send, self.recv = block, slot, send, recv
        self.base, self.y, self.c, self.z, self.x = here()

    def to(self, zk):
        return device(self.base, self.y, self.c, zk, self.x)

    def direct(self, zk):
        return remote(self.block(zk), self.slot(self.z), self.send.at[zk], self.recv.at[self.z],
                      self.to(zk))

    def far(self, zk, by):
        return remote(self.block(zk), self.slot(by), self.send.at[zk], self.recv.at[4],
                      self.to(by))

    def first(self, i):
        up = (self.z // 2)
        return up * i + (1 - up) * (3 - i)

    def start(self, zk):
        z = self.z
        late = ((z == 1) & (zk == 3)) | ((z == 2) & (zk == 0))
        end = ((z == 0) & (zk == 3)) | ((z == 3) & (zk == 0))
        pl.when((zk != z) & jnp.logical_not(late) & jnp.logical_not(end))(
            lambda: self.direct(zk).start())
        pl.when((z == 0) & (zk == 3))(lambda: self.far(3, 1).start())
        pl.when((z == 3) & (zk == 0))(lambda: self.far(0, 2).start())

    def merge(self, add):
        @pl.when(self.z == 1)
        def _():
            self.far(3, 1).wait_recv()
            add(self.block(3), self.slot(1))
            self.direct(3).start()

        @pl.when(self.z == 2)
        def _():
            self.far(0, 2).wait_recv()
            add(self.block(0), self.slot(2))
            self.direct(0).start()

    def arrive(self, zk):
        ref = self.slot(zk)
        remote(ref, ref, self.send.at[0], self.recv.at[zk], self.to(zk)).wait_recv()

    def middle(self):
        return (self.z == 1) | (self.z == 2)

    def wait(self):
        z = self.z

        @pl.when(self.middle())
        def _():
            for zk in (z - 1, z + 1, (z + 2) % 4):
                self.arrive(zk)

        @pl.when(jnp.logical_not(self.middle()))
        def _():
            for zk in (1, 2):
                self.arrive(zk)

    def collect(self, total):
        z = self.z
        pl.when(self.middle())(
            lambda: total([self.slot(zk) for zk in (z - 1, z + 1, (z + 2) % 4)]))
        pl.when(jnp.logical_not(self.middle()))(
            lambda: total([self.slot(zk) for zk in (1, 2)]))

    def sent(self):
        for zk in range(4):
            pl.when(self.z != zk)(lambda zk=zk: self.direct(zk).wait_send())


class RepShare:
    def __init__(self, at, send, recv):
        self.at, self.send, self.recv = at, send, recv
        _, self.y, self.c, _, _ = here()
        self.to_c, _, self.to_y = neighbours()
        self.r = 2 * self.y + self.c

    def copy(self, k, r, to):
        return remote(self.at(r), self.at(r), self.send.at[k], self.recv.at[k], to)

    def start(self):
        self.copy(0, self.r, self.to_y).start()
        self.copy(1, self.r, self.to_c).start()

    def forward(self):
        other = 2 * (1 - self.y) + self.c
        self.copy(0, other, self.to_y).wait_recv()
        self.copy(2, other, self.to_c).start()

    def finish(self):
        self.copy(1, 2 * self.y + 1 - self.c, self.to_c).wait_recv()
        self.copy(2, 2 * (1 - self.y) + 1 - self.c, self.to_c).wait_recv()

    def sent(self):
        self.copy(0, self.r, self.to_y).wait_send()
        self.copy(1, self.r, self.to_c).wait_send()
        self.copy(2, self.r, self.to_c).wait_send()


def first_dims(left, right):
    return lax.dot_general(left, right, (((0,), (0,)), ((), ())), preferred_element_type=F32)


def last_dims(left, right):
    return lax.dot_general(left, right, (((1,), (1,)), ((), ())), preferred_element_type=F32)


def head_back(dy, u, gain):
    inv = head_inverse(u)
    scaled = dy * gain
    gain_grad = jnp.sum(dy * u * inv, axis=0, keepdims=True)
    inner = jnp.sum(scaled * u, axis=-1, keepdims=True) * (1.0 / HEAD_DIM)
    return inv * scaled - u * (inv * inv * inv * inner), gain_grad


BWD_IN = ("n2", "cot_all", "wgu", "wd", "wo", "wq", "normed", "qkv", "q", "kv", "segs", "o", "att",
          "mid", "tok", "cot", "g_one", "g_two", "qg", "kg", "cos", "sin")
BWD_SMALL = ("mid", "tok", "cot", "g_one", "g_two", "qg", "kg", "cos", "sin")
BWD_OUT = ("mixed", "input_grad", "gu_g", "do_g", "qkv_g", "gains_g", "gu_slot",
           "do_slot")
SUM_B = tuple("input_grad" if n == "sum_out" else n + "_b" for n in SUM_NAMES)


def backward_kernel(names, *refs):
    m = dict(zip(names, refs))
    base, y, c, z, x = here()
    r = 2 * y + c
    to_c, to_x, to_y = neighbours()
    z_same = [device(base, y, c, (z + k) % 4, x) for k in range(1, 4)]
    mates = layer_mates()
    greet(mates + z_same)
    rows, width = m["tok"].shape
    span = 2 * rows
    keep = m["keep"]
    part = m["wd"].shape[0]
    main = (part // 128) * 128
    own_rows = m["wo"].shape[0]
    rest = part - main
    quarter_d, quarter_o = part // 4, own_rows // 4

    def order(k):
        return (y + 1 + k) % 2, (c + 1 + k // 2) % 2

    def load(k, src, dst):
        copy = pltpu.make_async_copy(src, dst, keep.at[k])
        copy.start()
        return copy

    n2, cot, wgu, wd = m["n2_v"], m["cot_v"], m["wgu_v"], m["wd_v"]
    first_loads = [
        load(0, m["wgu"], wgu), load(1, m["n2"], n2), load(2, m["cot_all"], cot),
        load(3, m["wd"].at[pl.ds(rest * x, main)], wd.at[pl.ds(0, main)]),
        load(4, m["wd"].at[pl.ds(main * (1 - x), rest)], wd.at[pl.ds(main, rest)]),
    ]
    later = [load(5 + i, m[n], m[n + "_v"]) for i, n in enumerate(
        ("wo", "wq", "qkv", "q", "kv", "segs", "o", "att"))]
    wd[pl.ds(main + rest, 128 - rest)] = jnp.zeros((128 - rest, width), BF16)
    for copy in first_loads:
        copy.wait()

    hidden, dgu, parts = m["hidden"], m["dgu"], m["part"]
    summed = SeqSum(parts, [m[n] for n in SUM_NAMES])

    def feed(k, carry):
        b, e = order(k)
        s = 2 * b + e
        at = pl.ds(s * span, span)
        gu = jnp.dot(n2[pl.ds(2 * s, 2)].reshape(span, width), wgu[...],
                     preferred_element_type=F32)
        dh = last_dims(cot[pl.ds(2 * s, 2)].reshape(span, width), wd[...])
        for lo, hi in ((0, main), (main, main + 128)):
            if lo == 0:
                gate, up = gu[:, :main], gu[:, main:2 * main]
            else:
                tile = gu[:, 2 * main:]
                gate, up = low_half(tile), low_half(roll(tile, 64))
            grad = dh[:, lo:hi]
            sigma = 1.0 / (1.0 + jnp.exp(-gate))
            active = gate * sigma
            hidden[at, lo:hi] = (active * up).astype(BF16)
            d_gate = grad * up * sigma * (1.0 + gate * (1.0 - sigma))
            d_up = grad * active
            if lo == 0:
                dgu[at, 0:main] = d_gate.astype(BF16)
                dgu[at, main:2 * main] = d_up.astype(BF16)
            else:
                dgu[at, 2 * main:] = (d_gate + roll(low_half(d_up), 64)).astype(BF16)
        out = last_dims(dgu[at], wgu[...]).astype(BF16)
        parts[pl.ds(2 * s, 2)] = out.reshape(2, rows, width)
        pl.when(k < 2)(lambda: summed.give(b))
        pl.when(k == 2)(summed.take_far)
        pl.when(k == 3)(summed.take_near)
        return carry

    lax.fori_loop(0, 4, feed, 0)

    ggu = m["ggu"]
    block_rows = 2 * own_rows
    gu_sum = ZSum(lambda zk: ggu.at[zk], lambda zk: m["gu_slot"].at[zk], m["zg_s"], m["zg_r"])

    def grad_gu(i, carry):
        zk = gu_sum.first(i)
        cols = pl.ds(pl.multiple_of(zk * block_rows, 128), block_rows)
        left = n2[:, :, cols].reshape(8 * rows, block_rows)
        ggu[zk] = first_dims(left, dgu[...]).astype(BF16)
        gu_sum.start(zk)
        return carry

    lax.fori_loop(0, 2, grad_gu, 0)
    summed.middle()
    lax.fori_loop(2, 4, grad_gu, 0)
    summed.finish()

    v = m["mid"][...]
    dv, gain_grad = norm_back(summed.out[...], v, inverse_rms(v), m["g_two"][...])
    m["row_two"][...] = gain_grad
    dmid = m["cot"][...].astype(F32) + dv
    m["dmid"][...] = dmid
    m["low"][...] = dmid.astype(BF16)
    branch = Gather(m["low"], m["db"], m["ga_s"], m["ga_r"], keep.at[13])
    branch.start()
    normed = n2
    copy_normed = load(1, m["normed"], normed)

    gdo, got = m["gdo"], m["got"]
    summed.sent()
    units = part // rest
    for j in range(0, main + 128, 128):
        grad = first_dims(hidden[:, j:j + 128], cot[...].reshape(8 * rows, width)).astype(BF16)
        for h in range(2):
            u = 2 * (j // 128) + h
            if u < units:
                to = (u + x) % units
                parts[to // 2, pl.ds(rest * (to % 2), rest)] = grad[rest * h:rest * (h + 1)]
    for i in range(4):
        lo = quarter_d * i
        first, last = lo // rows, (lo + quarter_d - 1) // rows + 1
        span_rows = parts[first:last].reshape((last - first) * rows, width)
        gdo[i, 0:quarter_d] = span_rows[lo - first * rows:lo - first * rows + quarter_d]
    branch.forward()

    mixed = SeqSum(parts, [m[n] for n in SUM_B])

    def down(k, carry):
        b, e = order(k)
        s = 2 * b + e
        out = jnp.dot(hidden[pl.ds(s * span, span)], wd[...], preferred_element_type=F32)
        parts[pl.ds(2 * s, 2)] = out.astype(BF16).reshape(2, rows, width)
        pl.when(k < 2)(lambda: mixed.give(b))
        pl.when(k == 2)(mixed.take_far)
        pl.when(k == 3)(mixed.take_near)
        return carry

    lax.fori_loop(0, 4, down, 0)
    branch.finish()

    def add_far(block, slot):
        copy = pltpu.make_async_copy(slot, dgu.at[pl.ds(0, block_rows)], keep.at[0])
        copy.start()
        copy.wait()
        block[...] = (block[...].astype(F32) + dgu[0:block_rows].astype(F32)).astype(BF16)

    gu_sum.merge(add_far)

    def hand(i, lo, n, ss, rs):
        return remote(gdo.at[i, pl.ds(lo, n)], got.at[r, pl.ds(lo, n)], ss.at[i], rs.at[r],
                      device(base, i // 2, i % 2, z, x))

    def hand_all(lo, n, ss, rs):
        for i in range(4):
            pl.when(r != i)(lambda i=i: hand(i, lo, n, ss, rs).start())
        got[r, lo:lo + n] = gdo[r, lo:lo + n]

    def handed(lo, n, ss, rs):
        for i in range(4):
            pl.when(r != i)(lambda i=i: remote(
                gdo.at[i, pl.ds(lo, n)], got.at[i, pl.ds(lo, n)], ss.at[i], rs.at[i],
                to_c).wait_recv())

    def hand_sent(lo, n, ss, rs):
        for i in range(4):
            pl.when(r != i)(lambda i=i: hand(i, lo, n, ss, rs).wait_send())

    hand_all(0, quarter_d, m["hd_s"], m["hd_r"])

    for copy in later:
        copy.wait()
    q_all, kv, segs, o_all, att = m["q_v"], m["kv_v"], m["segs_v"], m["o_v"], m["att_v"]
    wo, wq, qkv = m["wo_v"], m["wq_v"], m["qkv_v"]
    db, dkv, dqkv, acc, q_seg, do_v = m["db"], m["kv_v"], m["dqkv"], m["acc"], m["q_seg"], m["do"]
    own_kv = m["own_kv"]
    qg, kg, cos, sin = m["qg"][0:1], m["kg"][0:1], m["cos"][...], m["sin"][...]
    m["row_head"][...] = jnp.zeros((1, 128), F32)

    def kv_sum(s):
        return ZSum(lambda zk: dkv.at[zk, s], lambda zk: m["kv_slot"].at[zk, s],
                    m["zk_s"].at[s], m["zk_r"].at[s])

    def attend_one(k, carry):
        b, e = order(k)
        s = 2 * b + e
        grads = db[pl.ds(2 * s, 2)].reshape(span, width)
        d_att = last_dims(grads, wo[...])
        first = d_att[:, 0:128]
        third = jnp.concatenate([jnp.zeros((span, HEAD_DIM), F32), d_att[:, 128:192]], axis=1)
        d_out = jnp.concatenate([high_half(roll(first, 64)), high_half(first), third], axis=0)
        d_out = d_out.astype(BF16).astype(F32)
        o = o_all[s]
        d_out = (d_out * roll(o, 64)).astype(BF16)
        do_v[...] = d_out
        delta = jnp.sum(d_out.astype(F32) * high_half(o), axis=1, keepdims=True)
        q_seg[...] = segment_columns(segs, z, s)
        acc[...] = jnp.zeros_like(acc)

        def block(zk, diagonal):
            tile = kv[zk, s]
            q = q_all[s]
            d_out = do_v[...]
            p = exp_scores(q, tile, q_seg[...], segment_row(segs, zk, s), diagonal)
            ds = (p * (last_dims(d_out, tile) - delta)).astype(BF16)
            acc[...] += jnp.dot(ds, tile, preferred_element_type=F32)
            return first_dims(ds, q) + first_dims(p.astype(BF16), d_out)

        def step(zk, inner):
            dkv[zk, s] = block(zk, False).astype(BF16)
            pl.when((z == 3) & (zk == 0))(lambda: kv_sum(s).far(0, 2).start())
            pl.when(jnp.logical_not(((z == 3) | (z == 2)) & (zk == 0)))(
                lambda: kv_sum(s).direct(zk).start())
            return inner

        lax.fori_loop(0, z, step, 0)
        own_kv[s] = block(z, True)
        tiles = split_heads(qkv[s, :, 0:128], qkv[s, :, 128:256])
        back = []
        for j in range(GROUP):
            dy = rotated(low_half(acc[pl.ds(j * span, span)]) * HEAD_DIM ** (-0.5), cos, -sin)
            raw, gain_part = head_back(dy, tiles[j], qg)
            m["row_head"][...] += gain_part
            back.append(raw)
        dqkv[s, :, 0:128] = (back[0] + roll(back[1], 64)).astype(BF16)
        dqkv[s, :, 128:256] = back[2].astype(BF16)
        pl.when(k == 1)(mixed.middle)
        return carry

    lax.fori_loop(0, 4, attend_one, 0)

    for j in range(0, width, 512):
        cols = slice(j, j + 512)
        grad = first_dims(att[...].reshape(8 * rows, Q_COLS),
                          db[:, :, cols].reshape(8 * rows, 512)).astype(BF16)
        for i in range(4):
            gdo[i, quarter_d:quarter_d + quarter_o, cols] = grad[quarter_o * i:quarter_o * (i + 1)]
    hand_all(quarter_d, quarter_o, m["ho_s"], m["ho_r"])

    def kv_merge(k, carry):
        b, e = order(k)
        s = 2 * b + e

        @pl.when(z == 2)
        def _():
            one = kv_sum(s)
            one.far(0, 2).wait_recv()
            dkv[0, s] = (dkv[0, s].astype(F32) + m["kv_slot"][2, s].astype(F32)).astype(BF16)
            one.direct(0).start()
        return carry

    lax.fori_loop(0, 4, kv_merge, 0)
    mixed.finish()
    m["mixed"][...] = (m["mid"][...] + mixed.out[...]).astype(BF16)
    mixed.sent()

    handed(0, quarter_d, m["hd_s"], m["hd_r"])
    handed(quarter_d, quarter_o, m["ho_s"], m["ho_r"])
    do_sum = ZSum(lambda zk: got.at[zk], lambda zk: m["do_slot"].at[zk], m["zd_s"], m["zd_r"])

    def start_do(i, carry):
        do_sum.start(do_sum.first(i))
        return carry

    lax.fori_loop(0, 4, start_do, 0)

    inputs = SeqSum(parts, [m[n] for n in SUM_NAMES])

    def finish_one(k, carry):
        b, e = order(k)
        s = 2 * b + e
        for d in (1, 2):
            @pl.when(z + d < 4)
            def _():
                kv_sum(s).arrive(z + d)
                own_kv[s] += m["kv_slot"][z + d, s].astype(F32)
        total = own_kv[s]
        u = split_heads(qkv[s, :, 0:128], qkv[s, :, 128:256])[GROUP]
        dy = rotated(low_half(total), cos, -sin)
        raw, gain_part = head_back(dy, u, kg)
        m["row_head"][...] += roll(gain_part, 64)
        tile = dqkv[s, :, 128:256].astype(F32)
        dqkv[s, :, 128:256] = (low_half(tile) + roll(raw, 64)).astype(BF16)
        dqkv[s, :, 256:320] = roll(total, 64)[:, 0:HEAD_DIM].astype(BF16)
        out = last_dims(dqkv[s], wq[...]).astype(BF16)
        parts[pl.ds(2 * s, 2)] = out.reshape(2, rows, width)
        pl.when(k < 2)(lambda: inputs.give(b))
        pl.when(k == 2)(inputs.take_far)
        pl.when(k == 3)(inputs.take_near)
        return carry

    lax.fori_loop(0, 4, finish_one, 0)
    copy_normed.wait()
    gqkv = m["gqkv"]
    qkv_sum = ZSum(lambda zk: gqkv.at[zk], lambda zk: m["qkv_slot"].at[zk], m["zq_s"], m["zq_r"])

    def grad_qkv(i, carry):
        zk = qkv_sum.first(i)
        cols = pl.ds(pl.multiple_of(zk * block_rows, 128), block_rows)
        left = normed[:, :, cols].reshape(8 * rows, block_rows)
        gqkv[zk] = first_dims(left, dqkv[...].reshape(8 * rows, HEAD_COLS)).astype(BF16)
        qkv_sum.start(zk)
        return carry

    lax.fori_loop(0, 4, grad_qkv, 0)
    inputs.middle()

    def add_vmem(block, slot):
        block[...] = (block[...].astype(F32) + slot[...].astype(F32)).astype(BF16)

    hand_sent(0, quarter_d, m["hd_s"], m["hd_r"])
    hand_sent(quarter_d, quarter_o, m["ho_s"], m["ho_r"])

    def add_do(block, slot):
        copy = pltpu.make_async_copy(slot, gdo.at[0], keep.at[0])
        copy.start()
        copy.wait()
        block[...] = (block[...].astype(F32) + gdo[0].astype(F32)).astype(BF16)

    do_sum.merge(add_do)

    t_own = 2 * r + x
    gu_sum.sent()
    gu_sum.wait()

    def total_gu(slots):
        copies = []
        for i, slot in enumerate(slots):
            copy = pltpu.make_async_copy(slot, dgu.at[pl.ds(0, block_rows)], keep.at[0])
            copy.start()
            copy.wait()
            ggu[z] = (ggu[z].astype(F32) + dgu[0:block_rows].astype(F32)).astype(BF16)

    gu_sum.collect(total_gu)
    gu_out, qkv_out, do_out = m["gu_g"], m["qkv_g"], m["do_g"]

    def swap(src, out, ss, rs):
        return remote(src.at[z, pl.ds(own_rows * (1 - x), own_rows)], out.at[t_own], ss, rs, to_x)

    def keep_own(k, src, out):
        return pltpu.make_async_copy(src.at[z, pl.ds(own_rows * x, own_rows)], out.at[t_own],
                                     keep.at[k])

    def swapped(src, out, ss, rs):
        return remote(src.at[z, pl.ds(own_rows * x, own_rows)], out.at[2 * r + 1 - x], ss, rs,
                      to_x)

    gu_swap = swap(ggu, gu_out, m["xg_s"], m["xg_r"])
    gu_swap.start()
    gu_keep = keep_own(14, ggu, gu_out)
    gu_keep.start()
    gu_keep.wait()
    gu_share = RepShare(lambda i: gu_out.at[pl.ds(2 * i, 2)], m["rg_s"], m["rg_r"])

    inputs.finish()
    v = m["tok"][...].astype(F32)
    dv, gain_grad = norm_back(inputs.out[...], v, inverse_rms(v), m["g_one"][...])
    m["input_grad"][...] = m["dmid"][...] + dv

    rows_v = m["rows_v"]
    rows_v[0, 0:1] = gain_grad
    rows_v[0, 1:2] = m["row_two"][...]
    rows_v[0, 2:3, 0:128] = m["row_head"][...]

    def gain_copy(k):
        return remote(rows_v.at[0], rows_v.at[k], m["gn_s"].at[k - 1], m["gn_r"].at[k - 1],
                      mates[k - 1])

    for k in range(1, 8):
        gain_copy(k).start()

    swapped(ggu, gu_out, m["xg_s"], m["xg_r"]).wait_recv()
    gu_share.start()
    qkv_sum.merge(add_vmem)
    for k in range(1, 8):
        gain_copy(k).wait_recv()
    total = rows_v[0]
    for k in range(1, 8):
        total = total + rows_v[k]
    z_rows = m["z_rows"]
    z_rows[0] = total

    def gain_z(k):
        return remote(z_rows.at[0], z_rows.at[k], m["gz_s"].at[k - 1], m["gz_r"].at[k - 1],
                      z_same[k - 1])

    for k in range(1, 4):
        gain_z(k).start()

    do_sum.wait()

    def total_do(slots):
        copies = [pltpu.make_async_copy(slot, gdo.at[i], keep.at[i])
                  for i, slot in enumerate(slots)]
        for copy in copies:
            copy.start()
        for copy in copies:
            copy.wait()
        total = got[z].astype(F32)
        for i in range(len(slots)):
            total = total + gdo[i].astype(F32)
        m["do_own"][...] = total.astype(BF16)

    do_sum.collect(total_do)
    do_keep = pltpu.make_async_copy(m["do_own"], do_out.at[r], keep.at[15])
    do_keep.start()
    do_keep.wait()
    do_share = RepShare(lambda i: do_out.at[i], m["rd_s"], m["rd_r"])
    do_share.start()
    gu_share.forward()

    qkv_sum.wait()

    def total_qkv(slots):
        total = gqkv[z].astype(F32)
        for slot in slots:
            total = total + slot[...].astype(F32)
        m["qkv_own"][0] = total.astype(BF16)

    qkv_sum.collect(total_qkv)
    own = m["qkv_own"]
    qkv_swap = remote(own.at[0, pl.ds(own_rows * (1 - x), own_rows)], qkv_out.at[t_own],
                      m["xq_s"], m["xq_r"], to_x)
    qkv_swap.start()
    qkv_keep = pltpu.make_async_copy(own.at[0, pl.ds(own_rows * x, own_rows)],
                                     qkv_out.at[t_own], keep.at[16])
    qkv_keep.start()
    qkv_keep.wait()
    qkv_share = RepShare(lambda i: qkv_out.at[pl.ds(2 * i, 2)], m["rq_s"], m["rq_r"])
    remote(own.at[0, pl.ds(0, own_rows)], qkv_out.at[2 * r + 1 - x], m["xq_s"], m["xq_r"],
           to_x).wait_recv()
    qkv_share.start()
    do_share.forward()
    for k in range(1, 4):
        gain_z(k).wait_recv()
    m["gains_g"][...] = z_rows[0] + z_rows[1] + z_rows[2] + z_rows[3]
    qkv_share.forward()
    for share in (gu_share, do_share, qkv_share):
        share.finish()

    for share in (gu_share, do_share, qkv_share):
        share.sent()
    gu_swap.wait_send()
    qkv_swap.wait_send()
    for k in range(1, 8):
        gain_copy(k).wait_send()
    for k in range(1, 4):
        gain_z(k).wait_send()
    do_sum.sent()
    qkv_sum.sent()
    inputs.sent()

    def kv_sent(s, carry):
        for zk in range(3):
            pl.when(z > zk)(lambda zk=zk: kv_sum(s).direct(zk).wait_send())
        return carry

    lax.fori_loop(0, 4, kv_sent, 0)


def backward_call(f, tok, cot, qg, kg, cos, sin):
    shape = jax.ShapeDtypeStruct
    rows, width = tok.shape
    span = 2 * rows
    own_rows, part = f["wo_all"].shape[0], f["wd_all"].shape[0]
    cols = f["wgu_all"].shape[1]
    quarter = (part + own_rows) // 4
    args = {"n2": f["n2_all"], "cot_all": f["cot_all"], "wgu": f["wgu_all"], "wd": f["wd_all"],
            "wo": f["wo_all"], "wq": f["wq_all"], "tok": tok, "cot": cot, "qg": qg, "kg": kg,
            "cos": cos, "sin": sin}
    for n in ("normed", "qkv", "q", "kv", "segs", "o", "att", "mid", "g_one", "g_two"):
        args[n] = f[n]
    outs = {
        "mixed": shape((rows, width), BF16),
        "input_grad": shape((rows, width), F32),
        "gu_g": shape((8, own_rows, cols), BF16),
        "do_g": shape((4, quarter, width), BF16),
        "qkv_g": shape((8, own_rows, HEAD_COLS), BF16),
        "gains_g": shape((8, width), F32),
        "gu_slot": shape((4, 2 * own_rows, cols), BF16),
        "do_slot": shape((4, quarter, width), BF16),
    }
    same = lambda n, dtype=None: pltpu.VMEM(args[n].shape, dtype or args[n].dtype)
    buffers = {
        "n2_v": same("n2"), "cot_v": same("cot_all"), "wgu_v": same("wgu"),
        "wd_v": pltpu.VMEM(((part // 128 + 1) * 128, width), BF16),
        "wo_v": same("wo"), "wq_v": same("wq"), "qkv_v": same("qkv"), "q_v": same("q"),
        "kv_v": same("kv"), "segs_v": same("segs"), "o_v": same("o"), "att_v": same("att"),
        "hidden": pltpu.VMEM((8 * rows, (part // 128 + 1) * 128), BF16),
        "dgu": pltpu.VMEM((8 * rows, cols), BF16),
        "part": pltpu.VMEM((8, rows, width), BF16),
        "ggu": pltpu.VMEM((4, 2 * own_rows, cols), BF16),
        "gdo": pltpu.VMEM((4, quarter, width), BF16),
        "got": pltpu.VMEM((4, quarter, width), BF16),
        "do_own": pltpu.VMEM((quarter, width), BF16),
        "db": pltpu.VMEM((8, rows, width), BF16),
        "dmid": pltpu.VMEM((rows, width), F32),
        "low": pltpu.VMEM((rows, width), BF16),
        "kv_slot": same("kv"),
        "own_kv": pltpu.VMEM((4, span, 128), F32),
        "dqkv": pltpu.VMEM((4, span, HEAD_COLS), BF16),
        "acc": pltpu.VMEM((GROUP * span, 128), F32),
        "do": pltpu.VMEM((GROUP * span, 128), BF16),
        "q_seg": pltpu.VMEM((span, span), jnp.int32),
        "gqkv": pltpu.VMEM((4, 2 * own_rows, HEAD_COLS), BF16),
        "qkv_slot": pltpu.VMEM((4, 2 * own_rows, HEAD_COLS), BF16),
        "qkv_own": pltpu.VMEM((1, 2 * own_rows, HEAD_COLS), BF16),
        "row_two": pltpu.VMEM((1, width), F32),
        "row_head": pltpu.VMEM((1, 128), F32),
        "rows_v": pltpu.VMEM((8, 8, width), F32),
        "z_rows": pltpu.VMEM((4, 8, width), F32),
    }
    buffers.update(zip(SUM_NAMES, seq_scratch(width)))
    buffers.update((n, b) for n, b in zip(SUM_B, seq_scratch(width)) if n != "input_grad")
    two = pltpu.SemaphoreType.DMA
    sems = {
        "ga_s": dma(8), "ga_r": dma(8), "zg_s": dma(4), "zg_r": dma(5), "zd_s": dma(4),
        "zd_r": dma(5), "zq_s": dma(4), "zq_r": dma(5), "zk_s": two((4, 4)), "zk_r": two((4, 5)),
        "hd_s": dma(4), "hd_r": dma(4), "ho_s": dma(4), "ho_r": dma(4), "xg_s": two, "xg_r": two,
        "xq_s": two, "xq_r": two, "rg_s": dma(3), "rg_r": dma(3), "rd_s": dma(3), "rd_r": dma(3),
        "rq_s": dma(3), "rq_r": dma(3), "gn_s": dma(7), "gn_r": dma(7), "gz_s": dma(3),
        "gz_r": dma(3), "keep": dma(17),
    }
    names = BWD_IN + BWD_OUT + tuple(buffers) + tuple(sems)
    outs_list = pl.pallas_call(
        functools.partial(backward_kernel, names),
        name="backward",
        out_shape=tuple(outs[n] for n in BWD_OUT),
        in_specs=[VMEM if n in BWD_SMALL else ANY for n in BWD_IN],
        out_specs=tuple(VMEM if n in ("mixed", "input_grad", "gains_g") else ANY
                        for n in BWD_OUT),
        scratch_shapes=list(buffers.values()) + list(sems.values()),
        compiler_params=params(1, 63),
    )(*[args[n] for n in BWD_IN])
    return dict(zip(BWD_OUT, outs_list))


def order_kernel(gu, do, qkv, gu_o, down_o, out_o, qkv_o):
    which = pl.program_id(1)
    cols = gu.shape[2]
    main = cols // 2 // 128 * 128
    piece = cols
    quarter_d = down_o.shape[0]
    low = lanes((gu.shape[1], 128)) < HEAD_DIM
    first, second = gu[0, :, 2 * main:].astype(F32), gu[1, :, 2 * main:].astype(F32)

    @pl.when(which == 0)
    def _():
        gu_o[:, 0:main] = gu[0, :, 0:main].astype(F32)
        gu_o[:, main:main + 128] = jnp.where(low, first, roll(second, 64))
        gu_o[:, main + 128:] = gu[1, :, 0:main].astype(F32)
        down_o[...] = do[0, 0:quarter_d].astype(F32)

    @pl.when(which == 1)
    def _():
        gu_o[:, 0:main] = gu[0, :, main:2 * main].astype(F32)
        gu_o[:, main:main + 128] = jnp.where(low, roll(first, 64), second)
        gu_o[:, main + 128:] = gu[1, :, main:2 * main].astype(F32)
        out_o[...] = do[0, quarter_d:].astype(F32)

    @pl.when(which == 0)
    def _():
        i = pl.program_id(0)
        a, b = qkv[0].astype(F32), qkv[1].astype(F32)
        at = lambda start, n: pl.ds(pl.multiple_of(start, 128), n)
        q_cols, kv_cols = HEADS * HEAD_DIM, KV_HEADS * HEAD_DIM
        half = lambda v, w: jnp.where(low, v, w)
        a1, a2, b0, b1 = a[:, 128:256], a[:, 256:], b[:, 0:128], b[:, 128:256]
        qkv_o[:, at(i * 2 * Q_COLS, 128)] = a[:, 0:128]
        qkv_o[:, at(i * 2 * Q_COLS + 128, 128)] = half(a1, roll(b0, 64))
        qkv_o[:, at(i * 2 * Q_COLS + 256, 128)] = half(roll(b0, 64), roll(b1, 64))
        qkv_o[:, at(q_cols + i * 128, 128)] = half(roll(a1, 64), b1)
        qkv_o[:, at(q_cols + kv_cols + i * 128, 128)] = jnp.concatenate([a2, b[:, 256:]], axis=1)


def order_call(gu, do, qkv, part):
    shape = jax.ShapeDtypeStruct
    _, own_rows, cols = gu.shape
    width = do.shape[2]
    quarter_d = part // 4
    quarter_o = do.shape[1] - quarter_d
    return pl.pallas_call(
        order_kernel,
        name="final_order",
        grid=(4, 2),
        out_shape=(
            shape((own_rows, 8 * cols), F32), shape((part, width), F32),
            shape((4 * quarter_o, width), F32),
            shape((own_rows, (HEADS + 2 * KV_HEADS) * HEAD_DIM), F32)),
        in_specs=[
            pl.BlockSpec((2, own_rows, cols), lambda i, w: (i, 0, 0)),
            pl.BlockSpec((1, do.shape[1], width), lambda i, w: (i, 0, 0)),
            pl.BlockSpec((2, own_rows, qkv.shape[2]), lambda i, w: (i, 0, 0))],
        out_specs=(
            pl.BlockSpec((own_rows, cols), lambda i, w: (0, 4 * w + i)),
            pl.BlockSpec((quarter_d, width), lambda i, w: (i, 0)),
            pl.BlockSpec((quarter_o, width), lambda i, w: (i, 0)),
            pl.BlockSpec((own_rows, (HEADS + 2 * KV_HEADS) * HEAD_DIM), lambda i, w: (0, 0))),
        compiler_params=pltpu.CompilerParams(
            dimension_semantics=("arbitrary", "arbitrary"), vmem_limit_bytes=48 * 2**20),
    )(gu, do, qkv)


def rope_tables(positions):
    half = HEAD_DIM // 2
    freq = jnp.exp(-jnp.log(THETA) * jnp.arange(half, dtype=F32) * 2.0 / HEAD_DIM)
    angle = positions.astype(F32)[:, None] * freq[None, :]
    cos, sin = jnp.cos(angle), jnp.sin(angle)
    zero = jnp.zeros_like(cos)
    return jnp.concatenate([cos, cos, zero, zero], 1), jnp.concatenate([-sin, sin, zero, zero], 1)


def over_quads(array):
    reps = lax.axis_size("rep")
    if reps == 4:
        return array
    rows = [[j + 4 * q for q in range(reps // 4)] for j in range(4)]
    return lax.psum(array, "rep", axis_index_groups=rows)


def local(tokens, attn_gain, w_qkv, q_gain, k_gain, w_out, ffn_gain, w_gate_up, w_down,
          cotangent, segment_ids):
    rows, width = tokens.shape
    _, y, c, z, x = here()
    r = 2 * y + c
    q_width, kv_width = HEADS * HEAD_DIM, KV_HEADS * HEAD_DIM
    own_rows = w_qkv.shape[0]
    span = 2 * rows
    cut = lax.dynamic_slice_in_dim

    q_pair = cut(w_qkv, 2 * Q_COLS * r, 2 * Q_COLS, 1)
    k_pair = cut(w_qkv, q_width + 2 * HEAD_DIM * r, 2 * HEAD_DIM, 1)
    v_pair = cut(w_qkv, q_width + kv_width + 2 * HEAD_DIM * r, 2 * HEAD_DIM, 1)
    wq = jnp.stack([
        jnp.concatenate([
            q_pair[:, i * Q_COLS:(i + 1) * Q_COLS],
            k_pair[:, i * HEAD_DIM:(i + 1) * HEAD_DIM],
            v_pair[:, i * HEAD_DIM:(i + 1) * HEAD_DIM]], 1)
        for i in range(2)])
    gains = jnp.zeros((16, 256), BF16)
    gains = gains.at[0, :own_rows].set(attn_gain).at[1, :own_rows].set(ffn_gain)
    seg = jnp.broadcast_to(segment_ids[None, :], (8, rows))
    cos, sin = rope_tables(span * z + jnp.arange(span, dtype=jnp.int32))

    def padded(gain):
        return jnp.zeros((8, 128), F32).at[:, :HEAD_DIM].set(gain.astype(F32)[None])

    qg, kg = padded(q_gain), padded(k_gain)
    f = forward_call(tokens, cotangent, seg, wq, gains, w_gate_up, w_down, w_out, qg, kg, cos, sin)
    g = backward_call(f, tokens, cotangent, qg, kg, cos, sin)
    gu, down, out, qkv = order_call(
        over_quads(g["gu_g"]), over_quads(g["do_g"]), over_quads(g["qkv_g"]), w_down.shape[0])
    gains_sum = over_quads(g["gains_g"])
    place = 2 * z + x
    gain_one = cut(gains_sum[0], place * own_rows, own_rows, 0)
    gain_two = cut(gains_sum[1], place * own_rows, own_rows, 0)
    return (g["mixed"], g["input_grad"], gain_one, qkv, gains_sum[2, :HEAD_DIM],
            gains_sum[2, HEAD_DIM:2 * HEAD_DIM], out, gain_two, gu, down)


def solution(mesh):
    rows, split = P(("rep", "grp"), None), P("grp", None)
    return jax.shard_map(
        local,
        mesh=mesh,
        in_specs=(rows, P("grp"), split, P(), P(), split, P("grp"), split, split, rows,
                  P(("rep", "grp"))),
        out_specs=(rows, rows, P("grp"), split, P(), P(), split, P("grp"), split, split),
        check_vma=False,
    )
```

time: 2540 us -> 391 us (0.15)
  waiting for transfers between devices: 2110 us -> 0 us
  Pallas kernels: 0 us -> 370 us
  matrix products: 206 us -> 0 us
  blocking collectives: 82.8 us -> 0 us
  local copies, waits for them, and re-layouts: 75.1 us -> 14.2 us
  other arithmetic: 38.7 us -> 4.25 us
    reduce_scatter x5 -> x0, waiting for transfers between devices: 1120 us -> none  [the longest x1 452 us: local(): lax.psum_scatter(dot_first(normed_two, grad_gu).astype(jnp.bfloat16), 'gr...]
    all_gather x6 -> x0, waiting for transfers between devices: 903 us -> none  [the longest x1 536 us: local(): lax.all_gather(w_gate_up, 'grp', axis=0, tiled=True)]
    pallas_call x0 -> x3, Pallas kernels: none -> 370 us  [the longest x1 212 us: backward_call(): pl.pallas_call(functools.partial(backward_kernel, names), name='backward'...]
    dot_general x68 -> x0, matrix products: 206 us -> none  [the longest x28 75.4 us: dot_last(): lax.dot_general(left, right, (((1,), (1,)), ((), ())), preferred_element_...]
    unnamed x2 -> x0, blocking collectives: 59.1 us -> none
    psum x1 -> x0, waiting for transfers between devices: 53.6 us -> none  [local(): lax.psum(qkv_owned.astype(jnp.bfloat16), 'rep').astype(jnp.float32)]
    unnamed x14 -> x0, waiting for transfers between devices: 31.8 us -> none
  transfers between devices with their start and end apart: 13 -> 0, of which waited for: 13 -> 0; matrix products, arithmetic and copies ran while one was open for 7% -> 0% of each run, Pallas kernels for 0% -> 0%
where the time goes in v2:
time: 391 us; the launch traced here: 389 us
  Pallas kernels  370 us (95%)
  local copies, waits for them, and re-layouts  14.2 us (4%)
  other arithmetic  4.25 us (1%)
    pallas_call x1, Pallas kernels, backward_call(): pl.pallas_call(functools.partial(backward_kernel, names), name='backward'...  212 us
    pallas_call x1, Pallas kernels, forward_call(): pl.pallas_call(functools.partial(forward_kernel, names), name='forward',...  147 us
    pallas_call x1, Pallas kernels, order_call(): pl.pallas_call(order_kernel, name='final_order', grid=(4, 2), out_shape=(...  10.2 us

profile of v2, /device:TPU:0, one launch (start us, length us, event | category | flops | bytes accessed | tf_op | source)
XLA Modules:
  0.0 389.0 jit_solution(12066551617559054706)
XLA Ops:
  0.6 0.6 compare_reduce_fusion
  1.3 0.1 pad.19.clone
  1.4 1.3 broadcast_select_fusion
  2.7 0.7 reshape.138
  3.4 0.7 reshape.139
  4.0 0.6 scatter.27.refs_8_.refs_18_
  4.6 0.6 scatter.29.refs_9_.refs_19_
  5.2 1.2 broadcast_in_dim.2.refs_2_
  6.5 0.2 scatter.25.refs_4_
  6.6 0.0 copy-start.4
  6.7 1.0 constant_dynamic-slice_fusion.1
  7.7 1.1 constant_dynamic-slice_fusion.2
  8.8 0.1 maximum_bitcast_fusion
  8.9 0.8 pad_maximum_fusion.refs_3_
  9.7 0.5 fusion
  10.2 0.8 maximum_maximum_fusion.1
  11.1 0.0 copy-done.4
  11.1 147.5 %forward.1 = (bf16[8,128,1536]{2,1,0:T(8,128)(2,1)}, bf16[8,128,1536]{2,1,0:T(8,128)(2,1)}, bf16[8,128,1536]{2,1,0:T(8,128)(2,1)}, bf16[1536,320]{1,0:T(8,128)(2...) custom-call(bf16[128,1536]{1,0:T(8,128)(2,1)} %refs_14_.1, ...), custom_call_target="tpu_custom_call" | custom-call | tf_op jit(solution)/shard_map/forward/pallas_call | solution.py:761
  158.6 212.1 %backward.1 = (bf16[128,1536]{1,0:T(8,128)(2,1)}, f32[128,1536]{1,0:T(8,128)}, bf16[8,192,1152]{2,1,0:T(8,128)(2,1)}, bf16[4,192,1536]{2,1,0:T(8,128)(2,1)}, bf1...) custom-call(bf16[8,128,1536]{2,1,0:T(8,128)(2,1)} %get-tuple-element, ...), custom_call_target="tpu_custom_call" | custom-call | tf_op jit(solution)/shard_map/backward/pallas_call | solution.py:1416
  370.7 1.3 slice_bitcast_fusion
  372.0 0.9 fusion.1
  372.9 0.6 constant_dynamic-slice_fusion.3
  373.6 0.6 constant_dynamic-slice_fusion.4
  374.2 0.0 copy-start
  374.2 1.7 copy-done
  375.9 0.0 copy-start.1
  375.9 1.3 copy-done.1
  377.1 10.2 %final_order.1 = (f32[192,9216]{1,0:T(8,128)}, f32[576,1536]{1,0:T(8,128)}, f32[192,1536]{1,0:T(8,128)}, f32[192,2560]{1,0:T(8,128)}) custom-call(bf16[8,192,1152]{2,1,0:T(8,128)(2,1)} %get-tuple-element.103.gu, bf16[4,192,1536]{2,1,0:T(8,128)(2,1)S(1)} %copy-done, bf16[8,192,320]{2,1,0:T(8,128)(2,1)S(1)} %copy-done.1), custom_call_target="tpu_custom_call" | custom-call | tf_op jit(solution)/shard_map/final_order/pallas_call | solution.py:1473
  387.3 0.0 copy-done.3
  387.3 0.7 copy.25
  388.1 0.0 copy-done.2
  388.1 0.9 copy.26
  (8 shorter events, 0.0 us)
Async XLA Ops:
  6.6 4.4 %copy-start.4 = (bf16[16,256]{1,0:T(8,128)(2,1)}, bf16[16,256]{1,0:T(8,128)(2,1)S(1)}, u32[]{:S(2)}) copy-start(bf16[16,256]{1,0:T(8,128)(2,1)S(1)} %scatter.25.refs_4_) | copy-start | bytes 24580
  374.2 1.7 copy-start
  375.9 1.3 copy-start.1
  377.1 10.2 %copy-start.3 = (bf16[128,1536]{1,0:T(8,128)(2,1)S(1)}, bf16[128,1536]{1,0:T(8,128)(2,1)}, u32[]{:S(2)}) copy-start(bf16[128,1536]{1,0:T(8,128)(2,1)} %get-tuple-element.139) | copy-start | bytes 1179652
  377.1 11.0 %copy-start.2 = (f32[128,1536]{1,0:T(8,128)S(1)}, f32[128,1536]{1,0:T(8,128)}, u32[]{:S(2)}) copy-start(f32[128,1536]{1,0:T(8,128)} %get-tuple-element.140) | copy-start | bytes 2359300

commit v3 on v2

--- a/solution.py
+++ b/solution.py
@@ -153,12 +153,9 @@
 
 
 class Along:
-    def __init__(self, src, slot, send, recv, flip=False, mate=None):
+    def __init__(self, src, slot, send, recv):
         self.src, self.slot, self.send, self.recv = src, slot, send, recv
         self.base, self.y, self.c, self.z, self.x = here()
-        self.to = (1 - self.x) if flip else self.x
-        self.got = mate if flip else slot
-        self.flip = flip
 
     def at(self, zk, x):
         return device(self.base, self.y, self.c, zk, x)
@@ -166,23 +163,27 @@
     def copy(self, d):
         zk = (self.z + d + 4) % 4
         return remote(self.src, self.slot(self.z), self.send.at[d + 2], self.recv.at[self.z],
-                      self.at(zk, self.to))
+                      self.at(zk, self.x))
 
     def fits(self, d):
         return (self.z + d >= 0) & (self.z + d < 4)
 
-    def start(self):
-        if self.flip:
-            self.copy(0).start()
-        for d in (2, -2, 1, -1):
+    def first(self):
+        for d in (2, -2):
             pl.when(self.fits(d))(lambda d=d: self.copy(d).start())
+        pl.when(self.z == 2)(lambda: self.copy(1).start())
+        pl.when(self.z == 1)(lambda: self.copy(-1).start())
+
+    def second(self):
+        pl.when(self.z < 2)(lambda: self.copy(1).start())
+        pl.when(self.z >= 2)(lambda: self.copy(-1).start())
 
     def arrival(self, zk):
-        ref = self.got(zk)
+        ref = self.slot(zk)
         return remote(ref, ref, self.send.at[0], self.recv.at[zk], self.at(self.z, 1 - self.x))
 
     def passed(self, zk, to):
-        ref = self.got(zk)
+        ref = self.slot(zk)
         return remote(ref, ref, self.send.at[5], self.recv.at[zk], self.at(to, self.x))
 
     def forward(self):
@@ -198,9 +199,7 @@
 
     def wait(self, zk):
         early = ((self.z == 2) & (zk == 0)) | ((self.z == 1) & (zk == 3))
-        due = jnp.logical_not(early)
-        if not self.flip:
-            due = due & (self.z != zk)
+        due = jnp.logical_not(early) & (self.z != zk)
         pl.when(due)(lambda: self.arrival(zk).wait_recv())
 
     def finish(self):
@@ -208,8 +207,6 @@
             self.wait(zk)
 
     def sent(self):
-        if self.flip:
-            self.copy(0).wait_send()
         for d in (2, -2, 1, -1):
             pl.when(self.fits(d))(lambda d=d: self.copy(d).wait_send())
         pl.when(self.z == 2)(lambda: self.passed(0, 3).wait_send())
@@ -400,7 +397,6 @@
 
     tok = Gather(m["tok"], m["tok_all"], m["ga_s"], m["ga_r"], keep.at[0])
     cot = Gather(m["cot"], m["cot_all"], m["gb_s"], m["gb_r"], keep.at[1])
-    tok.start()
     segs = m["segs_v"]
     mates = layer_mates()
 
@@ -415,20 +411,21 @@
         return remote(m["gains"], m["gains_all"].at[own], m["gn_s"].at[k - 1],
                       m["gn_r"].at[k - 1], gain_target(k))
 
+    wq = m["wq_v"]
+
+    def wq_slot(zk, a):
+        return wq.at[pl.ds((2 * zk + a) * own_rows, own_rows)]
+
+    near = Along(m["wq"].at[x], lambda zk: wq_slot(zk, x), m["wa_s"], m["wa_r"])
+    flip = Along(wq_slot(z, 1 - x), lambda zk: wq_slot(zk, 1 - x), m["wb_s"], m["wb_r"])
+    over = remote(m["wq"].at[1 - x], wq_slot(z, x), m["wx_s"], m["wx_r"], to_x)
+    over_in = remote(m["wq"].at[x], wq_slot(z, 1 - x), m["wx_s"], m["wx_r"], to_x)
     for k in range(1, 8):
         seg_copy(k).start()
-    wq = m["wq_v"]
-
-    def wq_slot(zk, a):
-        return wq.at[pl.ds((2 * zk + a) * own_rows, own_rows)]
-
-    near = Along(m["wq"].at[x], lambda zk: wq_slot(zk, x), m["wa_s"], m["wa_r"])
-    flip = Along(m["wq"].at[1 - x], lambda zk: wq_slot(zk, x), m["wb_s"], m["wb_r"],
-                 flip=True, mate=lambda zk: wq_slot(zk, 1 - x))
-    near.start()
-    flip.start()
-    for k in range(1, 8):
-        gain_copy(k).start()
+    over.start()
+    near.first()
+    near.second()
+    tok.start()
     local = [
         local_copy(2, m["wq"].at[x], wq_slot(z, x)),
         local_copy(3, m["gains"], m["gains_all"].at[own]),
@@ -438,17 +435,33 @@
     ]
     for copy in local:
         copy.start()
+    for k in range(1, 8):
+        gain_copy(k).start()
     out_q = Along(m["wo"].at[pl.ds(quarter_o * r, quarter_o)], lambda zk: m["zo"].at[zk],
                   m["wo_s"], m["wo_r"])
     down_q = Along(m["wd"].at[pl.ds(quarter_d * r, quarter_d)], lambda zk: m["zd"].at[zk],
                    m["wd_s"], m["wd_r"])
-    out_q.start()
     quarters = [
         local_copy(7, m["wo"].at[pl.ds(quarter_o * r, quarter_o)], m["zo"].at[z]),
         local_copy(8, m["wd"].at[pl.ds(quarter_d * r, quarter_d)], m["zd"].at[z]),
     ]
     for copy in quarters:
         copy.start()
+    over_in.wait_recv()
+    flip.first()
+    flip.second()
+    out_q.first()
+    out_q.second()
+
+    def seg_up(k):
+        return remote(segs.at[z], segs.at[z], m["su_s"].at[k - 1], m["su_r"].at[z],
+                      device(base, y, c, (z + k) % 4, x))
+
+    for k in range(1, 8):
+        seg_copy(k).wait_recv()
+    local[2].wait()
+    for k in range(3, 0, -1):
+        pl.when(z + k < 4)(lambda k=k: seg_up(k).start())
 
     local[3].wait()
     local[4].wait()
@@ -474,25 +487,22 @@
 
     cross = remote(pair.at[1 - x], gu_rows(z, x), m["xc_s"], m["xc_r"], to_x)
     cross_in = remote(pair.at[x], gu_rows(z, 1 - x), m["xc_s"], m["xc_r"], to_x)
+    tok.forward()
     cross.start()
     mine = local_copy(5, pair.at[x], gu_rows(z, x))
     mine.start()
-
-    tok.forward()
     near.forward()
     flip.forward()
+    out_q.forward()
     tok.finish()
     cot.start()
     near.finish()
     flip.finish()
-    down_q.start()
-    out_q.forward()
     for k in range(1, 8):
         at = 2 * ((z + 4 - k // 2) % 4) + (x + k) % 2
         remote(m["gains"], m["gains_all"].at[at], m["gn_s"].at[k - 1], m["gn_r"].at[k - 1],
                to_c).wait_recv()
-        seg_copy(k).wait_recv()
-    for k in (0, 1, 2):
+    for k in (0, 1):
         local[k].wait()
     gather_gains = pltpu.make_async_copy(m["gains_all"], m["gains_v"], keep.at[3])
     gather_gains.start()
@@ -514,19 +524,8 @@
         return remote(kv.at[z, s], kv.at[z, s], m["kv_s"].at[d - 1, s], m["kv_r"].at[z, s],
                       device(base, y, c, (z + d) % 4, x))
 
-    def kv_pass(s):
-        return remote(kv.at[0, s], kv.at[0, s], m["kv_s"].at[2, s], m["kv_r"].at[0, s],
-                      device(base, y, c, 3, x))
-
     def kv_arrival(zk, s):
         return remote(kv.at[zk, s], kv.at[zk, s], m["kv_s"].at[0, s], m["kv_r"].at[zk, s], to_x)
-
-    def seg_up(k):
-        return remote(segs.at[z], segs.at[z], m["su_s"].at[k - 1], m["su_r"].at[z],
-                      device(base, y, c, (z + k) % 4, x))
-
-    for k in range(1, 4):
-        pl.when(z + k < 4)(lambda k=k: seg_up(k).start())
 
     def project(k, carry):
         b, e = order(k)
@@ -545,7 +544,7 @@
         u = rotated(u * head_inverse(u) * kg[0:1], cos, sin)
         v = jnp.concatenate([jnp.zeros((span, HEAD_DIM), F32), qkv[:, 256:320]], axis=1)
         kv[z, s] = (u + v).astype(BF16)
-        for d in (2, 1):
+        for d in (3, 2, 1):
             pl.when(z + d < 4)(lambda d=d: kv_copy(d, s).start())
         return carry
 
@@ -558,7 +557,10 @@
     mine.wait()
     cross_in.wait_recv()
     gu = Along(gu_unit(z), gu_unit, m["wg_s"], m["wg_r"])
-    gu.start()
+    down_q.first()
+    gu.first()
+    down_q.second()
+    gu.second()
     cot.forward()
 
     def hand(k, zk, src, dst, sems, n):
@@ -619,15 +621,9 @@
 
         block(z, True)
 
-        @pl.when(z == 2)
-        def _():
-            kv_arrival(0, s).wait_recv()
-            kv_pass(s).start()
-
         def step(i, inner):
             zk = z - 1 - i
-            pl.when(jnp.logical_not((z == 2) & (zk == 0)))(
-                lambda: kv_arrival(zk, s).wait_recv())
+            kv_arrival(zk, s).wait_recv()
             block(zk, False)
             return inner
 
@@ -655,21 +651,21 @@
             local_copy(18, segs, m["segs"]), local_copy(19, m["wo_v"], m["wo_all"])]
     for copy in more:
         copy.start()
+    summed.middle()
     down_q.forward()
-    summed.middle()
-    gu.forward()
     summed.finish()
     mid = m["tok"][...].astype(F32) + summed.out[...]
     m["mid"][...] = mid
     m["low"][...] = (mid * inverse_rms(mid) * m["g_two"][...]).astype(BF16)
     n2 = Gather(m["low"], m["n2_all"], m["gc_s"], m["gc_r"], keep.at[20])
     n2.start()
+    cot.finish()
+    n2.forward()
+    gu.forward()
     quarters[1].wait()
     down_q.finish()
     for zk in range(4):
         hand(13, zk, m["zd"], m["wd_all"], down_sems, quarter_d)
-    cot.finish()
-    n2.forward()
     n2.finish()
     handed(m["zd"], m["wd_all"], down_sems, quarter_d)
     gu.finish()
@@ -678,6 +674,7 @@
         along.sent()
     summed.sent()
     cross.wait_send()
+    over.wait_send()
     for k in range(1, 8):
         seg_copy(k).wait_send()
         gain_copy(k).wait_send()
@@ -685,9 +682,8 @@
         pl.when(z + k < 4)(lambda k=k: seg_up(k).wait_send())
 
     def kv_sent(s, carry):
-        for d in (1, 2):
+        for d in (1, 2, 3):
             pl.when(z + d < 4)(lambda d=d: kv_copy(d, s).wait_send())
-        pl.when(z == 2)(lambda: kv_pass(s).wait_send())
         return carry
 
     lax.fori_loop(0, 4, kv_sent, 0)
@@ -730,6 +726,7 @@
         "gc_r": dma(8), "sg_s": dma(7), "sg_r": dma(7), "gn_s": dma(7), "gn_r": dma(7),
         "wa_s": dma(6), "wa_r": dma(4), "wb_s": dma(6), "wb_r": dma(4), "wo_s": dma(6),
         "wo_r": dma(4), "wd_s": dma(6), "wd_r": dma(4), "wg_s": dma(6), "wg_r": dma(4),
+        "wx_s": pltpu.SemaphoreType.DMA, "wx_r": pltpu.SemaphoreType.DMA,
         "xc_s": pltpu.SemaphoreType.DMA, "xc_r": pltpu.SemaphoreType.DMA,
         "kv_s": pltpu.SemaphoreType.DMA((3, 4)), "kv_r": pltpu.SemaphoreType.DMA((4, 4)),
         "su_s": dma(3), "su_r": dma(4), "ho_s": dma(4), "ho_r": dma(4), "hd_s": dma(4),

time: 391 us -> 360 us (0.921)
  Pallas kernels: 370 us -> 340 us
    pallas_call x1, Pallas kernels: 147 us -> 132 us  [forward_call(): pl.pallas_call(functools.partial(forward_kernel, names), name='forward',...]
    pallas_call x1, Pallas kernels: 212 us -> 197 us  [backward_call(): pl.pallas_call(functools.partial(backward_kernel, names), name='backward'...]
where the time goes in v3:
time: 360 us; the launch traced here: 359 us
  Pallas kernels  340 us (94%)
  local copies, waits for them, and re-layouts  14.2 us (4%)
  other arithmetic  4.25 us (1%)
    pallas_call x1, Pallas kernels, backward_call(): pl.pallas_call(functools.partial(backward_kernel, names), name='backward'...  197 us
    pallas_call x1, Pallas kernels, forward_call(): pl.pallas_call(functools.partial(forward_kernel, names), name='forward',...  132 us
    pallas_call x1, Pallas kernels, order_call(): pl.pallas_call(order_kernel, name='final_order', grid=(4, 2), out_shape=(...  10.2 us

profile of v3, /device:TPU:0, one launch (start us, length us, event | category | flops | bytes accessed | tf_op | source)
XLA Modules:
  0.0 359.0 jit_solution(1203288978483918496)
XLA Ops:
  0.6 0.6 compare_reduce_fusion
  1.3 0.1 pad.19.clone
  1.4 1.3 broadcast_select_fusion
  2.7 0.7 reshape.138
  3.4 0.7 reshape.139
  4.0 0.6 scatter.27.refs_8_.refs_18_
  4.6 0.6 scatter.29.refs_9_.refs_19_
  5.2 1.2 broadcast_in_dim.2.refs_2_
  6.5 0.2 scatter.25.refs_4_
  6.6 0.0 copy-start.4
  6.7 1.0 constant_dynamic-slice_fusion.1
  7.7 1.1 constant_dynamic-slice_fusion.2
  8.8 0.1 maximum_bitcast_fusion
  8.9 0.8 pad_maximum_fusion.refs_3_
  9.7 0.5 fusion
  10.2 0.8 maximum_maximum_fusion.1
  11.1 0.0 copy-done.4
  11.1 132.1 %forward.1 = (bf16[8,128,1536]{2,1,0:T(8,128)(2,1)}, bf16[8,128,1536]{2,1,0:T(8,128)(2,1)}, bf16[8,128,1536]{2,1,0:T(8,128)(2,1)}, bf16[1536,320]{1,0:T(8,128)(2...) custom-call(bf16[128,1536]{1,0:T(8,128)(2,1)} %refs_14_.1, ...), custom_call_target="tpu_custom_call" | custom-call | tf_op jit(solution)/shard_map/forward/pallas_call | solution.py:758
  143.2 197.5 %backward.1 = (bf16[128,1536]{1,0:T(8,128)(2,1)}, f32[128,1536]{1,0:T(8,128)}, bf16[8,192,1152]{2,1,0:T(8,128)(2,1)}, bf16[4,192,1536]{2,1,0:T(8,128)(2,1)}, bf1...) custom-call(bf16[8,128,1536]{2,1,0:T(8,128)(2,1)} %get-tuple-element, ...), custom_call_target="tpu_custom_call" | custom-call | tf_op jit(solution)/shard_map/backward/pallas_call | solution.py:1413
  340.7 1.3 slice_bitcast_fusion
  342.0 0.9 fusion.1
  342.9 0.6 constant_dynamic-slice_fusion.3
  343.6 0.6 constant_dynamic-slice_fusion.4
  344.2 0.0 copy-start
  344.2 1.7 copy-done
  345.9 0.0 copy-start.1
  345.9 1.3 copy-done.1
  347.2 10.2 %final_order.1 = (f32[192,9216]{1,0:T(8,128)}, f32[576,1536]{1,0:T(8,128)}, f32[192,1536]{1,0:T(8,128)}, f32[192,2560]{1,0:T(8,128)}) custom-call(bf16[8,192,1152]{2,1,0:T(8,128)(2,1)} %get-tuple-element.103.gu, bf16[4,192,1536]{2,1,0:T(8,128)(2,1)S(1)} %copy-done, bf16[8,192,320]{2,1,0:T(8,128)(2,1)S(1)} %copy-done.1), custom_call_target="tpu_custom_call" | custom-call | tf_op jit(solution)/shard_map/final_order/pallas_call | solution.py:1470
  357.3 0.0 copy-done.3
  357.4 0.7 copy.25
  358.1 0.0 copy-done.2
  358.1 0.9 copy.26
  (8 shorter events, 0.0 us)
Async XLA Ops:
  6.6 4.4 %copy-start.4 = (bf16[16,256]{1,0:T(8,128)(2,1)}, bf16[16,256]{1,0:T(8,128)(2,1)S(1)}, u32[]{:S(2)}) copy-start(bf16[16,256]{1,0:T(8,128)(2,1)S(1)} %scatter.25.refs_4_) | copy-start | bytes 24580
  344.2 1.7 copy-start
  345.9 1.3 copy-start.1
  347.1 10.2 %copy-start.3 = (bf16[128,1536]{1,0:T(8,128)(2,1)S(1)}, bf16[128,1536]{1,0:T(8,128)(2,1)}, u32[]{:S(2)}) copy-start(bf16[128,1536]{1,0:T(8,128)(2,1)} %get-tuple-element.139) | copy-start | bytes 1179652
  347.1 11.0 %copy-start.2 = (f32[128,1536]{1,0:T(8,128)S(1)}, f32[128,1536]{1,0:T(8,128)}, u32[]{:S(2)}) copy-start(f32[128,1536]{1,0:T(8,128)} %get-tuple-element.140) | copy-start | bytes 2359300

commit v4 on v3

v4 whole, which is shorter than its diff:
```python
import functools

import jax
import jax.numpy as jnp
from jax import lax
from jax.experimental import pallas as pl
from jax.experimental.pallas import tpu as pltpu
from jax.sharding import PartitionSpec as P

HEADS = 24
KV_HEADS = 8
HEAD_DIM = 64
GROUP = HEADS // KV_HEADS
Q_COLS = GROUP * HEAD_DIM
HEAD_COLS = Q_COLS + 2 * HEAD_DIM

EPS = 1e-05
THETA = 1000000.0
MESH = pl.DeviceIdType.MESH
F32 = jnp.float32
BF16 = jnp.bfloat16

VMEM = pl.BlockSpec(memory_space=pltpu.VMEM)
ANY = pl.BlockSpec(memory_space=pl.ANY)


def here():
    rep = lax.axis_index("rep")
    grp = lax.axis_index("grp")
    r = rep % 4
    return rep - r, r // 2, r % 2, grp // 2, grp % 2


def device(base, y, c, z, x):
    return {"rep": base + 2 * y + c, "grp": 2 * z + x}


def remote(src, dst, send, recv, to):
    return pltpu.make_async_remote_copy(
        src_ref=src, dst_ref=dst, send_sem=send, recv_sem=recv, device_id=to, device_id_type=MESH
    )


def greet(targets):
    barrier = pltpu.get_barrier_semaphore()
    for to in targets:
        pl.semaphore_signal(barrier, inc=1, device_id=to, device_id_type=MESH)
    pl.semaphore_wait(barrier, len(targets))


def neighbours():
    base, y, c, z, x = here()
    to_c = device(base, y, 1 - c, z, x)
    to_x = device(base, y, c, z, 1 - x)
    to_y = device(base, 1 - y, c, z, x)
    return to_c, to_x, to_y


GATHER_SEMS = 8


class Gather:
    def __init__(self, src, out, send, recv, local):
        self.src, self.out, self.send, self.recv, self.local = src, out, send, recv, local
        _, y, c, _, x = here()
        self.to_c, self.to_x, self.to_y = neighbours()
        slot = lambda a, b, d: 4 * a + 2 * b + d
        self.own = slot(y, c, x)
        self.at_c, self.at_x, self.at_y = slot(y, 1 - c, x), slot(y, c, 1 - x), slot(1 - y, c, x)
        self.at_xc, self.at_yc = slot(y, 1 - c, 1 - x), slot(1 - y, 1 - c, x)
        self.at_xy, self.at_xyc = slot(1 - y, c, 1 - x), slot(1 - y, 1 - c, 1 - x)
        self.half = src.shape[0] // 2

    def part(self, ref, k):
        return ref.at[pl.ds(k * self.half, self.half)]

    def copy(self, k, src, dst, to):
        return remote(src, dst, self.send.at[k], self.recv.at[k], to)

    def start(self):
        out, src = self.out, self.src
        self.keep = pltpu.make_async_copy(src, out.at[self.own], self.local)
        self.keep.start()
        self.sent = [
            self.copy(0, src, out.at[self.own], self.to_x),
            self.copy(1, src, out.at[self.own], self.to_y),
            self.copy(2, src, out.at[self.own], self.to_c),
        ]
        for copy in self.sent:
            copy.start()

    def forward(self):
        out = self.out
        self.copy(0, self.src, out.at[self.at_x], self.to_x).wait_recv()
        first = self.part(out.at[self.at_x], 0)
        self.go(3, first, first, self.to_y)
        self.go(4, out.at[self.at_x], out.at[self.at_x], self.to_c)
        self.copy(1, self.src, out.at[self.at_y], self.to_y).wait_recv()
        second = self.part(out.at[self.at_y], 1)
        self.go(5, second, second, self.to_x)
        self.go(6, out.at[self.at_y], out.at[self.at_y], self.to_c)

    def go(self, k, src, dst, to):
        copy = self.copy(k, src, dst, to)
        copy.start()
        self.sent.append(copy)

    def finish(self):
        out = self.out
        first = self.part(out.at[self.at_xy], 0)
        second = self.part(out.at[self.at_xy], 1)
        self.copy(3, first, first, self.to_y).wait_recv()
        self.copy(5, second, second, self.to_x).wait_recv()
        self.go(7, out.at[self.at_xy], out.at[self.at_xy], self.to_c)
        for k, at in ((2, self.at_c), (4, self.at_xc), (6, self.at_yc), (7, self.at_xyc)):
            self.copy(k, out.at[at], out.at[at], self.to_c).wait_recv()
        for copy in self.sent:
            copy.wait_send()
        self.keep.wait()


def dma(n):
    return pltpu.SemaphoreType.DMA((n,))


def params(cid, limit=60):
    return pltpu.CompilerParams(
        collective_id=cid, has_side_effects=True, vmem_limit_bytes=limit * 2**20
    )


def inverse_rms(v):
    return lax.rsqrt(jnp.mean(v * v, axis=-1, keepdims=True) + EPS)


def norm_back(dy, v, inv, gain):
    scaled = dy * gain
    gain_grad = jnp.sum(dy * v * inv, axis=0, keepdims=True)
    inner = jnp.mean(scaled * v, axis=-1, keepdims=True)
    return inv * scaled - v * inv * inv * inv * inner, gain_grad


def when(cond):
    return pl.when(cond)


def lanes(shape):
    return lax.broadcasted_iota(jnp.int32, shape, len(shape) - 1)


def roll(v, by):
    return pltpu.roll(v, by % v.shape[-1], v.ndim - 1)


class Along:
    def __init__(self, src, slot, send, recv):
        self.src, self.slot, self.send, self.recv = src, slot, send, recv
        self.base, self.y, self.c, self.z, self.x = here()

    def at(self, zk, x):
        return device(self.base, self.y, self.c, zk, x)

    def copy(self, d):
        zk = (self.z + d + 4) % 4
        return remote(self.src, self.slot(self.z), self.send.at[d + 2], self.recv.at[self.z],
                      self.at(zk, self.x))

    def fits(self, d):
        return (self.z + d >= 0) & (self.z + d < 4)

    def first(self):
        for d in (2, -2):
            pl.when(self.fits(d))(lambda d=d: self.copy(d).start())
        pl.when(self.z == 2)(lambda: self.copy(1).start())
        pl.when(self.z == 1)(lambda: self.copy(-1).start())

    def second(self):
        pl.when(self.z < 2)(lambda: self.copy(1).start())
        pl.when(self.z >= 2)(lambda: self.copy(-1).start())

    def arrival(self, zk):
        ref = self.slot(zk)
        return remote(ref, ref, self.send.at[0], self.recv.at[zk], self.at(self.z, 1 - self.x))

    def passed(self, zk, to):
        ref = self.slot(zk)
        return remote(ref, ref, self.send.at[5], self.recv.at[zk], self.at(to, self.x))

    def forward(self):
        @pl.when(self.z == 2)
        def _():
            self.arrival(0).wait_recv()
            self.passed(0, 3).start()

        @pl.when(self.z == 1)
        def _():
            self.arrival(3).wait_recv()
            self.passed(3, 0).start()

    def wait(self, zk):
        early = ((self.z == 2) & (zk == 0)) | ((self.z == 1) & (zk == 3))
        due = jnp.logical_not(early) & (self.z != zk)
        pl.when(due)(lambda: self.arrival(zk).wait_recv())

    def finish(self):
        for zk in range(4):
            self.wait(zk)

    def sent(self):
        for d in (2, -2, 1, -1):
            pl.when(self.fits(d))(lambda d=d: self.copy(d).wait_send())
        pl.when(self.z == 2)(lambda: self.passed(0, 3).wait_send())
        pl.when(self.z == 1)(lambda: self.passed(3, 0).wait_send())


class Chain:
    def __init__(self, slot, send, recv):
        self.slot, self.send, self.recv = slot, send, recv
        self.base, self.y, self.c, self.z, self.x = here()

    def copy(self, k, zk, to):
        return remote(self.slot(zk), self.slot(zk), self.send.at[k], self.recv.at[zk],
                      device(self.base, self.y, self.c, to, self.x))

    def arrive(self, zk):
        self.copy(0, zk, self.z).wait_recv()

    def inner(self):
        return (self.z == 1) | (self.z == 2)

    def start_ends(self):
        pl.when(self.z == 0)(lambda: self.copy(0, 0, 1).start())
        pl.when(self.z == 3)(lambda: self.copy(1, 3, 2).start())

    def start_inner(self):
        z = self.z

        @pl.when(self.inner())
        def _():
            self.copy(0, z, z + 1).start()
            self.copy(1, z, z - 1).start()

    def pass_ends(self):
        @pl.when(self.z == 1)
        def _():
            self.arrive(0)
            self.copy(2, 0, 2).start()

        @pl.when(self.z == 2)
        def _():
            self.arrive(3)
            self.copy(3, 3, 1).start()

    def pass_inner(self):
        @pl.when(self.z == 1)
        def _():
            self.arrive(2)
            self.copy(3, 2, 0).start()

        @pl.when(self.z == 2)
        def _():
            self.arrive(1)
            self.copy(2, 1, 3).start()

    def second(self):
        self.pass_ends()
        self.pass_inner()

    def third(self):
        @pl.when(self.z == 2)
        def _():
            self.arrive(0)
            self.copy(4, 0, 3).start()

        @pl.when(self.z == 1)
        def _():
            self.arrive(3)
            self.copy(4, 3, 0).start()

    def finish(self):
        pl.when(self.z == 0)(lambda: [self.arrive(zk) for zk in (1, 2, 3)] and None)
        pl.when(self.z == 3)(lambda: [self.arrive(zk) for zk in (2, 1, 0)] and None)

    def sent(self):
        z = self.z
        pl.when(z < 3)(lambda: self.copy(0, z, z + 1).wait_send())
        pl.when(z > 0)(lambda: self.copy(1, z, z - 1).wait_send())

        @pl.when(self.inner())
        def _():
            self.copy(2, z - 1, z + 1).wait_send()
            self.copy(3, z + 1, z - 1).wait_send()
            self.copy(4, z, z + 1).wait_send()


class ChainSum:
    def __init__(self, block, slot, send, recv):
        self.block, self.slot, self.send, self.recv = block, slot, send, recv
        self.base, self.y, self.c, self.z, self.x = here()

    def copy(self, zk, to, at):
        return remote(self.block(zk), self.slot(at), self.send.at[zk], self.recv.at[at],
                      device(self.base, self.y, self.c, to, self.x))

    def arrive(self, at):
        self.copy(0, self.z, at).wait_recv()

    def start(self):
        @pl.when(self.z == 0)
        def _():
            for zk, at in ((3, 3), (2, 2), (1, 4)):
                self.copy(zk, 1, at).start()

        @pl.when(self.z == 3)
        def _():
            for zk in (0, 1, 2):
                self.copy(zk, 2, zk).start()

    def start_one(self, zk):
        for to, at in ((3, 3), (2, 2), (1, 4)):
            pl.when((self.z == 0) & (zk == to))(
                lambda to=to, at=at: self.copy(to, 1, at).start())
        for to in (0, 1, 2):
            pl.when((self.z == 3) & (zk == to))(lambda to=to: self.copy(to, 2, to).start())

    def first_hop(self, add):
        @pl.when(self.z == 1)
        def _():
            for zk, at in ((3, 3), (2, 4)):
                self.arrive(zk)
                add(self.block(zk), self.slot(zk))
                self.copy(zk, 2, at).start()

        @pl.when(self.z == 2)
        def _():
            for zk in (0, 1):
                self.arrive(zk)
                add(self.block(zk), self.slot(zk))
                self.copy(zk, 1, zk).start()

    def second_hop(self, add):
        @pl.when(self.z == 1)
        def _():
            self.arrive(0)
            add(self.block(0), self.slot(0))
            self.copy(0, 0, 0).start()

        @pl.when(self.z == 2)
        def _():
            self.arrive(3)
            add(self.block(3), self.slot(3))
            self.copy(3, 3, 4).start()

    def collect(self, total):
        z = self.z

        def take(ats):
            for at in ats:
                self.arrive(at)
            total([self.slot(at) for at in ats])

        pl.when(z == 0)(lambda: take([0]))
        pl.when(z == 3)(lambda: take([4]))
        pl.when((z == 1) | (z == 2))(lambda: take([z, 4]))

    def sent(self):
        for zk in range(4):
            pl.when(self.z != zk)(lambda zk=zk: self.copy(zk, 0, 0).wait_send())


def layer_mates():
    base, y, c, z, x = here()
    return [
        device(base, (y + k // 4) % 2, (c + k // 2) % 2, z, (x + k) % 2) for k in range(1, 8)
    ]


def z_mates():
    base, y, c, z, x = here()
    return [device(base, y, c, (z + k // 2) % 4, (x + k) % 2) for k in range(2, 8)]


def rotated(u, cos, sin):
    lane = lanes(u.shape)
    return u * cos + jnp.where(lane < 32, roll(u, -32), roll(u, 32)) * sin


def low_half(v):
    return jnp.where(lanes(v.shape) < HEAD_DIM, v, 0.0)


def high_half(v):
    return jnp.where(lanes(v.shape) >= HEAD_DIM, v, 0.0)


def split_heads(tile_a, tile_b):
    return [low_half(tile_a), low_half(roll(tile_a, 64)), low_half(tile_b),
            low_half(roll(tile_b, 64))]


def head_inverse(u):
    return lax.rsqrt(jnp.sum(u * u, axis=-1, keepdims=True) * (1.0 / HEAD_DIM) + EPS)


def exp_scores(q, kv, q_seg, k_seg, diagonal):
    s = lax.dot_general(q, kv, (((1,), (1,)), ((), ())), preferred_element_type=F32)
    allowed = q_seg == k_seg
    if diagonal:
        row = lax.broadcasted_iota(jnp.int32, allowed.shape, 0)
        col = lax.broadcasted_iota(jnp.int32, allowed.shape, 1)
        allowed = allowed & (col <= row)
    n = allowed.shape[0]
    return jnp.concatenate([
        jnp.where(allowed, jnp.exp(s[n * j:n * (j + 1)]), 0.0) for j in range(GROUP)], axis=0)


def segment_row(segs, zk, s):
    return jnp.concatenate([segs[zk, 2 * s, 0:1], segs[zk, 2 * s + 1, 0:1]], axis=1)


def segment_columns(segs, zk, s):
    parts = []
    for i in range(2):
        row = jnp.broadcast_to(segs[zk, 2 * s + i, 0:1], (128, 128))
        parts.append(jnp.transpose(row))
    col = jnp.concatenate(parts, axis=0)
    return jnp.concatenate([col, col], axis=1)


class SeqSum:
    def __init__(self, part, scratch):
        self.part = part
        (self.r1, self.chip, self.rx, self.ry, self.mine, self.late, self.out,
         self.send, self.recv) = scratch
        _, self.y, self.c, _, self.x = here()
        self.to_c, self.to_x, self.to_y = neighbours()

    def copy(self, k, src, dst, to):
        return remote(src, dst, self.send.at[k], self.recv.at[k], to)

    def swap(self, b, a):
        at = 2 * b + a
        return self.copy(at, self.part.at[4 * b + 2 * (1 - self.c) + a], self.r1.at[at], self.to_c)

    def give(self, b):
        for a in range(2):
            self.swap(b, a).start()

    def along_x(self, b):
        at = 2 * b + 1 - self.x
        return self.copy(4 + b, self.chip.at[at, pl.ds(0, 64)], self.rx.at[b], self.to_x)

    def along_y(self, a):
        at = 2 * (1 - self.y) + a
        return self.copy(6 + a, self.chip.at[at, pl.ds(64, 64)], self.ry.at[a], self.to_y)

    def last_y(self):
        return self.copy(8, self.mine.at[0], self.late.at[0], self.to_y)

    def last_x(self):
        return self.copy(9, self.mine.at[1], self.late.at[1], self.to_x)

    def total(self, b, a):
        self.swap(b, a).wait_recv()
        at = 2 * b + a
        return self.part[4 * b + 2 * self.c + a].astype(F32) + self.r1[at].astype(F32)

    def take_far(self):
        b = 1 - self.y
        for a in (1 - self.x, self.x):
            self.chip[2 * b + a] = self.total(b, a).astype(BF16)
            self.along_y(a).start()
            if a is not self.x:
                self.along_x(b).start()

    def take_near(self):
        b, x = self.y, self.x
        self.chip[2 * b + 1 - x] = self.total(b, 1 - x).astype(BF16)
        self.along_x(b).start()
        self.out[...] = self.total(b, x)

    def middle(self):
        x, y = self.x, self.y
        self.along_x(1 - y).wait_recv()
        self.mine[0] = (
            self.chip[2 * (1 - y) + x, 0:64].astype(F32) + self.rx[1 - y].astype(F32)
        ).astype(BF16)
        self.last_y().start()
        self.along_y(1 - x).wait_recv()
        self.mine[1] = (
            self.chip[2 * y + 1 - x, 64:128].astype(F32) + self.ry[1 - x].astype(F32)
        ).astype(BF16)
        self.last_x().start()

    def finish(self):
        x, y = self.x, self.y
        self.along_x(y).wait_recv()
        self.along_y(x).wait_recv()
        self.last_y().wait_recv()
        self.last_x().wait_recv()
        self.out[0:64] += self.rx[y].astype(F32) + self.late[0].astype(F32)
        self.out[64:128] += self.ry[x].astype(F32) + self.late[1].astype(F32)

    def given(self):
        for b in range(2):
            for a in range(2):
                self.swap(b, a).wait_send()

    def passed(self):
        for b in range(2):
            self.along_x(b).wait_send()
            self.along_y(b).wait_send()
        self.last_y().wait_send()
        self.last_x().wait_send()

    def sent(self):
        self.given()
        self.passed()


def seq_scratch(width):
    return [
        pltpu.VMEM((4, 128, width), BF16),
        pltpu.VMEM((4, 128, width), BF16),
        pltpu.VMEM((2, 64, width), BF16),
        pltpu.VMEM((2, 64, width), BF16),
        pltpu.VMEM((2, 64, width), BF16),
        pltpu.VMEM((2, 64, width), BF16),
        pltpu.VMEM((128, width), F32),
        dma(10),
        dma(10),
    ]


def first_dims(left, right):
    return lax.dot_general(left, right, (((0,), (0,)), ((), ())), preferred_element_type=F32)


def last_dims(left, right):
    return lax.dot_general(left, right, (((1,), (1,)), ((), ())), preferred_element_type=F32)


def swiglu(gate, up, grad):
    sigma = 1.0 / (1.0 + jnp.exp(-gate))
    active = gate * sigma
    d_gate = grad * up * sigma * (1.0 + gate * (1.0 - sigma))
    return ((active * up).astype(BF16), d_gate.astype(BF16), (grad * active).astype(BF16))


class DirectBoth:
    def __init__(self, half, slot, send, recv):
        self.half, self.slot, self.send, self.recv = half, slot, send, recv
        self.base, self.y, self.c, self.z, self.x = here()

    def copy(self, zk, a):
        return remote(self.half(zk, a), self.slot(self.z, self.x), self.send.at[zk, a],
                      self.recv.at[self.z, self.x], device(self.base, self.y, self.c, zk, a))

    def start(self, zk):
        self.copy(zk, 1 - self.x).start()
        pl.when(zk != self.z)(lambda: self.copy(zk, self.x).start())

    def arrive(self, zk, a):
        ref = self.slot(zk, a)
        remote(ref, ref, self.send.at[0, 0], self.recv.at[zk, a],
               device(self.base, self.y, self.c, self.z, 1 - self.x)).wait_recv()

    def sent(self):
        for k in range(1, 8):
            self.copy((self.z + k // 2) % 4, (self.x + k) % 2).wait_send()


class RepShare:
    def __init__(self, at, send, recv):
        self.at, self.send, self.recv = at, send, recv
        _, self.y, self.c, _, _ = here()
        self.to_c, _, self.to_y = neighbours()
        self.r = 2 * self.y + self.c

    def copy(self, k, r, to):
        return remote(self.at(r), self.at(r), self.send.at[k], self.recv.at[k], to)

    def start(self):
        self.copy(0, self.r, self.to_y).start()
        self.copy(1, self.r, self.to_c).start()

    def forward(self):
        other = 2 * (1 - self.y) + self.c
        self.copy(0, other, self.to_y).wait_recv()
        self.copy(2, other, self.to_c).start()

    def finish(self):
        self.copy(1, 2 * self.y + 1 - self.c, self.to_c).wait_recv()
        self.copy(2, 2 * (1 - self.y) + 1 - self.c, self.to_c).wait_recv()

    def sent(self):
        self.copy(0, self.r, self.to_y).wait_send()
        self.copy(1, self.r, self.to_c).wait_send()
        self.copy(2, self.r, self.to_c).wait_send()


def head_back(dy, u, gain):
    inv = head_inverse(u)
    scaled = dy * gain
    gain_grad = jnp.sum(dy * u * inv, axis=0, keepdims=True)
    inner = jnp.sum(scaled * u, axis=-1, keepdims=True) * (1.0 / HEAD_DIM)
    return inv * scaled - u * (inv * inv * inv * inner), gain_grad


def block_kernel(names, *refs):
    m = dict(zip(names, refs))
    base, y, c, z, x = here()
    r = 2 * y + c
    to_c, to_x, to_y = neighbours()
    greet(layer_mates() + z_mates())
    rows, width = m["tok"].shape
    quarter_o = m["wo"].shape[0] // 4
    own_rows = m["wq"].shape[1]
    half_cols = m["wgu"].shape[1] // 2
    piece = half_cols // 4
    part = piece // 2
    main = part // 128 * 128
    half_a = main // 2
    rows_a, rows_b, rest = half_a // 4, (part - half_a) // 4, part - main
    keep = m["keep"]
    own = 2 * z + x
    t_own = 2 * r + x

    def local_copy(k, src, dst):
        return pltpu.make_async_copy(src, dst, keep.at[k])

    hidden, dgu, wgu, wd_v = m["hidden"], m["dgu"], m["wgu_v"], m["wd_v"]
    cols_a = 2 * half_a
    cols_b = dgu.shape[1] - cols_a

    def raw(i):
        return dgu.at[pl.ds(i * own_rows, own_rows)]

    def pair(a, first, n):
        return dgu.at[pl.ds((2 + a) * own_rows, own_rows), pl.ds(first, n)]

    def loaded(k, src, dst):
        copy = local_copy(k, src, dst)
        copy.start()
        return copy

    tok = Gather(m["tok"], m["tok_all"], m["ga_s"], m["ga_r"], keep.at[0])
    cot = Gather(m["cot"], m["cot_v"], m["gb_s"], m["gb_r"], keep.at[1])
    segs = m["segs_v"]
    mates = layer_mates()

    def seg_copy(k):
        return remote(m["seg"], segs.at[z, t_own], m["sg_s"].at[k - 1], m["sg_r"].at[k - 1],
                      mates[k - 1])

    def gain_target(k):
        return device(base, y, c, (z + k // 2) % 4, (x + k) % 2)

    def gain_copy(k):
        return remote(m["gains"], m["gains_all"].at[own], m["gn_s"].at[k - 1],
                      m["gn_r"].at[k - 1], gain_target(k))

    wq = m["wq_v"]

    def wq_slot(zk, a):
        return wq.at[pl.ds((2 * zk + a) * own_rows, own_rows)]

    near = Along(m["wq"].at[x], lambda zk: wq_slot(zk, x), m["wa_s"], m["wa_r"])
    flip = Along(wq_slot(z, 1 - x), lambda zk: wq_slot(zk, 1 - x), m["wb_s"], m["wb_r"])
    over = remote(m["wq"].at[1 - x], wq_slot(z, x), m["wx_s"], m["wx_r"], to_x)
    over_in = remote(m["wq"].at[x], wq_slot(z, 1 - x), m["wx_s"], m["wx_r"], to_x)
    for k in range(1, 8):
        seg_copy(k).start()
    over.start()
    near.first()
    near.second()
    tok.start()
    local = [
        local_copy(2, m["wq"].at[x], wq_slot(z, x)),
        local_copy(3, m["gains"], m["gains_all"].at[own]),
        local_copy(4, m["seg"], segs.at[z, t_own]),
        local_copy(5, m["wgu"].at[:, pl.ds(piece * r, piece)], raw(0)),
        local_copy(6, m["wgu"].at[:, pl.ds(half_cols + piece * r, piece)], raw(1)),
    ]
    for copy in local:
        copy.start()
    for k in range(1, 8):
        gain_copy(k).start()
    out_q = Along(m["wo"].at[pl.ds(quarter_o * r, quarter_o)], lambda zk: m["zo"].at[zk],
                  m["wo_s"], m["wo_r"])
    last = r // 3
    tail_at = rest * x + half_a + rows_b * r + 16 - last * x * part
    quarters = [
        local_copy(7, m["wo"].at[pl.ds(quarter_o * r, quarter_o)], m["zo"].at[z]),
        local_copy(8, m["wd"].at[pl.ds(rest * x + rows_a * r, rows_a)], m["za"].at[z]),
        local_copy(13, m["wd"].at[pl.ds(rest * x + half_a + rows_b * r, 16)],
                   m["zb"].at[z, pl.ds(0, 16)]),
        local_copy(14, m["wd"].at[pl.ds(tail_at, rows_b - 16)],
                   m["zb"].at[z, pl.ds(16, rows_b - 16)]),
    ]
    for copy in quarters:
        copy.start()
    over_in.wait_recv()
    flip.first()
    flip.second()
    out_q.first()
    out_q.second()

    def seg_up(k):
        return remote(segs.at[z], segs.at[z], m["su_s"].at[k - 1], m["su_r"].at[z],
                      device(base, y, c, (z + k) % 4, x))

    for k in range(1, 8):
        seg_copy(k).wait_recv()
    local[2].wait()
    for k in range(3, 0, -1):
        pl.when(z + k < 4)(lambda k=k: seg_up(k).start())

    local[3].wait()
    local[4].wait()
    gate, up = raw(0), raw(1)
    for a in range(2):
        at = a * (piece - main)
        for i, src in enumerate((gate, up)):
            pair(a, i * half_a, half_a)[...] = src[:, at:at + half_a]
            pair(a, cols_a + i * half_a, half_a)[...] = src[:, at + half_a:at + main]
    g_tile = gate[:, main:main + 128].astype(F32)
    u_tile = up[:, main:main + 128].astype(F32)
    low = lanes(g_tile.shape) < HEAD_DIM
    pair(0, 2 * main, 128)[...] = jnp.where(low, g_tile, roll(u_tile, 64)).astype(BF16)
    pair(1, 2 * main, 128)[...] = jnp.where(low, roll(g_tile, 64), u_tile).astype(BF16)

    def unit(first, n):
        return lambda zk: wgu.at[pl.ds(2 * zk * own_rows, 2 * own_rows), pl.ds(first, n)]

    def crossing(first, n, ss, rs, k):
        cols = pl.ds(first, n)
        mine = wgu.at[pl.ds((2 * z + x) * own_rows, own_rows), cols]
        other = wgu.at[pl.ds((2 * z + 1 - x) * own_rows, own_rows), cols]
        return (remote(pair(1 - x, first, n), mine, ss, rs, to_x),
                remote(pair(x, first, n), other, ss, rs, to_x),
                local_copy(k, pair(x, first, n), mine))

    cross_a, cross_a_in, mine_a = crossing(0, cols_a, m["xa_s"], m["xa_r"], 5)
    cross_b, cross_b_in, mine_b = crossing(cols_a, cols_b, m["xb_s"], m["xb_r"], 6)
    gate_a = Chain(unit(0, cols_a), m["ca_s"], m["ca_r"])
    gate_b = Chain(unit(cols_a, cols_b), m["cb_s"], m["cb_r"])
    down_a = Chain(lambda zk: m["za"].at[zk], m["da_s"], m["da_r"])
    down_b = Chain(lambda zk: m["zb"].at[zk], m["db_s"], m["db_r"])
    tok.forward()
    for copy in (cross_a, mine_a, cross_b, mine_b):
        copy.start()
    near.forward()
    flip.forward()
    out_q.forward()
    tok.finish()
    cot.start()
    near.finish()
    flip.finish()
    for k in range(1, 8):
        at = 2 * ((z + 4 - k // 2) % 4) + (x + k) % 2
        remote(m["gains"], m["gains_all"].at[at], m["gn_s"].at[k - 1], m["gn_r"].at[k - 1],
               to_c).wait_recv()
    for k in (0, 1):
        local[k].wait()
    gather_gains = pltpu.make_async_copy(m["gains_all"], m["gains_v"], keep.at[3])
    gather_gains.start()
    gather_gains.wait()
    gain_rows = []
    for i in range(2):
        gain_rows.append(jnp.concatenate(
            [m["gains_v"][k, 0:16].astype(F32)[i:i + 1, :own_rows] for k in range(8)], axis=1))
    m["g_one"][...], m["g_two"][...] = gain_rows
    kv = m["kv_v"]
    q_all, qkv_all = m["q_v"], m["qkv_v"]
    qg, kg, cos, sin = m["qg"][...], m["kg"][...], m["cos"][...], m["sin"][...]
    span = 2 * rows

    def order(k):
        return (y + 1 + k) % 2, (c + 1 + k // 2) % 2

    def kv_copy(d, s):
        return remote(kv.at[z, s], kv.at[z, s], m["kv_s"].at[d - 1, s], m["kv_r"].at[z, s],
                      device(base, y, c, (z + d) % 4, x))

    def kv_arrival(zk, s):
        return remote(kv.at[zk, s], kv.at[zk, s], m["kv_s"].at[0, s], m["kv_r"].at[zk, s], to_x)

    def project(k, carry):
        b, e = order(k)
        s = 2 * b + e
        tokens = m["tok_all"][pl.ds(2 * s, 2)].reshape(span, width).astype(F32)
        normed = (tokens * inverse_rms(tokens) * m["g_one"][...]).astype(BF16)
        m["tok_all"][pl.ds(2 * s, 2)] = normed.reshape(2, rows, width)
        qkv = jnp.dot(normed, wq[...], preferred_element_type=F32)
        qkv_all[s] = qkv[:, 0:256]
        heads = split_heads(qkv[:, 0:128], qkv[:, 128:256])
        for j in range(GROUP):
            u = heads[j]
            u = rotated(u * head_inverse(u) * qg[0:1], cos, sin) * HEAD_DIM ** (-0.5)
            q_all[s, pl.ds(j * span, span)] = u.astype(BF16)
        u = heads[GROUP]
        u = rotated(u * head_inverse(u) * kg[0:1], cos, sin)
        v = jnp.concatenate([jnp.zeros((span, HEAD_DIM), F32), qkv[:, 256:320]], axis=1)
        kv[z, s] = (u + v).astype(BF16)
        for d in (3, 2, 1):
            pl.when(z + d < 4)(lambda d=d: kv_copy(d, s).start())
        return carry

    lax.fori_loop(0, 4, project, 0)
    for copy in quarters[1:]:
        copy.wait()
    down_a.start_ends()
    down_a.start_inner()
    for copy in (mine_a, mine_b):
        copy.wait()
    cross_a_in.wait_recv()
    gate_a.start_ends()
    gate_a.start_inner()
    cross_b_in.wait_recv()
    down_b.start_ends()
    gate_b.start_ends()
    cot.forward()

    def hand(k, zk, src, dst, sems, n):
        ss, rs = sems
        to = device(base, zk // 2, zk % 2, z, x)
        pl.when(r != zk)(lambda: remote(src.at[zk], dst.at[pl.ds(n * r, n)], ss.at[zk],
                                        rs.at[r], to).start())

        @pl.when(r == zk)
        def _():
            copy = local_copy(k, src.at[zk], dst.at[pl.ds(n * r, n)])
            copy.start()
            copy.wait()

    def handed(src, dst, sems, n):
        ss, rs = sems
        for rk in range(4):
            ref = dst.at[pl.ds(n * rk, n)]
            pl.when(r != rk)(lambda ref=ref, rk=rk: remote(
                src.at[0], ref, ss.at[0], rs.at[rk], to_x).wait_recv())

    def hand_sent(src, dst, sems, n):
        ss, rs = sems
        for zk in range(4):
            pl.when(r != zk)(lambda zk=zk: remote(
                src.at[zk], dst.at[pl.ds(0, n)], ss.at[zk], rs.at[0], to_x).wait_send())

    quarters[0].wait()
    out_q.finish()
    out_sems = (m["ho_s"], m["ho_r"])
    a_sems, b_sems = (m["hd_s"], m["hd_r"]), (m["hb_s"], m["hb_r"])
    for zk in range(4):
        hand(13, zk, m["zo"], m["wo_v"], out_sems, quarter_o)

    for k in range(1, 4):
        pl.when(z - k >= 0)(lambda k=k: remote(
            segs.at[0], segs.at[(z + 4 - k) % 4], m["su_s"].at[k - 1],
            m["su_r"].at[(z + 4 - k) % 4], to_x).wait_recv())

    summed = SeqSum(m["part"], [m[n] for n in SUM_NAMES])
    inv_all, att = m["inv_v"], m["att_v"]
    acc, q_seg = m["acc"], m["q_seg"]

    def attend_one(k, carry):
        b, e = order(k)
        s = 2 * b + e
        q_seg[...] = segment_columns(segs, z, s)

        def block(zk, diagonal):
            tile = kv[zk, s]
            p = exp_scores(q_all[s], tile, q_seg[...], segment_row(segs, zk, s), diagonal)
            ones = jnp.where(lanes(tile.shape) < HEAD_DIM, 1.0, tile.astype(F32)).astype(BF16)
            add = jnp.dot(p.astype(BF16), ones, preferred_element_type=F32)
            if diagonal:
                acc[...] = add
            else:
                acc[...] += add

        block(z, True)

        def step(i, inner):
            zk = z - 1 - i
            kv_arrival(zk, s).wait_recv()
            block(zk, False)
            return inner

        lax.fori_loop(0, z, step, 0)
        total = acc[...]
        inv = 1.0 / jnp.where(lanes(total.shape) < HEAD_DIM, total, 1.0)
        inv = jnp.where(lanes(total.shape) < HEAD_DIM, inv, roll(inv, 64))
        o = high_half(total * inv)
        lane = lanes((span, 128))
        inv_all[s] = jnp.where(lane < 32, inv[0:span], jnp.where(
            lane < 64, inv[span:2 * span], inv[2 * span:]))
        first, second, third = o[0:span], o[span:2 * span], o[2 * span:]
        att[s, :, 0:128] = (roll(first, 64) + second).astype(BF16)
        att[s, :, 128:192] = roll(third, 64)[:, 0:HEAD_DIM].astype(BF16)
        pl.when(k == 0)(lambda: handed(m["zo"], m["wo_v"], out_sems, quarter_o))
        out = jnp.dot(att[s], m["wo_v"][...], preferred_element_type=F32).astype(BF16)
        m["part"][pl.ds(2 * s, 2)] = out.reshape(2, rows, width)
        pl.when(k < 2)(lambda: summed.give(b))
        pl.when(k == 2)(summed.take_far)
        pl.when(k == 3)(summed.take_near)
        return carry

    lax.fori_loop(0, 4, attend_one, 0)
    down_a.second()
    gate_a.second()
    summed.middle()
    down_a.third()
    summed.finish()
    mid = m["tok"][...].astype(F32) + summed.out[...]
    m["mid"][...] = mid
    m["low"][...] = (mid * inverse_rms(mid) * m["g_two"][...]).astype(BF16)
    n2_all, cot_all = m["n2_v"], m["cot_v"]
    n2 = Gather(m["low"], n2_all, m["gc_s"], m["gc_r"], keep.at[20])
    n2.start()
    cot.finish()
    gate_a.third()
    down_b.pass_ends()
    gate_b.pass_ends()
    down_b.start_inner()
    gate_b.start_inner()
    n2.forward()
    down_a.finish()
    wda, wdb = wd_v.at[pl.ds(0, half_a)], wd_v.at[pl.ds(half_a, part - half_a)]
    for zk in range(4):
        hand(13, zk, m["za"], wda, a_sems, rows_a)
    n2.finish()
    gate_a.finish()
    handed(m["za"], wda, a_sems, rows_a)
    cross_a.wait_send()
    cross_b.wait_send()

    def feed_first(s, carry):
        at = pl.ds(pl.multiple_of(s * span, span), span)
        gu = jnp.dot(n2_all[pl.ds(2 * s, 2)].reshape(span, width), wgu[:, :cols_a],
                     preferred_element_type=F32)
        dh = last_dims(cot_all[pl.ds(2 * s, 2)].reshape(span, width), wd_v[0:half_a])
        hidden[at, 0:half_a], dgu[at, 0:half_a], dgu[at, half_a:cols_a] = swiglu(
            gu[:, :half_a], gu[:, half_a:], dh)
        return carry

    lax.fori_loop(0, 4, feed_first, 0)
    down_b.third()
    gate_b.third()
    down_b.pass_inner()
    gate_b.pass_inner()
    block_rows = 2 * own_rows
    gga, gdo, got_a = m["gga"], m["gdo"], m["got_a"]
    gate_sum = ChainSum(lambda zk: gga.at[zk], lambda at: m["gga_slot"].at[at], m["ys_s"],
                        m["ys_r"])
    down_sum = ChainSum(lambda zk: got_a.at[zk], lambda at: m["gda_slot"].at[at], m["yd_s"],
                        m["yd_r"])

    def grad_gate(zk, carry):
        cols = pl.ds(pl.multiple_of(zk * block_rows, 128), block_rows)
        left = n2_all[:, :, cols].reshape(8 * rows, block_rows)
        gga[zk] = first_dims(left, dgu[:, :cols_a]).astype(BF16)
        return carry

    lax.fori_loop(0, 4, grad_gate, 0)
    gate_sum.start()
    for j in range(0, half_a, 128):
        grad = first_dims(hidden[:, j:j + 128], cot_all[...].reshape(8 * rows, width))
        for h in range(128 // rows_a):
            gdo[j // rows_a + h, 0:rows_a] = grad[rows_a * h:rows_a * (h + 1)].astype(BF16)

    def spread_from(i):
        return gdo.at[i, pl.ds(0, rows_a)]

    def spread(i):
        return remote(spread_from(i), got_a.at[r], m["ha_s"].at[i], m["ha_r"].at[r],
                      device(base, i // 2, i % 2, z, x))

    for i in range(4):
        pl.when(r != i)(lambda i=i: spread(i).start())
    got_a[r] = gdo[r, 0:rows_a]

    def add(block, slot):
        block[...] = (block[...].astype(F32) + slot[...].astype(F32)).astype(BF16)

    gate_sum.first_hop(add)
    down_b.finish()
    for zk in range(4):
        hand(13, zk, m["zb"], wdb, b_sems, rows_b)
    gate_b.finish()
    handed(m["zb"], wdb, b_sems, rows_b)
    for i in range(4):
        pl.when(r != i)(lambda i=i: remote(
            spread_from(i), got_a.at[i], m["ha_s"].at[i], m["ha_r"].at[i], to_c).wait_recv())
    down_sum.start()
    gate_sum.second_hop(add)
    summed.sent()

    def total_in(block):
        def total(slots):
            value = block[...].astype(F32)
            for slot in slots:
                value = value + slot[...].astype(F32)
            block[...] = value.astype(BF16)
        return total

    parts, n2, cot_v, normed = m["part"], m["n2_v"], m["cot_v"], m["tok_all"]
    wd_v[pl.ds(part, 128 - rest)] = jnp.zeros((128 - rest, width), BF16)

    def feed(k, carry):
        b, e = order(k)
        s = 2 * b + e
        at = pl.ds(pl.multiple_of(s * span, span), span)
        gu = jnp.dot(n2[pl.ds(2 * s, 2)].reshape(span, width), wgu[:, cols_a:],
                     preferred_element_type=F32)
        dh = last_dims(cot_v[pl.ds(2 * s, 2)].reshape(span, width), wd_v[half_a:])
        (hidden[at, half_a:2 * half_a], dgu[at, cols_a:cols_a + half_a],
         dgu[at, cols_a + half_a:cols_a + 2 * half_a]) = swiglu(
            gu[:, :half_a], gu[:, half_a:2 * half_a], dh[:, :half_a])
        tile = gu[:, 2 * half_a:]
        gate, up, grad = low_half(tile), low_half(roll(tile, 64)), dh[:, half_a:]
        sigma = 1.0 / (1.0 + jnp.exp(-gate))
        active = gate * sigma
        hidden[at, 2 * half_a:] = (active * up).astype(BF16)
        d_gate = grad * up * sigma * (1.0 + gate * (1.0 - sigma))
        dgu[at, cols_a + 2 * half_a:] = (
            d_gate + roll(low_half(grad * active), 64)).astype(BF16)
        out = last_dims(dgu[at], wgu[...]).astype(BF16)
        parts[pl.ds(2 * s, 2)] = out.reshape(2, rows, width)
        pl.when(k < 2)(lambda: summed.give(b))
        pl.when(k == 2)(summed.take_far)
        pl.when(k == 3)(summed.take_near)
        return carry

    lax.fori_loop(0, 4, feed, 0)
    down_sum.first_hop(add)

    ggu = m["ggu"]
    gu_sum = ChainSum(lambda zk: ggu.at[zk], lambda at: m["gu_slot"].at[at], m["zg_s"], m["zg_r"])

    def farthest(i):
        up = z // 2
        return up * i + (1 - up) * (3 - i)

    def grad_gu(i, carry):
        zk = farthest(i)
        cols = pl.ds(pl.multiple_of(zk * block_rows, 128), block_rows)
        left = n2[:, :, cols].reshape(8 * rows, block_rows)
        ggu[zk] = first_dims(left, dgu[:, cols_a:]).astype(BF16)
        gu_sum.start_one(zk)
        return carry

    lax.fori_loop(0, 2, grad_gu, 0)
    summed.middle()
    lax.fori_loop(2, 4, grad_gu, 0)
    down_sum.second_hop(add)
    summed.finish()

    v = m["mid"][...]
    dv, gain_grad = norm_back(summed.out[...], v, inverse_rms(v), m["g_two"][...])
    m["row_two"][...] = gain_grad
    dmid = cot_v[t_own].astype(F32) + dv
    m["dmid"][...] = dmid
    m["low"][...] = dmid.astype(BF16)
    branch = Gather(m["low"], m["db"], m["gd_s"], m["gd_r"], keep.at[12])
    branch.start()

    got = m["got"]
    quarter_d = rows_b
    summed.sent()
    for i in range(4):
        pl.when(r != i)(lambda i=i: spread(i).wait_send())
    for j in range(0, half_a + 128, 128):
        at = half_a + j
        grad = first_dims(hidden[:, at:at + 128], cot_v[...].reshape(8 * rows, width))
        parts[j // 128] = grad.astype(BF16)
    for i in range(4):
        lo = quarter_d * i
        first, last = lo // rows, (lo + quarter_d - 1) // rows + 1
        span_rows = parts[first:last].reshape((last - first) * rows, width)
        gdo[i, 0:quarter_d] = span_rows[lo - first * rows:lo - first * rows + quarter_d]
    def give(i, lo, n, ss, rs):
        return remote(gdo.at[i, pl.ds(lo, n)], got.at[r, pl.ds(lo, n)], ss.at[i], rs.at[r],
                      device(base, i // 2, i % 2, z, x))

    def give_all(lo, n, ss, rs):
        for i in range(4):
            pl.when(r != i)(lambda i=i: give(i, lo, n, ss, rs).start())
        got[r, lo:lo + n] = gdo[r, lo:lo + n]

    def given(lo, n, ss, rs):
        for i in range(4):
            pl.when(r != i)(lambda i=i: remote(
                gdo.at[i, pl.ds(lo, n)], got.at[i, pl.ds(lo, n)], ss.at[i], rs.at[i],
                to_c).wait_recv())

    def give_sent(lo, n, ss, rs):
        for i in range(4):
            pl.when(r != i)(lambda i=i: give(i, lo, n, ss, rs).wait_send())

    branch.forward()
    give_all(0, quarter_d, m["he_s"], m["he_r"])
    gu_sum.first_hop(add)

    gate_sum.collect(total_in(gga.at[z]))
    down_sum.collect(total_in(got_a.at[z]))
    branch.finish()
    mixed = SeqSum(parts, [m[n] for n in SUM_NAMES])

    def down(k, carry):
        b, e = order(k)
        s = 2 * b + e
        out = jnp.dot(hidden[pl.ds(s * span, span)], wd_v[...], preferred_element_type=F32)
        parts[pl.ds(2 * s, 2)] = out.astype(BF16).reshape(2, rows, width)
        pl.when(k < 2)(lambda: mixed.give(b))
        pl.when(k == 2)(mixed.take_far)
        pl.when(k == 3)(mixed.take_near)
        return carry

    lax.fori_loop(0, 4, down, 0)

    def swap(src, out, ss, rs):
        return remote(src.at[pl.ds(own_rows * (1 - x), own_rows)], out.at[t_own], ss, rs, to_x)

    def keep_own(k, src, out):
        copy = pltpu.make_async_copy(src.at[pl.ds(own_rows * x, own_rows)], out.at[t_own],
                                     keep.at[k])
        copy.start()
        return copy

    def swapped(src, out, ss, rs):
        return remote(src.at[pl.ds(own_rows * x, own_rows)], out.at[2 * r + 1 - x], ss, rs, to_x)

    def pairs(out):
        return lambda i: out.at[pl.ds(2 * i, 2)]

    ga_out, gb_out, qkv_out = m["ga_g"], m["gb_g"], m["qkv_g"]
    ga_swap = swap(gga.at[z], ga_out, m["xs_s"], m["xs_r"])
    ga_swap.start()
    ga_keep = keep_own(14, gga.at[z], ga_out)
    da_keep = loaded(15, got_a.at[z], m["da_g"].at[r])
    ga_share = RepShare(pairs(ga_out), m["ra_s"], m["ra_r"])
    da_share = RepShare(lambda i: m["da_g"].at[i], m["rc_s"], m["rc_r"])


    wo, qkv, dkv = m["wo_v"], qkv_all, kv
    db, dqkv, do_v = m["db"], m["dqkv"], m["do"]
    own_kv = m["own_kv"]
    m["row_head"][...] = jnp.zeros((1, 128), F32)

    down_rest = ChainSum(lambda zk: got.at[zk, pl.ds(0, quarter_d)],
                         lambda at: m["down_slot"].at[at], m["zd_s"], m["zd_r"])

    def start_down():
        given(0, quarter_d, m["he_s"], m["he_r"])
        down_rest.start()

    def share_first():
        ga_keep.wait()
        da_keep.wait()
        swapped(gga.at[z], ga_out, m["xs_s"], m["xs_r"]).wait_recv()
        ga_share.start()
        da_share.start()

    kv_slot = m["kv_slot"]

    def kv_down(zk, s):
        return remote(dkv.at[zk, s], kv_slot.at[zk, s], m["zk_s"].at[zk, s], m["zk_r"].at[zk, s],
                      device(base, y, c, (z + 3) % 4, x))

    def kv_merge(k):
        b, e = order(k)
        s = 2 * b + e

        def one(zk, inner):
            kv_down(zk, s).wait_recv()
            dkv[zk, s] = (dkv[zk, s].astype(F32) + kv_slot[zk, s].astype(F32)).astype(BF16)
            kv_down(zk, s).start()
            return inner

        @pl.when((z == 1) | (z == 2))
        def _():
            lax.fori_loop(0, z, one, 0)

    def attend_back(k, carry):
        b, e = order(k)
        s = 2 * b + e
        grads = db[pl.ds(2 * s, 2)].reshape(span, width)
        d_att = last_dims(grads, wo[...])
        first = d_att[:, 0:128]
        third = jnp.concatenate([jnp.zeros((span, HEAD_DIM), F32), d_att[:, 128:192]], axis=1)
        d_out = [high_half(roll(first, 64)), high_half(first), third]
        att_a = att[s, :, 0:128].astype(F32)
        att_b = att[s, :, 128:192].astype(F32)
        att_b = jnp.concatenate([jnp.zeros((span, HEAD_DIM), F32), att_b], axis=1)
        deltas = []
        for j, o in enumerate((roll(att_a, 64), att_a, att_b)):
            inv = inv_all[s][:, 32 * j:32 * j + 1]
            part_j = (d_out[j].astype(BF16).astype(F32) * inv).astype(BF16)
            do_v[pl.ds(j * span, span)] = part_j
            deltas.append(jnp.sum(part_j.astype(F32) * o, axis=1, keepdims=True))
        delta = jnp.concatenate(deltas, axis=0)
        q_seg[...] = segment_columns(segs, z, s)
        acc[...] = jnp.zeros_like(acc)

        def block(zk, diagonal):
            tile = kv[zk, s]
            q = q_all[s]
            d_out = do_v[...]
            p = exp_scores(q, tile, q_seg[...], segment_row(segs, zk, s), diagonal)
            ds = (p * (last_dims(d_out, tile) - delta)).astype(BF16)
            acc[...] += jnp.dot(ds, tile, preferred_element_type=F32)
            return first_dims(ds, q) + first_dims(p.astype(BF16), d_out)

        def step(zk, inner):
            dkv[zk, s] = block(zk, False).astype(BF16)
            pl.when(z == 3)(lambda: kv_down(zk, s).start())
            return inner

        lax.fori_loop(0, z, step, 0)
        own_kv[s] = block(z, True)
        tiles = split_heads(qkv[s, :, 0:128], qkv[s, :, 128:256])
        back = []
        for j in range(GROUP):
            dy = rotated(low_half(acc[pl.ds(j * span, span)]) * HEAD_DIM ** (-0.5), cos, -sin)
            raw, gain_part = head_back(dy, tiles[j], qg[0:1])
            m["row_head"][...] += gain_part
            back.append(raw)
        dqkv[s, :, 0:128] = (back[0] + roll(back[1], 64)).astype(BF16)
        dqkv[s, :, 128:256] = back[2].astype(BF16)
        pl.when(k >= 1)(lambda: kv_merge(k - 1))
        pl.when(k == 0)(mixed.middle)
        pl.when(k == 1)(lambda: gu_sum.second_hop(add))
        pl.when(k == 2)(mixed.finish)
        pl.when(k == 2)(share_first)
        pl.when(k == 3)(start_down)
        return carry

    lax.fori_loop(0, 4, attend_back, 0)
    kv_merge(3)
    m["mixed"][...] = (m["mid"][...] + mixed.out[...]).astype(BF16)
    mixed.sent()
    free = m["free"]
    for to in (to_c, to_x, to_y):
        pl.semaphore_signal(free, inc=1, device_id=to, device_id_type=MESH)

    for j in range(0, width, 512):
        cols = slice(j, j + 512)
        grad = first_dims(att[...].reshape(8 * rows, Q_COLS),
                          db[:, :, cols].reshape(8 * rows, 512)).astype(BF16)
        for i in range(4):
            gdo[i, quarter_d:quarter_d + quarter_o, cols] = grad[quarter_o * i:quarter_o * (i + 1)]
    give_all(quarter_d, quarter_o, m["hf_s"], m["hf_r"])

    pl.semaphore_wait(free, 3)

    inputs = SeqSum(parts, [m[n] for n in SUM_NAMES])

    def finish_one(k, carry):
        b, e = order(k)
        s = 2 * b + e
        @pl.when(z < 3)
        def _():
            kv_down(z, s).wait_recv()
            own_kv[s] += kv_slot[z, s].astype(F32)

        total = own_kv[s]
        u = split_heads(qkv[s, :, 0:128], qkv[s, :, 128:256])[GROUP]
        dy = rotated(low_half(total), cos, -sin)
        raw, gain_part = head_back(dy, u, kg[0:1])
        m["row_head"][...] += roll(gain_part, 64)
        tile = dqkv[s, :, 128:256].astype(F32)
        dqkv[s, :, 128:256] = (low_half(tile) + roll(raw, 64)).astype(BF16)
        dqkv[s, :, 256:320] = roll(total, 64)[:, 0:HEAD_DIM].astype(BF16)
        out = last_dims(dqkv[s], wq[...]).astype(BF16)
        parts[pl.ds(2 * s, 2)] = out.reshape(2, rows, width)
        pl.when(k < 2)(lambda: inputs.give(b))
        pl.when(k == 2)(inputs.take_far)
        pl.when(k == 3)(inputs.take_near)
        return carry

    lax.fori_loop(0, 4, finish_one, 0)
    gqkv = m["gqkv"]
    qkv_sum = DirectBoth(lambda zk, a: gqkv.at[zk, pl.ds(own_rows * a, own_rows)],
                         lambda zk, a: m["qkv_slot"].at[zk, a], m["zq_s"], m["zq_r"])

    def grad_qkv(i, carry):
        zk = farthest(i)
        cols = pl.ds(pl.multiple_of(zk * block_rows, 128), block_rows)
        left = normed[:, :, cols].reshape(8 * rows, block_rows)
        gqkv[zk] = first_dims(left, dqkv[...].reshape(8 * rows, HEAD_COLS)).astype(BF16)
        qkv_sum.start(zk)
        return carry

    lax.fori_loop(0, 4, grad_qkv, 0)
    inputs.middle()
    given(quarter_d, quarter_o, m["hf_s"], m["hf_r"])
    out_sum = ChainSum(lambda zk: got.at[zk, pl.ds(quarter_d, quarter_o)],
                       lambda at: m["out_slot"].at[at], m["zo_s"], m["zo_r"])
    out_sum.start()


    gu_sum.collect(total_in(ggu.at[z]))
    gb_swap = swap(ggu.at[z], gb_out, m["xg_s"], m["xg_r"])
    gb_swap.start()
    gb_keep = keep_own(14, ggu.at[z], gb_out)
    ga_share.forward()
    da_share.forward()

    inputs.finish()
    v = m["tok"][...].astype(F32)
    dv, gain_grad = norm_back(inputs.out[...], v, inverse_rms(v), m["g_one"][...])
    m["input_grad"][...] = m["dmid"][...] + dv

    def gain_rows_of(k):
        return m["mid"].at[pl.ds(8 * k, 8)]

    gains_own = gain_rows_of(0)
    gains_own[0:1] = gain_grad
    gains_own[1:2] = m["row_two"][...]
    gains_own[2:3, 0:128] = m["row_head"][...]

    def gain_sum(k):
        return remote(gains_own, gain_rows_of(k), m["gm_s"].at[k - 1], m["gm_r"].at[k - 1],
                      mates[k - 1])

    for k in range(1, 8):
        gain_sum(k).start()

    gb_keep.wait()
    swapped(ggu.at[z], gb_out, m["xg_s"], m["xg_r"]).wait_recv()
    gb_share = RepShare(pairs(gb_out), m["rg_s"], m["rg_r"])
    gb_share.start()
    for k in range(1, 8):
        gain_sum(k).wait_recv()
    total = gains_own[...]
    for k in range(1, 8):
        total = total + gain_rows_of(k)[...]
    z_rows = m["z_rows"]
    z_rows[0] = total

    def gain_z(k):
        return remote(z_rows.at[0], z_rows.at[k], m["gz_s"].at[k - 1], m["gz_r"].at[k - 1],
                      device(base, y, c, (z + k) % 4, x))

    for k in range(1, 4):
        gain_z(k).start()

    down_rest.first_hop(add)
    out_sum.first_hop(add)

    qkv_own = m["qkv_slot"].at[z]
    total = gqkv[z, pl.ds(own_rows * x, own_rows)].astype(F32)
    for k in (1, 3, 2):
        qkv_sum.arrive((z + k) % 4, x)
        total = total + m["qkv_slot"][(z + k) % 4, x].astype(F32)
    qkv_own[x] = total.astype(BF16)
    total = jnp.zeros((own_rows, HEAD_COLS), F32)
    for k in (0, 1, 3, 2):
        qkv_sum.arrive((z + k) % 4, 1 - x)
        total = total + m["qkv_slot"][(z + k) % 4, 1 - x].astype(F32)
    qkv_own[1 - x] = total.astype(BF16)
    qkv_keep = loaded(16, qkv_own, pairs(qkv_out)(r))
    qkv_keep.wait()
    qkv_share = RepShare(pairs(qkv_out), m["rq_s"], m["rq_r"])
    qkv_share.start()

    down_rest.second_hop(add)
    out_sum.second_hop(add)
    down_rest.collect(total_in(got.at[z, pl.ds(0, quarter_d)]))
    db_keep = loaded(15, got.at[z, pl.ds(0, quarter_d)], m["db_g"].at[r])
    db_keep.wait()
    db_share = RepShare(lambda i: m["db_g"].at[i], m["rd_s"], m["rd_r"])
    db_share.start()
    out_own = got.at[z, pl.ds(quarter_d, quarter_o)]
    out_sum.collect(total_in(out_own))
    out_keep = loaded(0, out_own, m["out_g"].at[r])
    out_keep.wait()
    out_share = RepShare(lambda i: m["out_g"].at[i], m["re_s"], m["re_r"])
    out_share.start()
    gb_share.forward()
    db_share.forward()
    for k in range(1, 4):
        gain_z(k).wait_recv()
    m["gains_g"][...] = z_rows[0] + z_rows[1] + z_rows[2] + z_rows[3]
    out_share.forward()
    qkv_share.forward()
    shares = (ga_share, da_share, gb_share, db_share, out_share, qkv_share)
    for share in shares:
        share.finish()

    for share in shares:
        share.sent()
    for copy in (ga_swap, gb_swap):
        copy.wait_send()
    for k in range(1, 8):
        gain_sum(k).wait_send()
    for k in range(1, 4):
        gain_z(k).wait_send()
    for flow in (gu_sum, down_rest, qkv_sum, out_sum, inputs):
        flow.sent()
    give_sent(0, quarter_d, m["he_s"], m["he_r"])
    give_sent(quarter_d, quarter_o, m["hf_s"], m["hf_r"])

    def dkv_sent(s, carry):
        for zk in range(3):
            pl.when(z > zk)(lambda zk=zk: kv_down(zk, s).wait_send())
        return carry

    lax.fori_loop(0, 4, dkv_sent, 0)
    for flow in (near, flip, out_q, gate_a, gate_b, down_a, down_b, gate_sum, down_sum):
        flow.sent()
    over.wait_send()
    for k in range(1, 8):
        seg_copy(k).wait_send()
        gain_copy(k).wait_send()
    for k in range(1, 4):
        pl.when(z + k < 4)(lambda k=k: seg_up(k).wait_send())

    def kv_sent(s, carry):
        for d in (1, 2, 3):
            pl.when(z + d < 4)(lambda d=d: kv_copy(d, s).wait_send())
        return carry

    lax.fori_loop(0, 4, kv_sent, 0)
    hand_sent(m["zo"], m["wo_v"], out_sems, quarter_o)
    hand_sent(m["za"], wda, a_sems, rows_a)
    hand_sent(m["zb"], wdb, b_sems, rows_b)


SUM_NAMES = ("r1", "chip", "rx", "ry", "mine", "late", "sum_out", "sum_s", "sum_r")
IN = ("tok", "cot", "seg", "wq", "gains", "wgu", "wd", "wo", "qg", "kg", "cos", "sin")
OUT = ("mixed", "input_grad", "gains_g", "ga_g", "gb_g", "da_g", "db_g", "out_g", "qkv_g",
       "zo", "za", "zb", "gains_all")


def block_call(*args):
    shape = jax.ShapeDtypeStruct
    tok, _, seg, wq, gains, wgu, wd, wo = args[:8]
    rows, width = tok.shape
    span = 2 * rows
    own_rows = wq.shape[1]
    part = wgu.shape[1] // 16
    half_a = part // 256 * 128
    part_b = part - half_a
    cols_a, cols_b = 2 * half_a, 2 * half_a + 128
    quarter_a, quarter_d, quarter_o = half_a // 4, part_b // 4, own_rows // 4
    heads = GROUP * span
    outs = {
        "mixed": shape((rows, width), BF16),
        "input_grad": shape((rows, width), F32),
        "gains_g": shape((8, width), F32),
        "ga_g": shape((8, own_rows, cols_a), BF16),
        "gb_g": shape((8, own_rows, cols_b), BF16),
        "da_g": shape((4, quarter_a, width), BF16),
        "db_g": shape((4, quarter_d, width), BF16),
        "out_g": shape((4, quarter_o, width), BF16),
        "qkv_g": shape((8, own_rows, HEAD_COLS), BF16),
        "zo": shape((4, quarter_o, width), BF16),
        "za": shape((4, quarter_a, width), BF16),
        "zb": shape((4, quarter_d, width), BF16),
        "gains_all": shape((8,) + gains.shape, BF16),
    }
    buffers = {
        "tok_all": ((8, rows, width), BF16), "cot_v": ((8, rows, width), BF16),
        "n2_v": ((8, rows, width), BF16), "db": ((8, rows, width), BF16),
        "part": ((8, rows, width), BF16),
        "segs_v": ((4, 8) + seg.shape, seg.dtype), "gains_v": ((8,) + gains.shape, BF16),
        "wq_v": ((width, HEAD_COLS), BF16), "wo_v": ((Q_COLS, width), BF16),
        "wgu_v": ((width, cols_a + cols_b), BF16), "wd_v": ((2 * half_a + 128, width), BF16),
        "hidden": ((8 * rows, 2 * half_a + 128), BF16),
        "dgu": ((8 * rows, cols_a + cols_b), BF16),
        "qkv_v": ((4, span, 256), F32), "q_v": ((4, heads, 128), BF16),
        "kv_v": ((4, 4, span, 128), BF16), "kv_slot": ((3, 4, span, 128), BF16),
        "own_kv": ((4, span, 128), F32), "inv_v": ((4, span, 128), F32),
        "att_v": ((4, span, Q_COLS), BF16), "acc": ((heads, 128), F32),
        "do": ((heads, 128), BF16), "q_seg": ((span, span), jnp.int32),
        "dqkv": ((4, span, HEAD_COLS), BF16),
        "mid": ((rows, width), F32), "dmid": ((rows, width), F32), "low": ((rows, width), BF16),
        "g_one": ((1, width), F32), "g_two": ((1, width), F32),
        "gga": ((4, 2 * own_rows, cols_a), BF16), "gga_slot": ((5, 2 * own_rows, cols_a), BF16),
        "ggu": ((4, 2 * own_rows, cols_b), BF16), "gu_slot": ((5, 2 * own_rows, cols_b), BF16),
        "got_a": ((4, quarter_a, width), BF16),
        "gda_slot": ((5, quarter_a, width), BF16),
        "gdo": ((4, quarter_d + quarter_o, width), BF16),
        "got": ((4, quarter_d + quarter_o, width), BF16),
        "down_slot": ((5, quarter_d, width), BF16),
        "out_slot": ((5, quarter_o, width), BF16),
        "gqkv": ((4, 2 * own_rows, HEAD_COLS), BF16),
        "qkv_slot": ((4, 2, own_rows, HEAD_COLS), BF16),
        "row_two": ((1, width), F32), "row_head": ((1, 128), F32),
        "z_rows": ((4, 8, width), F32),
    }
    counts = {
        "ga": (8, 8), "gb": (8, 8), "gc": (8, 8), "gd": (8, 8), "sg": (7, 7), "gn": (7, 7),
        "gm": (7, 7), "gz": (3, 3), "wa": (6, 4), "wb": (6, 4), "wo": (6, 4), "wx": (1, 1),
        "xa": (1, 1), "xb": (1, 1), "xs": (1, 1), "xg": (1, 1), "ca": (5, 4), "cb": (5, 4),
        "da": (5, 4), "db": (5, 4), "ys": (4, 5), "yd": (4, 5), "zg": (4, 5), "zd": (4, 5),
        "zo": (4, 5), "zq": ((4, 2), (4, 2)), "zk": ((3, 4), (3, 4)), "kv": ((3, 4), (4, 4)),
        "su": (3, 4), "ha": (4, 4), "hb": (4, 4), "hd": (4, 4), "he": (4, 4), "hf": (4, 4),
        "ho": (4, 4), "ra": (3, 3), "rc": (3, 3), "rd": (3, 3), "re": (3, 3), "rg": (3, 3),
        "rq": (3, 3),
    }
    sem = pltpu.SemaphoreType.DMA
    many = lambda n: sem if n == 1 else sem(n if isinstance(n, tuple) else (n,))
    sems = {"keep": dma(21), "free": pltpu.SemaphoreType.REGULAR}
    for n, (send, recv) in counts.items():
        sems[n + "_s"], sems[n + "_r"] = many(send), many(recv)
    scratch = {n: pltpu.VMEM(*v) for n, v in buffers.items()}
    scratch.update(zip(SUM_NAMES, seq_scratch(width)))
    names = IN + OUT + tuple(scratch) + tuple(sems)
    got = pl.pallas_call(
        functools.partial(block_kernel, names),
        name="block",
        out_shape=tuple(outs[n] for n in OUT),
        in_specs=[ANY if n in ("cot", "wgu", "wd", "wo") else VMEM for n in IN],
        out_specs=tuple(VMEM if n in ("mixed", "input_grad", "gains_g") else ANY for n in OUT),
        scratch_shapes=list(scratch.values()) + list(sems.values()),
        compiler_params=params(0, 63),
    )(*args)
    return dict(zip(OUT, got))


def order_kernel(ga, gb, da, db, out, qkv, gu_o, down_o, out_o, qkv_o):
    which, i = pl.program_id(1), pl.program_id(0)
    half_a = ga.shape[2] // 2
    half_b = (gb.shape[2] - 128) // 2
    main = half_a + half_b
    low = lanes((ga.shape[1], 128)) < HEAD_DIM

    def at(start, n, step=128):
        return pl.ds(pl.multiple_of(start, step), n)

    def columns(w):
        first, second = gb[0, :, 2 * half_b:].astype(F32), gb[1, :, 2 * half_b:].astype(F32)
        if w == 0:
            tile = jnp.where(low, first, roll(second, 64))
        else:
            tile = jnp.where(low, roll(first, 64), second)
        gu_o[:, main:main + 128] = tile
        for k in range(2):
            lo = k * (main + 128)
            gu_o[:, lo:lo + half_a] = ga[k, :, w * half_a:(w + 1) * half_a].astype(F32)
            gu_o[:, lo + half_a:lo + main] = gb[k, :, w * half_b:(w + 1) * half_b].astype(F32)

    @pl.when(which == 0)
    def _():
        columns(0)
        x = lax.axis_index("grp") % 2
        part = down_o.shape[0]
        rows_a, rows_b = da.shape[1], db.shape[1]
        shift = (part - main) * x
        down_o[at(rows_a * i + shift, rows_a, 16)] = da[0].astype(F32)
        start = half_a + rows_b * i + shift
        down_o[at(start, 16, 16)] = db[0, 0:16].astype(F32)
        start = start + 16 - (i // 3) * x * part
        down_o[at(start, rows_b - 16, 16)] = db[0, 16:].astype(F32)

    @pl.when(which == 1)
    def _():
        columns(1)
        out_o[...] = out[0].astype(F32)
        a, b = qkv[0].astype(F32), qkv[1].astype(F32)
        q_cols, kv_cols = HEADS * HEAD_DIM, KV_HEADS * HEAD_DIM
        half = lambda v, w: jnp.where(low, v, w)
        a1, a2, b0, b1 = a[:, 128:256], a[:, 256:], b[:, 0:128], b[:, 128:256]
        qkv_o[:, at(i * 2 * Q_COLS, 128)] = a[:, 0:128]
        qkv_o[:, at(i * 2 * Q_COLS + 128, 128)] = half(a1, roll(b0, 64))
        qkv_o[:, at(i * 2 * Q_COLS + 256, 128)] = half(roll(b0, 64), roll(b1, 64))
        qkv_o[:, at(q_cols + i * 128, 128)] = half(roll(a1, 64), b1)
        qkv_o[:, at(q_cols + kv_cols + i * 128, 128)] = jnp.concatenate([a2, b[:, 256:]], axis=1)


def order_call(ga, gb, da, db, out, qkv):
    shape = jax.ShapeDtypeStruct
    _, own_rows, cols_a = ga.shape
    cols = cols_a + gb.shape[2]
    width = da.shape[2]
    part = 4 * (da.shape[1] + db.shape[1])
    qkv_cols = (HEADS + 2 * KV_HEADS) * HEAD_DIM
    block = lambda v, n: pl.BlockSpec((n,) + v.shape[1:], lambda i, w: (i, 0, 0))
    return pl.pallas_call(
        order_kernel,
        name="final_order",
        grid=(4, 2),
        out_shape=(
            shape((own_rows, 8 * cols), F32), shape((part, width), F32),
            shape((4 * out.shape[1], width), F32), shape((own_rows, qkv_cols), F32)),
        in_specs=[block(ga, 2), block(gb, 2), block(da, 1), block(db, 1), block(out, 1),
                  block(qkv, 2)],
        out_specs=(
            pl.BlockSpec((own_rows, cols), lambda i, w: (0, 4 * w + i)),
            pl.BlockSpec((part, width), lambda i, w: (0, 0)),
            pl.BlockSpec((out.shape[1], width), lambda i, w: (i, 0)),
            pl.BlockSpec((own_rows, qkv_cols), lambda i, w: (0, 0))),
        compiler_params=pltpu.CompilerParams(
            dimension_semantics=("arbitrary", "arbitrary"), vmem_limit_bytes=48 * 2**20),
    )(ga, gb, da, db, out, qkv)


def rope_tables(positions):
    half = HEAD_DIM // 2
    freq = jnp.exp(-jnp.log(THETA) * jnp.arange(half, dtype=F32) * 2.0 / HEAD_DIM)
    angle = positions.astype(F32)[:, None] * freq[None, :]
    cos, sin = jnp.cos(angle), jnp.sin(angle)
    zero = jnp.zeros_like(cos)
    return jnp.concatenate([cos, cos, zero, zero], 1), jnp.concatenate([-sin, sin, zero, zero], 1)


def over_quads(array):
    reps = lax.axis_size("rep")
    if reps == 4:
        return array
    rows = [[j + 4 * q for q in range(reps // 4)] for j in range(4)]
    return lax.psum(array, "rep", axis_index_groups=rows)


def local(tokens, attn_gain, w_qkv, q_gain, k_gain, w_out, ffn_gain, w_gate_up, w_down,
          cotangent, segment_ids):
    rows, width = tokens.shape
    _, y, c, z, x = here()
    r = 2 * y + c
    q_width, kv_width = HEADS * HEAD_DIM, KV_HEADS * HEAD_DIM
    own_rows = w_qkv.shape[0]
    span = 2 * rows
    cut = lax.dynamic_slice_in_dim

    q_pair = cut(w_qkv, 2 * Q_COLS * r, 2 * Q_COLS, 1)
    k_pair = cut(w_qkv, q_width + 2 * HEAD_DIM * r, 2 * HEAD_DIM, 1)
    v_pair = cut(w_qkv, q_width + kv_width + 2 * HEAD_DIM * r, 2 * HEAD_DIM, 1)
    wq = jnp.stack([
        jnp.concatenate([
            q_pair[:, i * Q_COLS:(i + 1) * Q_COLS],
            k_pair[:, i * HEAD_DIM:(i + 1) * HEAD_DIM],
            v_pair[:, i * HEAD_DIM:(i + 1) * HEAD_DIM]], 1)
        for i in range(2)])
    gains = jnp.zeros((16, 256), BF16)
    gains = gains.at[0, :own_rows].set(attn_gain).at[1, :own_rows].set(ffn_gain)
    seg = jnp.broadcast_to(segment_ids[None, :], (8, rows))
    cos, sin = rope_tables(span * z + jnp.arange(span, dtype=jnp.int32))

    def padded(gain):
        return jnp.zeros((8, 128), F32).at[:, :HEAD_DIM].set(gain.astype(F32)[None])

    qg, kg = padded(q_gain), padded(k_gain)
    g = block_call(tokens, cotangent, seg, wq, gains, w_gate_up, w_down, w_out, qg, kg, cos, sin)
    gu, down, out, qkv = order_call(
        *[over_quads(g[n]) for n in ("ga_g", "gb_g", "da_g", "db_g", "out_g", "qkv_g")])
    gains_sum = over_quads(g["gains_g"])
    place = 2 * z + x
    gain_one = cut(gains_sum[0], place * own_rows, own_rows, 0)
    gain_two = cut(gains_sum[1], place * own_rows, own_rows, 0)
    return (g["mixed"], g["input_grad"], gain_one, qkv, gains_sum[2, :HEAD_DIM],
            gains_sum[2, HEAD_DIM:2 * HEAD_DIM], out, gain_two, gu, down)


def solution(mesh):
    rows, split = P(("rep", "grp"), None), P("grp", None)
    return jax.shard_map(
        local,
        mesh=mesh,
        in_specs=(rows, P("grp"), split, P(), P(), split, P("grp"), split, split, rows,
                  P(("rep", "grp"))),
        out_specs=(rows, rows, P("grp"), split, P(), P(), split, P("grp"), split, split),
        check_vma=False,
    )
```

time: 360 us -> 327 us (0.908)
  Pallas kernels: 340 us -> 303 us
    pallas_call x2 -> x1, Pallas kernels: 330 us -> 294 us  [block_call(): pl.pallas_call(functools.partial(block_kernel, names), name='block', out_...]
    unnamed x12 -> x18, local copies, waits for them, and re-layouts: 4.58 us -> 7.72 us
where the time goes in v4:
time: 327 us; the launch traced here: 326 us
  Pallas kernels  303 us (93%)
  local copies, waits for them, and re-layouts  17.4 us (5%)
  other arithmetic  4.25 us (1%)
    pallas_call x1, Pallas kernels, block_call(): pl.pallas_call(functools.partial(block_kernel, names), name='block', out_...  294 us
    pallas_call x1, Pallas kernels, order_call(): pl.pallas_call(order_kernel, name='final_order', grid=(4, 2), out_shape=(...  9.05 us
    unnamed x18, local copies, waits for them, and re-layouts  7.72 us

profile of v4, /device:TPU:0, one launch (start us, length us, event | category | flops | bytes accessed | tf_op | source)
XLA Modules:
  0.0 325.8 jit_solution(17499578725632080172)
XLA Ops:
  0.6 0.6 compare_reduce_fusion
  1.3 0.1 pad.19.clone
  1.4 1.3 broadcast_select_fusion
  2.7 0.7 reshape.138
  3.4 0.7 reshape.139
  4.0 0.6 scatter.27.refs_8_
  4.6 0.6 scatter.29.refs_9_
  5.2 1.2 broadcast_in_dim.2.refs_2_
  6.5 0.2 scatter.25.refs_4_
  6.7 0.0 copy-start.7
  6.7 1.0 constant_dynamic-slice_fusion.1
  7.7 1.1 constant_dynamic-slice_fusion.2
  8.8 0.1 maximum_bitcast_fusion
  8.9 0.8 pad_maximum_fusion.refs_3_
  9.7 0.5 fusion
  10.3 0.8 maximum_maximum_fusion.1
  11.1 0.0 copy-done.7
  11.1 294.4 %block.1 = (bf16[128,1536]{1,0:T(8,128)(2,1)}, f32[128,1536]{1,0:T(8,128)}, f32[8,1536]{1,0:T(8,128)}, bf16[8,192,512]{2,1,0:T(8,128)(2,1)}, bf16[8,192,640]{2,1...) custom-call(bf16[128,1536]{1,0:T(8,128)(2,1)} %refs_0_.1, ...), custom_call_target="tpu_custom_call" | custom-call | tf_op jit(solution)/shard_map/block/pallas_call | solution.py:1511
  305.5 1.3 slice_bitcast_fusion
  306.8 0.9 fusion.1
  307.7 0.6 constant_dynamic-slice_fusion.3
  308.4 0.6 constant_dynamic-slice_fusion.4
  309.0 1.4 copy-done
  310.4 1.3 copy-done.1
  311.7 1.2 copy-done.2
  312.9 1.1 copy-done.3
  314.0 1.1 copy-done.4
  315.1 9.0 %final_order.1 = (f32[192,9216]{1,0:T(8,128)}, f32[576,1536]{1,0:T(8,128)}, f32[192,1536]{1,0:T(8,128)}, f32[192,2560]{1,0:T(8,128)}) custom-call(bf16[8,192,512]{2,1,0:T(8,128)(2,1)S(1)} %copy-done, bf16[8,192,640]{2,1,0:T(8,128)(2,1)} %get-tuple-element.75.gb, bf16[4,64,1536]{2,1,0:T(8,128)(2,1)S(1)} %copy-done.3, bf16[4,80,1536]{2,1,0:T(8,128)(2,1)S(1)} %copy-done.2, ...), custom_call_target="tpu_custom_call" | custom-call | tf_op jit(solution)/shard_map/final_order/pallas_call | solution.py:1581
  324.1 0.0 copy-done.6
  324.1 0.7 copy.25
  324.9 0.0 copy-done.5
  324.9 0.9 copy.26
  (13 shorter events, 0.0 us)
Async XLA Ops:
  6.7 4.4 %copy-start.7 = (bf16[16,256]{1,0:T(8,128)(2,1)}, bf16[16,256]{1,0:T(8,128)(2,1)S(1)}, u32[]{:S(2)}) copy-start(bf16[16,256]{1,0:T(8,128)(2,1)S(1)} %scatter.25.refs_4_) | copy-start | bytes 24580
  309.0 1.4 copy-start
  310.4 1.3 copy-start.1
  311.7 1.2 copy-start.2
  312.9 1.1 copy-start.3
  314.0 1.1 copy-start.4
  315.1 9.1 %copy-start.6 = (bf16[128,1536]{1,0:T(8,128)(2,1)S(1)}, bf16[128,1536]{1,0:T(8,128)(2,1)}, u32[]{:S(2)}) copy-start(bf16[128,1536]{1,0:T(8,128)(2,1)} %get-tuple-element.113) | copy-start | bytes 1179652
  315.1 9.8 %copy-start.5 = (f32[128,1536]{1,0:T(8,128)S(1)}, f32[128,1536]{1,0:T(8,128)}, u32[]{:S(2)}) copy-start(f32[128,1536]{1,0:T(8,128)} %get-tuple-element.114) | copy-start | bytes 2359300

commit v5 on v4

--- a/solution.py
+++ b/solution.py
@@ -56,12 +56,9 @@
     return to_c, to_x, to_y
 
 
-GATHER_SEMS = 8
-
-
 class Gather:
     def __init__(self, src, out, send, recv, local):
-        self.src, self.out, self.send, self.recv, self.local = src, out, send, recv, local
+        self.src, self.out, self.send, self.recv = src, out, send, recv
         _, y, c, _, x = here()
         self.to_c, self.to_x, self.to_y = neighbours()
         slot = lambda a, b, d: 4 * a + 2 * b + d
@@ -70,53 +67,63 @@
         self.at_xc, self.at_yc = slot(y, 1 - c, 1 - x), slot(1 - y, 1 - c, x)
         self.at_xy, self.at_xyc = slot(1 - y, c, 1 - x), slot(1 - y, 1 - c, 1 - x)
         self.half = src.shape[0] // 2
-
-    def part(self, ref, k):
-        return ref.at[pl.ds(k * self.half, self.half)]
-
-    def copy(self, k, src, dst, to):
+        self.keep = pltpu.make_async_copy(src, out.at[self.own], local)
+
+    def part(self, at, k):
+        return self.out.at[at, pl.ds(k * self.half, self.half)]
+
+    def copy(self, k):
+        out, own = self.out, self.out.at[self.own]
+        src, dst, to = (
+            lambda: (self.src, own, self.to_x),
+            lambda: (self.src, own, self.to_y),
+            lambda: (self.src, own, self.to_c),
+            lambda: (self.part(self.at_x, 0),) * 2 + (self.to_y,),
+            lambda: (out.at[self.at_x],) * 2 + (self.to_c,),
+            lambda: (self.part(self.at_y, 1),) * 2 + (self.to_x,),
+            lambda: (out.at[self.at_y],) * 2 + (self.to_c,),
+            lambda: (out.at[self.at_xy],) * 2 + (self.to_c,),
+        )[k]()
         return remote(src, dst, self.send.at[k], self.recv.at[k], to)
 
+    def arrive(self, k):
+        out = self.out
+        ref = (
+            lambda: out.at[self.at_x], lambda: out.at[self.at_y], lambda: out.at[self.at_c],
+            lambda: self.part(self.at_xy, 0), lambda: out.at[self.at_xc],
+            lambda: self.part(self.at_xy, 1), lambda: out.at[self.at_yc],
+            lambda: out.at[self.at_xyc],
+        )[k]()
+        remote(ref, ref, self.send.at[k], self.recv.at[k], self.to_c).wait_recv()
+
     def start(self):
-        out, src = self.out, self.src
-        self.keep = pltpu.make_async_copy(src, out.at[self.own], self.local)
         self.keep.start()
-        self.sent = [
-            self.copy(0, src, out.at[self.own], self.to_x),
-            self.copy(1, src, out.at[self.own], self.to_y),
-            self.copy(2, src, out.at[self.own], self.to_c),
-        ]
-        for copy in self.sent:
-            copy.start()
+        for k in range(3):
+            self.copy(k).start()
 
     def forward(self):
-        out = self.out
-        self.copy(0, self.src, out.at[self.at_x], self.to_x).wait_recv()
-        first = self.part(out.at[self.at_x], 0)
-        self.go(3, first, first, self.to_y)
-        self.go(4, out.at[self.at_x], out.at[self.at_x], self.to_c)
-        self.copy(1, self.src, out.at[self.at_y], self.to_y).wait_recv()
-        second = self.part(out.at[self.at_y], 1)
-        self.go(5, second, second, self.to_x)
-        self.go(6, out.at[self.at_y], out.at[self.at_y], self.to_c)
-
-    def go(self, k, src, dst, to):
-        copy = self.copy(k, src, dst, to)
-        copy.start()
-        self.sent.append(copy)
+        self.arrive(0)
+        self.copy(3).start()
+        self.copy(4).start()
+        self.arrive(1)
+        self.copy(5).start()
+        self.copy(6).start()
+
+    def cross(self):
+        self.arrive(3)
+        self.arrive(5)
+        self.copy(7).start()
 
     def finish(self):
-        out = self.out
-        first = self.part(out.at[self.at_xy], 0)
-        second = self.part(out.at[self.at_xy], 1)
-        self.copy(3, first, first, self.to_y).wait_recv()
-        self.copy(5, second, second, self.to_x).wait_recv()
-        self.go(7, out.at[self.at_xy], out.at[self.at_xy], self.to_c)
-        for k, at in ((2, self.at_c), (4, self.at_xc), (6, self.at_yc), (7, self.at_xyc)):
-            self.copy(k, out.at[at], out.at[at], self.to_c).wait_recv()
-        for copy in self.sent:
-            copy.wait_send()
+        self.cross()
+        for k in (2, 4, 6, 7):
+            self.arrive(k)
         self.keep.wait()
+        self.sent()
+
+    def sent(self):
+        for k in range(8):
+            self.copy(k).wait_send()
 
 
 def dma(n):
@@ -323,17 +330,18 @@
         for to in (0, 1, 2):
             pl.when((self.z == 3) & (zk == to))(lambda to=to: self.copy(to, 2, to).start())
 
-    def first_hop(self, add):
+    def first_hop(self, add, which=(0, 1)):
         @pl.when(self.z == 1)
         def _():
-            for zk, at in ((3, 3), (2, 4)):
+            for i in which:
+                zk, at = ((3, 3), (2, 4))[i]
                 self.arrive(zk)
                 add(self.block(zk), self.slot(zk))
                 self.copy(zk, 2, at).start()
 
         @pl.when(self.z == 2)
         def _():
-            for zk in (0, 1):
+            for zk in which:
                 self.arrive(zk)
                 add(self.block(zk), self.slot(zk))
                 self.copy(zk, 1, zk).start()
@@ -545,6 +553,31 @@
     active = gate * sigma
     d_gate = grad * up * sigma * (1.0 + gate * (1.0 - sigma))
     return ((active * up).astype(BF16), d_gate.astype(BF16), (grad * active).astype(BF16))
+
+
+class Direct:
+    def __init__(self, block, slot, send, recv):
+        self.block, self.slot, self.send, self.recv = block, slot, send, recv
+        self.base, self.y, self.c, self.z, self.x = here()
+
+    def copy(self, zk):
+        return remote(self.block(zk), self.slot(self.z), self.send.at[zk], self.recv.at[self.z],
+                      device(self.base, self.y, self.c, zk, self.x))
+
+    def start(self, zk):
+        pl.when(zk != self.z)(lambda: self.copy(zk).start())
+
+    def take(self):
+        for k in (1, 3, 2):
+            zk = (self.z + k) % 4
+            ref = self.slot(zk)
+            remote(ref, ref, self.send.at[0], self.recv.at[zk],
+                   device(self.base, self.y, self.c, zk, self.x)).wait_recv()
+            yield ref[...].astype(F32)
+
+    def sent(self):
+        for zk in range(4):
+            pl.when(self.z != zk)(lambda zk=zk: self.copy(zk).wait_send())
 
 
 class DirectBoth:
@@ -934,6 +967,9 @@
     cross_a.wait_send()
     cross_b.wait_send()
 
+    down_b.third()
+    gate_b.third()
+
     def feed_first(s, carry):
         at = pl.ds(pl.multiple_of(s * span, span), span)
         gu = jnp.dot(n2_all[pl.ds(2 * s, 2)].reshape(span, width), wgu[:, :cols_a],
@@ -941,11 +977,12 @@
         dh = last_dims(cot_all[pl.ds(2 * s, 2)].reshape(span, width), wd_v[0:half_a])
         hidden[at, 0:half_a], dgu[at, 0:half_a], dgu[at, half_a:cols_a] = swiglu(
             gu[:, :half_a], gu[:, half_a:], dh)
+        out = last_dims(dgu[at, 0:cols_a], wgu[:, :cols_a]).astype(BF16)
+        m["part"][pl.ds(2 * s, 2)] = out.reshape(2, rows, width)
         return carry
 
+    summed.given()
     lax.fori_loop(0, 4, feed_first, 0)
-    down_b.third()
-    gate_b.third()
     down_b.pass_inner()
     gate_b.pass_inner()
     block_rows = 2 * own_rows
@@ -993,7 +1030,7 @@
             spread_from(i), got_a.at[i], m["ha_s"].at[i], m["ha_r"].at[i], to_c).wait_recv())
     down_sum.start()
     gate_sum.second_hop(add)
-    summed.sent()
+    summed.passed()
 
     def total_in(block):
         def total(slots):
@@ -1024,8 +1061,9 @@
         d_gate = grad * up * sigma * (1.0 + gate * (1.0 - sigma))
         dgu[at, cols_a + 2 * half_a:] = (
             d_gate + roll(low_half(grad * active), 64)).astype(BF16)
-        out = last_dims(dgu[at], wgu[...]).astype(BF16)
-        parts[pl.ds(2 * s, 2)] = out.reshape(2, rows, width)
+        out = last_dims(dgu[at, cols_a:], wgu[:, cols_a:])
+        out = out + parts[pl.ds(2 * s, 2)].reshape(span, width).astype(F32)
+        parts[pl.ds(2 * s, 2)] = out.astype(BF16).reshape(2, rows, width)
         pl.when(k < 2)(lambda: summed.give(b))
         pl.when(k == 2)(summed.take_far)
         pl.when(k == 3)(summed.take_near)
@@ -1063,21 +1101,32 @@
     m["low"][...] = dmid.astype(BF16)
     branch = Gather(m["low"], m["db"], m["gd_s"], m["gd_r"], keep.at[12])
     branch.start()
+    gu_sum.first_hop(add, (0,))
 
     got = m["got"]
     quarter_d = rows_b
-    summed.sent()
     for i in range(4):
         pl.when(r != i)(lambda i=i: spread(i).wait_send())
     for j in range(0, half_a + 128, 128):
         at = half_a + j
         grad = first_dims(hidden[:, at:at + 128], cot_v[...].reshape(8 * rows, width))
-        parts[j // 128] = grad.astype(BF16)
-    for i in range(4):
-        lo = quarter_d * i
-        first, last = lo // rows, (lo + quarter_d - 1) // rows + 1
-        span_rows = parts[first:last].reshape((last - first) * rows, width)
-        gdo[i, 0:quarter_d] = span_rows[lo - first * rows:lo - first * rows + quarter_d]
+        grad = grad.astype(BF16)
+        for i in range(4):
+            lo, hi = max(j, quarter_d * i), min(j + 128, quarter_d * (i + 1))
+            if lo < hi:
+                gdo[i, lo - quarter_d * i:hi - quarter_d * i] = grad[lo - j:hi - j]
+
+    summed.sent()
+
+    def down(s, carry):
+        at = pl.ds(pl.multiple_of(s * span, span), span)
+        out = jnp.dot(hidden[at], wd_v[...], preferred_element_type=F32)
+        parts[pl.ds(2 * s, 2)] = out.astype(BF16).reshape(2, rows, width)
+        return carry
+
+    lax.fori_loop(0, 4, down, 0)
+    mixed = SeqSum(parts, [m[n] for n in SUM_NAMES])
+
     def give(i, lo, n, ss, rs):
         return remote(gdo.at[i, pl.ds(lo, n)], got.at[r, pl.ds(lo, n)], ss.at[i], rs.at[r],
                       device(base, i // 2, i % 2, z, x))
@@ -1098,25 +1147,12 @@
             pl.when(r != i)(lambda i=i: give(i, lo, n, ss, rs).wait_send())
 
     branch.forward()
+    branch.arrive(2)
+    branch.keep.wait()
     give_all(0, quarter_d, m["he_s"], m["he_r"])
-    gu_sum.first_hop(add)
-
-    gate_sum.collect(total_in(gga.at[z]))
-    down_sum.collect(total_in(got_a.at[z]))
-    branch.finish()
-    mixed = SeqSum(parts, [m[n] for n in SUM_NAMES])
-
-    def down(k, carry):
-        b, e = order(k)
-        s = 2 * b + e
-        out = jnp.dot(hidden[pl.ds(s * span, span)], wd_v[...], preferred_element_type=F32)
-        parts[pl.ds(2 * s, 2)] = out.astype(BF16).reshape(2, rows, width)
-        pl.when(k < 2)(lambda: mixed.give(b))
-        pl.when(k == 2)(mixed.take_far)
-        pl.when(k == 3)(mixed.take_near)
-        return carry
-
-    lax.fori_loop(0, 4, down, 0)
+    mixed.give(0)
+    mixed.give(1)
+    gu_sum.first_hop(add, (1,))
 
     def swap(src, out, ss, rs):
         return remote(src.at[pl.ds(own_rows * (1 - x), own_rows)], out.at[t_own], ss, rs, to_x)
@@ -1135,9 +1171,8 @@
 
     ga_out, gb_out, qkv_out = m["ga_g"], m["gb_g"], m["qkv_g"]
     ga_swap = swap(gga.at[z], ga_out, m["xs_s"], m["xs_r"])
-    ga_swap.start()
-    ga_keep = keep_own(14, gga.at[z], ga_out)
-    da_keep = loaded(15, got_a.at[z], m["da_g"].at[r])
+    ga_keep = local_copy(14, gga.at[z, pl.ds(own_rows * x, own_rows)], ga_out.at[t_own])
+    da_keep = local_copy(15, got_a.at[z], m["da_g"].at[r])
     ga_share = RepShare(pairs(ga_out), m["ra_s"], m["ra_r"])
     da_share = RepShare(lambda i: m["da_g"].at[i], m["rc_s"], m["rc_r"])
 
@@ -1150,9 +1185,11 @@
     down_rest = ChainSum(lambda zk: got.at[zk, pl.ds(0, quarter_d)],
                          lambda at: m["down_slot"].at[at], m["zd_s"], m["zd_r"])
 
-    def start_down():
-        given(0, quarter_d, m["he_s"], m["he_r"])
-        down_rest.start()
+    def swap_first():
+        gate_sum.collect(total_in(gga.at[z]))
+        down_sum.collect(total_in(got_a.at[z]))
+        for copy in (ga_swap, ga_keep, da_keep):
+            copy.start()
 
     def share_first():
         ga_keep.wait()
@@ -1161,6 +1198,9 @@
         ga_share.start()
         da_share.start()
 
+    def order_back(k):
+        return (y + k // 2) % 2, (c + 1 + k) % 2
+
     kv_slot = m["kv_slot"]
 
     def kv_down(zk, s):
@@ -1168,7 +1208,7 @@
                       device(base, y, c, (z + 3) % 4, x))
 
     def kv_merge(k):
-        b, e = order(k)
+        b, e = order_back(k)
         s = 2 * b + e
 
         def one(zk, inner):
@@ -1182,7 +1222,10 @@
             lax.fori_loop(0, z, one, 0)
 
     def attend_back(k, carry):
-        b, e = order(k)
+        pl.when(k == 0)(lambda: branch.arrive(4))
+        pl.when(k == 1)(branch.cross)
+        pl.when(k == 2)(lambda: [branch.arrive(6), branch.arrive(7)] and None)
+        b, e = order_back(k)
         s = 2 * b + e
         grads = db[pl.ds(2 * s, 2)].reshape(span, width)
         d_att = last_dims(grads, wo[...])
@@ -1228,15 +1271,19 @@
         dqkv[s, :, 0:128] = (back[0] + roll(back[1], 64)).astype(BF16)
         dqkv[s, :, 128:256] = back[2].astype(BF16)
         pl.when(k >= 1)(lambda: kv_merge(k - 1))
-        pl.when(k == 0)(mixed.middle)
-        pl.when(k == 1)(lambda: gu_sum.second_hop(add))
-        pl.when(k == 2)(mixed.finish)
-        pl.when(k == 2)(share_first)
-        pl.when(k == 3)(start_down)
+        pl.when(k == 0)(lambda: gu_sum.second_hop(add))
+        pl.when(k == 0)(mixed.take_far)
+        pl.when(k == 0)(mixed.take_near)
+        pl.when(k == 1)(swap_first)
+        pl.when(k == 2)(mixed.middle)
+        pl.when(k == 3)(share_first)
+        pl.when(k == 3)(lambda: given(0, quarter_d, m["he_s"], m["he_r"]))
         return carry
 
     lax.fori_loop(0, 4, attend_back, 0)
     kv_merge(3)
+    down_rest.start()
+    mixed.finish()
     m["mixed"][...] = (m["mid"][...] + mixed.out[...]).astype(BF16)
     mixed.sent()
     free = m["free"]
@@ -1250,13 +1297,17 @@
         for i in range(4):
             gdo[i, quarter_d:quarter_d + quarter_o, cols] = grad[quarter_o * i:quarter_o * (i + 1)]
     give_all(quarter_d, quarter_o, m["hf_s"], m["hf_r"])
+    gu_sum.collect(total_in(ggu.at[z]))
+    gb_swap = swap(ggu.at[z], gb_out, m["xg_s"], m["xg_r"])
+    gb_swap.start()
+    gb_keep = keep_own(14, ggu.at[z], gb_out)
 
     pl.semaphore_wait(free, 3)
 
     inputs = SeqSum(parts, [m[n] for n in SUM_NAMES])
 
     def finish_one(k, carry):
-        b, e = order(k)
+        b, e = (y + (k + 1) // 2) % 2, (c + 1 + k // 2) % 2
         s = 2 * b + e
         @pl.when(z < 3)
         def _():
@@ -1279,6 +1330,7 @@
         return carry
 
     lax.fori_loop(0, 4, finish_one, 0)
+    down_rest.first_hop(add)
     gqkv = m["gqkv"]
     qkv_sum = DirectBoth(lambda zk, a: gqkv.at[zk, pl.ds(own_rows * a, own_rows)],
                          lambda zk, a: m["qkv_slot"].at[zk, a], m["zq_s"], m["zq_r"])
@@ -1293,16 +1345,16 @@
 
     lax.fori_loop(0, 4, grad_qkv, 0)
     inputs.middle()
+    down_rest.second_hop(add)
     given(quarter_d, quarter_o, m["hf_s"], m["hf_r"])
-    out_sum = ChainSum(lambda zk: got.at[zk, pl.ds(quarter_d, quarter_o)],
-                       lambda at: m["out_slot"].at[at], m["zo_s"], m["zo_r"])
-    out_sum.start()
-
-
-    gu_sum.collect(total_in(ggu.at[z]))
-    gb_swap = swap(ggu.at[z], gb_out, m["xg_s"], m["xg_r"])
-    gb_swap.start()
-    gb_keep = keep_own(14, ggu.at[z], gb_out)
+    out_sum = Direct(lambda zk: got.at[zk, pl.ds(quarter_d, quarter_o)],
+                     lambda zk: m["out_slot"].at[zk], m["zo_s"], m["zo_r"])
+
+    def start_out(i, carry):
+        out_sum.start(farthest(i))
+        return carry
+
+    lax.fori_loop(0, 4, start_out, 0)
     ga_share.forward()
     da_share.forward()
 
@@ -1325,11 +1377,13 @@
 
     for k in range(1, 8):
         gain_sum(k).start()
-
     gb_keep.wait()
     swapped(ggu.at[z], gb_out, m["xg_s"], m["xg_r"]).wait_recv()
     gb_share = RepShare(pairs(gb_out), m["rg_s"], m["rg_r"])
     gb_share.start()
+
+    down_rest.collect(total_in(got.at[z, pl.ds(0, quarter_d)]))
+    db_keep = loaded(15, got.at[z, pl.ds(0, quarter_d)], m["db_g"].at[r])
     for k in range(1, 8):
         gain_sum(k).wait_recv()
     total = gains_own[...]
@@ -1344,9 +1398,10 @@
 
     for k in range(1, 4):
         gain_z(k).start()
-
-    down_rest.first_hop(add)
-    out_sum.first_hop(add)
+    db_keep.wait()
+    db_share = RepShare(lambda i: m["db_g"].at[i], m["rd_s"], m["rd_r"])
+    db_share.start()
+    gb_share.forward()
 
     qkv_own = m["qkv_slot"].at[z]
     total = gqkv[z, pl.ds(own_rows * x, own_rows)].astype(F32)
@@ -1364,26 +1419,21 @@
     qkv_share = RepShare(pairs(qkv_out), m["rq_s"], m["rq_r"])
     qkv_share.start()
 
-    down_rest.second_hop(add)
-    out_sum.second_hop(add)
-    down_rest.collect(total_in(got.at[z, pl.ds(0, quarter_d)]))
-    db_keep = loaded(15, got.at[z, pl.ds(0, quarter_d)], m["db_g"].at[r])
-    db_keep.wait()
-    db_share = RepShare(lambda i: m["db_g"].at[i], m["rd_s"], m["rd_r"])
-    db_share.start()
     out_own = got.at[z, pl.ds(quarter_d, quarter_o)]
-    out_sum.collect(total_in(out_own))
+    total = out_own[...].astype(F32)
+    for term in out_sum.take():
+        total = total + term
+    out_own[...] = total.astype(BF16)
     out_keep = loaded(0, out_own, m["out_g"].at[r])
     out_keep.wait()
     out_share = RepShare(lambda i: m["out_g"].at[i], m["re_s"], m["re_r"])
     out_share.start()
-    gb_share.forward()
     db_share.forward()
     for k in range(1, 4):
         gain_z(k).wait_recv()
     m["gains_g"][...] = z_rows[0] + z_rows[1] + z_rows[2] + z_rows[3]
+    qkv_share.forward()
     out_share.forward()
-    qkv_share.forward()
     shares = (ga_share, da_share, gb_share, db_share, out_share, qkv_share)
     for share in shares:
         share.finish()
@@ -1396,7 +1446,7 @@
         gain_sum(k).wait_send()
     for k in range(1, 4):
         gain_z(k).wait_send()
-    for flow in (gu_sum, down_rest, qkv_sum, out_sum, inputs):
+    for flow in (branch, gu_sum, down_rest, qkv_sum, out_sum, inputs):
         flow.sent()
     give_sent(0, quarter_d, m["he_s"], m["he_r"])
     give_sent(quarter_d, quarter_o, m["hf_s"], m["hf_r"])
@@ -1484,7 +1534,7 @@
         "gdo": ((4, quarter_d + quarter_o, width), BF16),
         "got": ((4, quarter_d + quarter_o, width), BF16),
         "down_slot": ((5, quarter_d, width), BF16),
-        "out_slot": ((5, quarter_o, width), BF16),
+        "out_slot": ((4, quarter_o, width), BF16),
         "gqkv": ((4, 2 * own_rows, HEAD_COLS), BF16),
         "qkv_slot": ((4, 2, own_rows, HEAD_COLS), BF16),
         "row_two": ((1, width), F32), "row_head": ((1, 128), F32),
@@ -1495,7 +1545,7 @@
         "gm": (7, 7), "gz": (3, 3), "wa": (6, 4), "wb": (6, 4), "wo": (6, 4), "wx": (1, 1),
         "xa": (1, 1), "xb": (1, 1), "xs": (1, 1), "xg": (1, 1), "ca": (5, 4), "cb": (5, 4),
         "da": (5, 4), "db": (5, 4), "ys": (4, 5), "yd": (4, 5), "zg": (4, 5), "zd": (4, 5),
-        "zo": (4, 5), "zq": ((4, 2), (4, 2)), "zk": ((3, 4), (3, 4)), "kv": ((3, 4), (4, 4)),
+        "zo": (4, 4), "zq": ((4, 2), (4, 2)), "zk": ((3, 4), (3, 4)), "kv": ((3, 4), (4, 4)),
         "su": (3, 4), "ha": (4, 4), "hb": (4, 4), "hd": (4, 4), "he": (4, 4), "hf": (4, 4),
         "ho": (4, 4), "ra": (3, 3), "rc": (3, 3), "rd": (3, 3), "re": (3, 3), "rg": (3, 3),
         "rq": (3, 3),

time: 327 us -> 313 us (0.957)
  Pallas kernels: 303 us -> 288 us
    pallas_call x1, Pallas kernels: 294 us -> 279 us  [block_call(): pl.pallas_call(functools.partial(block_kernel, names), name='block', out_...]
where the time goes in v5:
time: 313 us; the launch traced here: 310 us
  Pallas kernels  288 us (92%)
  local copies, waits for them, and re-layouts  17.4 us (6%)
  other arithmetic  4.25 us (1%)
    pallas_call x1, Pallas kernels, block_call(): pl.pallas_call(functools.partial(block_kernel, names), name='block', out_...  279 us
    pallas_call x1, Pallas kernels, order_call(): pl.pallas_call(order_kernel, name='final_order', grid=(4, 2), out_shape=(...  9.05 us
    unnamed x18, local copies, waits for them, and re-layouts  7.72 us

profile of v5, /device:TPU:0, one launch (start us, length us, event | category | flops | bytes accessed | tf_op | source)
XLA Modules:
  0.0 309.9 jit_solution(15399043510842710145)
XLA Ops:
  0.6 0.6 compare_reduce_fusion
  1.3 0.1 pad.19.clone
  1.4 1.3 broadcast_select_fusion
  2.7 0.7 reshape.138
  3.4 0.7 reshape.139
  4.0 0.6 scatter.27.refs_8_
  4.6 0.6 scatter.29.refs_9_
  5.2 1.2 broadcast_in_dim.2.refs_2_
  6.5 0.2 scatter.25.refs_4_
  6.7 0.0 copy-start.7
  6.7 1.0 constant_dynamic-slice_fusion.1
  7.7 1.1 constant_dynamic-slice_fusion.2
  8.8 0.1 maximum_bitcast_fusion
  8.9 0.8 pad_maximum_fusion.refs_3_
  9.7 0.5 fusion
  10.3 0.8 maximum_maximum_fusion.1
  11.1 0.0 copy-done.7
  11.1 278.6 %block.1 = (bf16[128,1536]{1,0:T(8,128)(2,1)}, f32[128,1536]{1,0:T(8,128)}, f32[8,1536]{1,0:T(8,128)}, bf16[8,192,512]{2,1,0:T(8,128)(2,1)}, bf16[8,192,640]{2,1...) custom-call(bf16[128,1536]{1,0:T(8,128)(2,1)} %refs_0_.1, ...), custom_call_target="tpu_custom_call" | custom-call | tf_op jit(solution)/shard_map/block/pallas_call | solution.py:1561
  289.7 1.3 slice_bitcast_fusion
  291.0 0.9 fusion.1
  291.9 0.6 constant_dynamic-slice_fusion.3
  292.5 0.6 constant_dynamic-slice_fusion.4
  293.2 1.4 copy-done
  294.6 1.3 copy-done.1
  295.8 1.2 copy-done.2
  297.0 1.1 copy-done.3
  298.2 1.1 copy-done.4
  299.2 9.0 %final_order.1 = (f32[192,9216]{1,0:T(8,128)}, f32[576,1536]{1,0:T(8,128)}, f32[192,1536]{1,0:T(8,128)}, f32[192,2560]{1,0:T(8,128)}) custom-call(bf16[8,192,512]{2,1,0:T(8,128)(2,1)S(1)} %copy-done, bf16[8,192,640]{2,1,0:T(8,128)(2,1)} %get-tuple-element.75.gb, bf16[4,64,1536]{2,1,0:T(8,128)(2,1)S(1)} %copy-done.3, bf16[4,80,1536]{2,1,0:T(8,128)(2,1)S(1)} %copy-done.2, ...), custom_call_target="tpu_custom_call" | custom-call | tf_op jit(solution)/shard_map/final_order/pallas_call | solution.py:1631
  308.3 0.0 copy-done.6
  308.3 0.7 copy.25
  309.0 0.0 copy-done.5
  309.0 0.9 copy.26
  (13 shorter events, 0.0 us)
Async XLA Ops:
  6.7 4.4 %copy-start.7 = (bf16[16,256]{1,0:T(8,128)(2,1)}, bf16[16,256]{1,0:T(8,128)(2,1)S(1)}, u32[]{:S(2)}) copy-start(bf16[16,256]{1,0:T(8,128)(2,1)S(1)} %scatter.25.refs_4_) | copy-start | bytes 24580
  293.2 1.4 copy-start
  294.6 1.3 copy-start.1
  295.8 1.2 copy-start.2
  297.0 1.1 copy-start.3
  298.2 1.1 copy-start.4
  299.2 9.1 %copy-start.6 = (bf16[128,1536]{1,0:T(8,128)(2,1)S(1)}, bf16[128,1536]{1,0:T(8,128)(2,1)}, u32[]{:S(2)}) copy-start(bf16[128,1536]{1,0:T(8,128)(2,1)} %get-tuple-element.113) | copy-start | bytes 1179652
  299.2 9.8 %copy-start.5 = (f32[128,1536]{1,0:T(8,128)S(1)}, f32[128,1536]{1,0:T(8,128)}, u32[]{:S(2)}) copy-start(f32[128,1536]{1,0:T(8,128)} %get-tuple-element.114) | copy-start | bytes 2359300

commit v6 on v5

--- a/solution.py
+++ b/solution.py
@@ -645,10 +645,36 @@
     base, y, c, z, x = here()
     r = 2 * y + c
     to_c, to_x, to_y = neighbours()
+    q_cols, kv_cols = HEADS * HEAD_DIM, KV_HEADS * HEAD_DIM
+    raw_q = [
+        pltpu.make_async_copy(m["wqkv"].at[:, pl.ds(first + n * r, n)],
+                              m["wq_raw"].at[:, pl.ds(to, n)], m["keep"].at[k])
+        for k, (first, to, n) in enumerate((
+            (0, 0, 2 * Q_COLS), (q_cols, 2 * Q_COLS, 2 * HEAD_DIM),
+            (q_cols + kv_cols, 2 * Q_COLS + 2 * HEAD_DIM, 2 * HEAD_DIM)))]
+    for copy in raw_q:
+        copy.start()
+    small = m["small"][...].astype(F32)
+    m["seg"][...] = jnp.broadcast_to(small[:, 512:640], (8, 128)).astype(jnp.int32)
+    m["gains"][...] = jnp.concatenate(
+        [small[:, 0:256], small[:, 256:512], jnp.zeros((14, 256), F32)], axis=0).astype(BF16)
+    qg, kg = low_half(roll(small[:, 128:256], 64)), low_half(roll(small[:, 384:512], 64))
     greet(layer_mates() + z_mates())
+    for copy in raw_q:
+        copy.wait()
+    tiles = [m["wq_raw"][:, 128 * i:128 * (i + 1)].astype(F32) for i in range(5)]
+    low_lanes = lanes(tiles[0].shape) < HEAD_DIM
+    half_of = lambda v, w: jnp.where(low_lanes, v, w).astype(BF16)
+    q0, q1, q2, k_tile, v_tile = tiles
+    m["wq"][0, :, 0:128] = q0.astype(BF16)
+    m["wq"][0, :, 128:256] = half_of(q1, roll(k_tile, 64))
+    m["wq"][0, :, 256:] = v_tile[:, 0:HEAD_DIM].astype(BF16)
+    m["wq"][1, :, 0:128] = half_of(roll(q1, 64), roll(q2, 64))
+    m["wq"][1, :, 128:256] = half_of(roll(q2, 64), k_tile)
+    m["wq"][1, :, 256:] = roll(v_tile, 64)[:, 0:HEAD_DIM].astype(BF16)
     rows, width = m["tok"].shape
     quarter_o = m["wo"].shape[0] // 4
-    own_rows = m["wq"].shape[1]
+    own_rows = m["wqkv"].shape[0]
     half_cols = m["wgu"].shape[1] // 2
     piece = half_cols // 4
     part = piece // 2
@@ -806,7 +832,7 @@
     m["g_one"][...], m["g_two"][...] = gain_rows
     kv = m["kv_v"]
     q_all, qkv_all = m["q_v"], m["qkv_v"]
-    qg, kg, cos, sin = m["qg"][...], m["kg"][...], m["cos"][...], m["sin"][...]
+    cos, sin = low_half(m["rope"][...]), low_half(roll(m["rope"][...], 64))
     span = 2 * rows
 
     def order(k):
@@ -830,10 +856,10 @@
         heads = split_heads(qkv[:, 0:128], qkv[:, 128:256])
         for j in range(GROUP):
             u = heads[j]
-            u = rotated(u * head_inverse(u) * qg[0:1], cos, sin) * HEAD_DIM ** (-0.5)
+            u = rotated(u * head_inverse(u) * qg, cos, sin) * HEAD_DIM ** (-0.5)
             q_all[s, pl.ds(j * span, span)] = u.astype(BF16)
         u = heads[GROUP]
-        u = rotated(u * head_inverse(u) * kg[0:1], cos, sin)
+        u = rotated(u * head_inverse(u) * kg, cos, sin)
         v = jnp.concatenate([jnp.zeros((span, HEAD_DIM), F32), qkv[:, 256:320]], axis=1)
         kv[z, s] = (u + v).astype(BF16)
         for d in (3, 2, 1):
@@ -1265,7 +1291,7 @@
         back = []
         for j in range(GROUP):
             dy = rotated(low_half(acc[pl.ds(j * span, span)]) * HEAD_DIM ** (-0.5), cos, -sin)
-            raw, gain_part = head_back(dy, tiles[j], qg[0:1])
+            raw, gain_part = head_back(dy, tiles[j], qg)
             m["row_head"][...] += gain_part
             back.append(raw)
         dqkv[s, :, 0:128] = (back[0] + roll(back[1], 64)).astype(BF16)
@@ -1284,7 +1310,9 @@
     kv_merge(3)
     down_rest.start()
     mixed.finish()
-    m["mixed"][...] = (m["mid"][...] + mixed.out[...]).astype(BF16)
+    branch.sent()
+    m["low"][...] = (m["mid"][...] + mixed.out[...]).astype(BF16)
+    mixed_out = loaded(17, m["low"], m["mixed"])
     mixed.sent()
     free = m["free"]
     for to in (to_c, to_x, to_y):
@@ -1317,7 +1345,7 @@
         total = own_kv[s]
         u = split_heads(qkv[s, :, 0:128], qkv[s, :, 128:256])[GROUP]
         dy = rotated(low_half(total), cos, -sin)
-        raw, gain_part = head_back(dy, u, kg[0:1])
+        raw, gain_part = head_back(dy, u, kg)
         m["row_head"][...] += roll(gain_part, 64)
         tile = dqkv[s, :, 128:256].astype(F32)
         dqkv[s, :, 128:256] = (low_half(tile) + roll(raw, 64)).astype(BF16)
@@ -1361,7 +1389,8 @@
     inputs.finish()
     v = m["tok"][...].astype(F32)
     dv, gain_grad = norm_back(inputs.out[...], v, inverse_rms(v), m["g_one"][...])
-    m["input_grad"][...] = m["dmid"][...] + dv
+    m["dmid"][...] += dv
+    grad_out = loaded(18, m["dmid"], m["input_grad"])
 
     def gain_rows_of(k):
         return m["mid"].at[pl.ds(8 * k, 8)]
@@ -1446,7 +1475,9 @@
         gain_sum(k).wait_send()
     for k in range(1, 4):
         gain_z(k).wait_send()
-    for flow in (branch, gu_sum, down_rest, qkv_sum, out_sum, inputs):
+    mixed_out.wait()
+    grad_out.wait()
+    for flow in (gu_sum, down_rest, qkv_sum, out_sum, inputs):
         flow.sent()
     give_sent(0, quarter_d, m["he_s"], m["he_r"])
     give_sent(quarter_d, quarter_o, m["hf_s"], m["hf_r"])
@@ -1478,17 +1509,18 @@
 
 
 SUM_NAMES = ("r1", "chip", "rx", "ry", "mine", "late", "sum_out", "sum_s", "sum_r")
-IN = ("tok", "cot", "seg", "wq", "gains", "wgu", "wd", "wo", "qg", "kg", "cos", "sin")
+IN = ("tok", "cot", "small", "wqkv", "wgu", "wd", "wo", "rope")
 OUT = ("mixed", "input_grad", "gains_g", "ga_g", "gb_g", "da_g", "db_g", "out_g", "qkv_g",
        "zo", "za", "zb", "gains_all")
 
 
 def block_call(*args):
     shape = jax.ShapeDtypeStruct
-    tok, _, seg, wq, gains, wgu, wd, wo = args[:8]
+    tok, _, _, wqkv, wgu, wd, wo = args[:7]
     rows, width = tok.shape
     span = 2 * rows
-    own_rows = wq.shape[1]
+    own_rows = wqkv.shape[0]
+    seg, gains = shape((8, rows), jnp.int32), shape((16, 256), BF16)
     part = wgu.shape[1] // 16
     half_a = part // 256 * 128
     part_b = part - half_a
@@ -1514,6 +1546,8 @@
         "tok_all": ((8, rows, width), BF16), "cot_v": ((8, rows, width), BF16),
         "n2_v": ((8, rows, width), BF16), "db": ((8, rows, width), BF16),
         "part": ((8, rows, width), BF16),
+        "seg": (seg.shape, seg.dtype), "gains": (gains.shape, BF16),
+        "wq": ((2, own_rows, HEAD_COLS), BF16), "wq_raw": ((own_rows, 640), BF16),
         "segs_v": ((4, 8) + seg.shape, seg.dtype), "gains_v": ((8,) + gains.shape, BF16),
         "wq_v": ((width, HEAD_COLS), BF16), "wo_v": ((Q_COLS, width), BF16),
         "wgu_v": ((width, cols_a + cols_b), BF16), "wd_v": ((2 * half_a + 128, width), BF16),
@@ -1562,98 +1596,158 @@
         functools.partial(block_kernel, names),
         name="block",
         out_shape=tuple(outs[n] for n in OUT),
-        in_specs=[ANY if n in ("cot", "wgu", "wd", "wo") else VMEM for n in IN],
-        out_specs=tuple(VMEM if n in ("mixed", "input_grad", "gains_g") else ANY for n in OUT),
+        in_specs=[ANY if n in ("cot", "wqkv", "wgu", "wd", "wo") else VMEM for n in IN],
+        out_specs=tuple(VMEM if n == "gains_g" else ANY for n in OUT),
         scratch_shapes=list(scratch.values()) + list(sems.values()),
         compiler_params=params(0, 63),
     )(*args)
     return dict(zip(OUT, got))
 
 
-def order_kernel(ga, gb, da, db, out, qkv, gu_o, down_o, out_o, qkv_o):
-    which, i = pl.program_id(1), pl.program_id(0)
-    half_a = ga.shape[2] // 2
-    half_b = (gb.shape[2] - 128) // 2
+def order_kernel(names, *refs):
+    m = dict(zip(names, refs))
+    half_a = m["ga"].shape[2] // 2
+    half_b = (m["gb"].shape[2] - 128) // 2
     main = half_a + half_b
-    low = lanes((ga.shape[1], 128)) < HEAD_DIM
-
-    def at(start, n, step=128):
-        return pl.ds(pl.multiple_of(start, step), n)
-
-    def columns(w):
-        first, second = gb[0, :, 2 * half_b:].astype(F32), gb[1, :, 2 * half_b:].astype(F32)
-        if w == 0:
-            tile = jnp.where(low, first, roll(second, 64))
-        else:
-            tile = jnp.where(low, roll(first, 64), second)
-        gu_o[:, main:main + 128] = tile
-        for k in range(2):
-            lo = k * (main + 128)
-            gu_o[:, lo:lo + half_a] = ga[k, :, w * half_a:(w + 1) * half_a].astype(F32)
-            gu_o[:, lo + half_a:lo + main] = gb[k, :, w * half_b:(w + 1) * half_b].astype(F32)
-
-    @pl.when(which == 0)
-    def _():
-        columns(0)
-        x = lax.axis_index("grp") % 2
-        part = down_o.shape[0]
-        rows_a, rows_b = da.shape[1], db.shape[1]
-        shift = (part - main) * x
-        down_o[at(rows_a * i + shift, rows_a, 16)] = da[0].astype(F32)
+    cols = 2 * main + 128
+    own_rows = m["ga"].shape[1]
+    low = lanes((own_rows, 128)) < HEAD_DIM
+    x = lax.axis_index("grp") % 2
+
+    def fetch(k, src, dst):
+        copy = pltpu.make_async_copy(src, dst, m["load"].at[k])
+        copy.start()
+        return copy
+
+    def store(k, src, dst):
+        copy = pltpu.make_async_copy(src, dst, m["save"].at[k])
+        copy.start()
+        return copy
+
+    ga, gb = m["ga_v"], m["gb_v"]
+    pair = lambda i: pl.ds(2 * i, 2)
+    wide = [(fetch(2 * i, m["ga"].at[pair(i)], ga.at[pair(i)]),
+             fetch(2 * i + 1, m["gb"].at[pair(i)], gb.at[pair(i)])) for i in range(4)]
+    rest = {n: fetch(8 + k, m[n], m[n + "_v"])
+            for k, n in enumerate(("db", "qkv", "da", "out", "ig", "mixed"))}
+    saved = []
+    for i in range(4):
+        for copy in wide[i]:
+            copy.wait()
+        first, second = ga.at[2 * i], ga.at[2 * i + 1]
+        tiles = [gb[2 * i + k, :, 2 * half_b:].astype(F32) for k in range(2)]
+        for w in range(2):
+            to = m["gu_v"].at[4 * w + i]
+            for k in range(2):
+                lo = k * (main + 128)
+                to[:, lo:lo + half_a] = ga[2 * i + k, :, w * half_a:(w + 1) * half_a].astype(F32)
+                to[:, lo + half_a:lo + main] = (
+                    gb[2 * i + k, :, w * half_b:(w + 1) * half_b].astype(F32))
+            if w == 0:
+                to[:, main:main + 128] = jnp.where(low, tiles[0], roll(tiles[1], 64))
+            else:
+                to[:, main:main + 128] = jnp.where(low, roll(tiles[0], 64), tiles[1])
+            saved.append(store(
+                4 * w + i, to, m["gu_o"].at[:, pl.ds((4 * w + i) * cols, cols)]))
+
+    rest["da"].wait()
+    rest["db"].wait()
+    da, db, down = m["da_v"], m["db_v"], m["down_v"]
+    part = down.shape[0]
+    rows_a, rows_b = da.shape[1], db.shape[1]
+    shift = (part - main) * x
+
+    def at(start, n):
+        return pl.ds(pl.multiple_of(start, 16), n)
+
+    for i in range(4):
+        down[at(rows_a * i + shift, rows_a)] = da[i].astype(F32)
         start = half_a + rows_b * i + shift
-        down_o[at(start, 16, 16)] = db[0, 0:16].astype(F32)
-        start = start + 16 - (i // 3) * x * part
-        down_o[at(start, rows_b - 16, 16)] = db[0, 16:].astype(F32)
-
-    @pl.when(which == 1)
-    def _():
-        columns(1)
-        out_o[...] = out[0].astype(F32)
-        a, b = qkv[0].astype(F32), qkv[1].astype(F32)
-        q_cols, kv_cols = HEADS * HEAD_DIM, KV_HEADS * HEAD_DIM
-        half = lambda v, w: jnp.where(low, v, w)
+        down[at(start, 16)] = db[i, 0:16].astype(F32)
+        down[at(start + 16 - (i // 3) * x * part, rows_b - 16)] = db[i, 16:].astype(F32)
+    saved.append(store(8, down, m["down_o"]))
+    rest["qkv"].wait()
+    qkv_v, qkv_f = m["qkv_v"], m["qkv_f"]
+    q_cols, kv_cols = HEADS * HEAD_DIM, KV_HEADS * HEAD_DIM
+    half = lambda v, w: jnp.where(low, v, w)
+    for i in range(4):
+        a, b = qkv_v[2 * i].astype(F32), qkv_v[2 * i + 1].astype(F32)
         a1, a2, b0, b1 = a[:, 128:256], a[:, 256:], b[:, 0:128], b[:, 128:256]
-        qkv_o[:, at(i * 2 * Q_COLS, 128)] = a[:, 0:128]
-        qkv_o[:, at(i * 2 * Q_COLS + 128, 128)] = half(a1, roll(b0, 64))
-        qkv_o[:, at(i * 2 * Q_COLS + 256, 128)] = half(roll(b0, 64), roll(b1, 64))
-        qkv_o[:, at(q_cols + i * 128, 128)] = half(roll(a1, 64), b1)
-        qkv_o[:, at(q_cols + kv_cols + i * 128, 128)] = jnp.concatenate([a2, b[:, 256:]], axis=1)
-
-
-def order_call(ga, gb, da, db, out, qkv):
+        lo = i * 2 * Q_COLS
+        qkv_f[:, lo:lo + 128] = a[:, 0:128]
+        qkv_f[:, lo + 128:lo + 256] = half(a1, roll(b0, 64))
+        qkv_f[:, lo + 256:lo + 384] = half(roll(b0, 64), roll(b1, 64))
+        lo = q_cols + i * 128
+        qkv_f[:, lo:lo + 128] = half(roll(a1, 64), b1)
+        lo = lo + kv_cols
+        qkv_f[:, lo:lo + 128] = jnp.concatenate([a2, b[:, 256:]], axis=1)
+    saved.append(store(9, qkv_f, m["qkv_o"]))
+    rest["out"].wait()
+    n = m["out_v"].shape[1]
+    for i in range(4):
+        m["out_f"][n * i:n * (i + 1)] = m["out_v"][i].astype(F32)
+    saved.append(store(10, m["out_f"], m["out_o"]))
+    for k, n in ((11, "ig"), (12, "mixed")):
+        rest[n].wait()
+        saved.append(store(k, m[n + "_v"], m[n + "_o"]))
+    gains = m["gains"][...]
+    width = gains.shape[1]
+    turned = pltpu.roll(gains, (width - own_rows * lax.axis_index("grp")) % width, 1)
+    m["one_o"][...] = turned[0:1, 0:own_rows]
+    m["two_o"][...] = turned[1:2, 0:own_rows]
+    m["q_o"][...] = gains[2:3, 0:HEAD_DIM]
+    m["k_o"][...] = gains[2:3, HEAD_DIM:2 * HEAD_DIM]
+    for copy in saved:
+        copy.wait()
+
+
+def order_call(g):
     shape = jax.ShapeDtypeStruct
+    ga, gb, da, db, out, qkv, mixed, ig = (g[n] for n in ORDER_IN)
     _, own_rows, cols_a = ga.shape
     cols = cols_a + gb.shape[2]
     width = da.shape[2]
     part = 4 * (da.shape[1] + db.shape[1])
     qkv_cols = (HEADS + 2 * KV_HEADS) * HEAD_DIM
-    block = lambda v, n: pl.BlockSpec((n,) + v.shape[1:], lambda i, w: (i, 0, 0))
-    return pl.pallas_call(
-        order_kernel,
+    outs = {
+        "gu_o": shape((own_rows, 8 * cols), F32), "down_o": shape((part, width), F32),
+        "out_o": shape((own_rows, width), F32), "qkv_o": shape((own_rows, qkv_cols), F32),
+        "ig_o": shape(ig.shape, F32), "mixed_o": shape(mixed.shape, BF16),
+        "one_o": shape((1, own_rows), F32), "two_o": shape((1, own_rows), F32),
+        "q_o": shape((1, HEAD_DIM), F32), "k_o": shape((1, HEAD_DIM), F32),
+    }
+    ins = ("ga", "gb", "da", "db", "out", "qkv", "mixed", "ig")
+    scratch = {n + "_v": pltpu.VMEM(v.shape, v.dtype)
+               for n, v in zip(ins, (ga, gb, da, db, out, qkv, mixed, ig))}
+    scratch["gu_v"] = pltpu.VMEM((8, own_rows, cols), F32)
+    scratch["down_v"] = pltpu.VMEM((part, width), F32)
+    scratch["out_f"] = pltpu.VMEM((own_rows, width), F32)
+    scratch["qkv_f"] = pltpu.VMEM((own_rows, qkv_cols), F32)
+    scratch["load"], scratch["save"] = dma(14), dma(13)
+    names = ins + ("gains",) + tuple(outs) + tuple(scratch)
+    got = pl.pallas_call(
+        functools.partial(order_kernel, names),
         name="final_order",
-        grid=(4, 2),
-        out_shape=(
-            shape((own_rows, 8 * cols), F32), shape((part, width), F32),
-            shape((4 * out.shape[1], width), F32), shape((own_rows, qkv_cols), F32)),
-        in_specs=[block(ga, 2), block(gb, 2), block(da, 1), block(db, 1), block(out, 1),
-                  block(qkv, 2)],
-        out_specs=(
-            pl.BlockSpec((own_rows, cols), lambda i, w: (0, 4 * w + i)),
-            pl.BlockSpec((part, width), lambda i, w: (0, 0)),
-            pl.BlockSpec((out.shape[1], width), lambda i, w: (i, 0)),
-            pl.BlockSpec((own_rows, qkv_cols), lambda i, w: (0, 0))),
-        compiler_params=pltpu.CompilerParams(
-            dimension_semantics=("arbitrary", "arbitrary"), vmem_limit_bytes=48 * 2**20),
-    )(ga, gb, da, db, out, qkv)
-
-
-def rope_tables(positions):
+        out_shape=tuple(outs.values()),
+        in_specs=[ANY] * 8 + [VMEM],
+        out_specs=(ANY,) * 6 + (VMEM,) * 4,
+        scratch_shapes=list(scratch.values()),
+        compiler_params=pltpu.CompilerParams(vmem_limit_bytes=62 * 2**20),
+    )(ga, gb, da, db, out, qkv, mixed, ig, g["gains_g"])
+    return dict(zip(outs, got))
+
+
+ORDER_IN = ("ga_g", "gb_g", "da_g", "db_g", "out_g", "qkv_g", "mixed", "input_grad")
+
+
+def rope_table(start, rows):
     half = HEAD_DIM // 2
-    freq = jnp.exp(-jnp.log(THETA) * jnp.arange(half, dtype=F32) * 2.0 / HEAD_DIM)
-    angle = positions.astype(F32)[:, None] * freq[None, :]
-    cos, sin = jnp.cos(angle), jnp.sin(angle)
-    zero = jnp.zeros_like(cos)
-    return jnp.concatenate([cos, cos, zero, zero], 1), jnp.concatenate([-sin, sin, zero, zero], 1)
+    lane = lax.broadcasted_iota(jnp.int32, (rows, 4 * half), 1)
+    freq = jnp.exp(-jnp.log(THETA) * (lane % half).astype(F32) * 2.0 / HEAD_DIM)
+    position = start + lax.broadcasted_iota(jnp.int32, (rows, 4 * half), 0)
+    angle = position.astype(F32) * freq
+    sine = jnp.sin(angle)
+    return jnp.where(lane < 2 * half, jnp.cos(angle), jnp.where(lane < 3 * half, -sine, sine))
 
 
 def over_quads(array):
@@ -1669,38 +1763,21 @@
     rows, width = tokens.shape
     _, y, c, z, x = here()
     r = 2 * y + c
-    q_width, kv_width = HEADS * HEAD_DIM, KV_HEADS * HEAD_DIM
-    own_rows = w_qkv.shape[0]
     span = 2 * rows
-    cut = lax.dynamic_slice_in_dim
-
-    q_pair = cut(w_qkv, 2 * Q_COLS * r, 2 * Q_COLS, 1)
-    k_pair = cut(w_qkv, q_width + 2 * HEAD_DIM * r, 2 * HEAD_DIM, 1)
-    v_pair = cut(w_qkv, q_width + kv_width + 2 * HEAD_DIM * r, 2 * HEAD_DIM, 1)
-    wq = jnp.stack([
-        jnp.concatenate([
-            q_pair[:, i * Q_COLS:(i + 1) * Q_COLS],
-            k_pair[:, i * HEAD_DIM:(i + 1) * HEAD_DIM],
-            v_pair[:, i * HEAD_DIM:(i + 1) * HEAD_DIM]], 1)
-        for i in range(2)])
-    gains = jnp.zeros((16, 256), BF16)
-    gains = gains.at[0, :own_rows].set(attn_gain).at[1, :own_rows].set(ffn_gain)
-    seg = jnp.broadcast_to(segment_ids[None, :], (8, rows))
-    cos, sin = rope_tables(span * z + jnp.arange(span, dtype=jnp.int32))
-
-    def padded(gain):
-        return jnp.zeros((8, 128), F32).at[:, :HEAD_DIM].set(gain.astype(F32)[None])
-
-    qg, kg = padded(q_gain), padded(k_gain)
-    g = block_call(tokens, cotangent, seg, wq, gains, w_gate_up, w_down, w_out, qg, kg, cos, sin)
-    gu, down, out, qkv = order_call(
-        *[over_quads(g[n]) for n in ("ga_g", "gb_g", "da_g", "db_g", "out_g", "qkv_g")])
-    gains_sum = over_quads(g["gains_g"])
-    place = 2 * z + x
-    gain_one = cut(gains_sum[0], place * own_rows, own_rows, 0)
-    gain_two = cut(gains_sum[1], place * own_rows, own_rows, 0)
-    return (g["mixed"], g["input_grad"], gain_one, qkv, gains_sum[2, :HEAD_DIM],
-            gains_sum[2, HEAD_DIM:2 * HEAD_DIM], out, gain_two, gu, down)
+    rope = rope_table(span * z, span)
+    parts = (attn_gain, q_gain, ffn_gain, k_gain, segment_ids)
+    total = sum(v.shape[0] for v in parts)
+    small, at = 0.0, 0
+    for v in parts:
+        n = v.shape[0]
+        small = small + jnp.pad(v.astype(F32)[None], ((0, 0), (at, total - at - n)))
+        at += n
+    g = block_call(tokens, cotangent, small, w_qkv, w_gate_up, w_down, w_out, rope)
+    g = {n: over_quads(v) if n.endswith("_g") else v for n, v in g.items()}
+    o = order_call(g)
+    flat = lambda n: o[n].reshape(-1)
+    return (o["mixed_o"], o["ig_o"], flat("one_o"), o["qkv_o"], flat("q_o"), flat("k_o"),
+            o["out_o"], flat("two_o"), o["gu_o"], o["down_o"])
 
 
 def solution(mesh):

time: 313 us -> 295 us (0.942)
  local copies, waits for them, and re-layouts: 17.4 us -> 1.32 us
    unnamed x18 -> x0, local copies, waits for them, and re-layouts: 7.72 us -> none
where the time goes in v6:
time: 295 us; the launch traced here: 293 us
  Pallas kernels  287 us (97%)
  other arithmetic  3.21 us (1%)
    pallas_call x1, Pallas kernels, block_call(): pl.pallas_call(functools.partial(block_kernel, names), name='block', out_...  278 us
    pallas_call x1, Pallas kernels, order_call(): pl.pallas_call(functools.partial(order_kernel, names), name='final_order'...  9.32 us

profile of v6, /device:TPU:0, one launch (start us, length us, event | category | flops | bytes accessed | tf_op | source)
XLA Modules:
  0.0 292.8 jit_solution(6417846209221347213)
XLA Ops:
  0.7 0.7 convert_bitcast_fusion
  1.3 0.7 broadcast_in_dim.19
  2.0 0.7 broadcast_in_dim.21
  2.6 1.3 pad_add_fusion.refs_2_
  4.0 1.2 fusion.refs_7_
  5.2 278.1 %block.1 = (bf16[128,1536]{1,0:T(8,128)(2,1)}, f32[128,1536]{1,0:T(8,128)}, f32[8,1536]{1,0:T(8,128)}, bf16[8,192,512]{2,1,0:T(8,128)(2,1)}, bf16[8,192,640]{2,1...) custom-call(bf16[128,1536]{1,0:T(8,128)(2,1)} %refs_0_.1, ...), custom_call_target="tpu_custom_call" | custom-call | tf_op jit(solution)/shard_map/block/pallas_call | solution.py:1595
  283.3 9.3 %final_order.1 = (f32[192,9216]{1,0:T(8,128)}, f32[576,1536]{1,0:T(8,128)}, f32[192,1536]{1,0:T(8,128)}, f32[192,2560]{1,0:T(8,128)}, f32[128,1536]{1,0:T(8,128)...) custom-call(bf16[8,192,512]{2,1,0:T(8,128)(2,1)} %get-tuple-element., ...), custom_call_target="tpu_custom_call" | custom-call | tf_op jit(solution)/shard_map/final_order/pallas_call | solution.py:1728
  (4 shorter events, 0.0 us)

commit v7 on v6

--- a/solution.py
+++ b/solution.py
@@ -346,18 +346,16 @@
                 add(self.block(zk), self.slot(zk))
                 self.copy(zk, 1, zk).start()
 
-    def second_hop(self, add):
-        @pl.when(self.z == 1)
-        def _():
-            self.arrive(0)
-            add(self.block(0), self.slot(0))
-            self.copy(0, 0, 0).start()
-
-        @pl.when(self.z == 2)
-        def _():
-            self.arrive(3)
-            add(self.block(3), self.slot(3))
-            self.copy(3, 3, 4).start()
+    def second_hop(self, add, inner=(1, 2)):
+        for z, zk, to, at in ((1, 0, 0, 0), (2, 3, 3, 4)):
+            if z not in inner:
+                continue
+
+            @pl.when(self.z == z)
+            def _():
+                self.arrive(zk)
+                add(self.block(zk), self.slot(zk))
+                self.copy(zk, to, at).start()
 
     def collect(self, total):
         z = self.z
@@ -436,12 +434,15 @@
 
 
 class SeqSum:
-    def __init__(self, part, scratch):
-        self.part = part
-        (self.r1, self.chip, self.rx, self.ry, self.mine, self.late, self.out,
+    def __init__(self, part, scratch, by_x=False):
+        self.part, self.by_x = part, by_x
+        (self.r1, self.chip, self.rx, self.mine, self.late, self.out,
          self.send, self.recv) = scratch
         _, self.y, self.c, _, self.x = here()
         self.to_c, self.to_x, self.to_y = neighbours()
+        rows = part.shape[1]
+        self.top = pl.ds(0, rows if by_x else rows // 2)
+        self.low = pl.ds(rows // 2, rows // 2)
 
     def copy(self, k, src, dst, to):
         return remote(src, dst, self.send.at[k], self.recv.at[k], to)
@@ -456,17 +457,17 @@
 
     def along_x(self, b):
         at = 2 * b + 1 - self.x
-        return self.copy(4 + b, self.chip.at[at, pl.ds(0, 64)], self.rx.at[b], self.to_x)
+        return self.copy(4 + b, self.chip.at[at, self.top], self.rx.at[b, self.top], self.to_x)
 
     def along_y(self, a):
         at = 2 * (1 - self.y) + a
-        return self.copy(6 + a, self.chip.at[at, pl.ds(64, 64)], self.ry.at[a], self.to_y)
+        return self.copy(6 + a, self.chip.at[at, self.low], self.rx.at[a, self.low], self.to_y)
 
     def last_y(self):
-        return self.copy(8, self.mine.at[0], self.late.at[0], self.to_y)
+        return self.copy(8, self.mine.at[self.top], self.late.at[self.top], self.to_y)
 
     def last_x(self):
-        return self.copy(9, self.mine.at[1], self.late.at[1], self.to_x)
+        return self.copy(9, self.mine.at[self.low], self.late.at[self.low], self.to_x)
 
     def total(self, b, a):
         self.swap(b, a).wait_recv()
@@ -477,9 +478,10 @@
         b = 1 - self.y
         for a in (1 - self.x, self.x):
             self.chip[2 * b + a] = self.total(b, a).astype(BF16)
-            self.along_y(a).start()
             if a is not self.x:
                 self.along_x(b).start()
+            if not self.by_x:
+                self.along_y(a).start()
 
     def take_near(self):
         b, x = self.y, self.x
@@ -488,26 +490,30 @@
         self.out[...] = self.total(b, x)
 
     def middle(self):
-        x, y = self.x, self.y
+        x, y, top, low = self.x, self.y, self.top, self.low
         self.along_x(1 - y).wait_recv()
-        self.mine[0] = (
-            self.chip[2 * (1 - y) + x, 0:64].astype(F32) + self.rx[1 - y].astype(F32)
+        self.mine[top] = (
+            self.chip[2 * (1 - y) + x, top].astype(F32) + self.rx[1 - y, top].astype(F32)
         ).astype(BF16)
         self.last_y().start()
+        if self.by_x:
+            return
         self.along_y(1 - x).wait_recv()
-        self.mine[1] = (
-            self.chip[2 * y + 1 - x, 64:128].astype(F32) + self.ry[1 - x].astype(F32)
+        self.mine[low] = (
+            self.chip[2 * y + 1 - x, low].astype(F32) + self.rx[1 - x, low].astype(F32)
         ).astype(BF16)
         self.last_x().start()
 
     def finish(self):
-        x, y = self.x, self.y
+        x, y, top, low = self.x, self.y, self.top, self.low
         self.along_x(y).wait_recv()
+        self.last_y().wait_recv()
+        self.out[top] += self.rx[y, top].astype(F32) + self.late[top].astype(F32)
+        if self.by_x:
+            return
         self.along_y(x).wait_recv()
-        self.last_y().wait_recv()
         self.last_x().wait_recv()
-        self.out[0:64] += self.rx[y].astype(F32) + self.late[0].astype(F32)
-        self.out[64:128] += self.ry[x].astype(F32) + self.late[1].astype(F32)
+        self.out[low] += self.rx[x, low].astype(F32) + self.late[low].astype(F32)
 
     def given(self):
         for b in range(2):
@@ -517,9 +523,11 @@
     def passed(self):
         for b in range(2):
             self.along_x(b).wait_send()
-            self.along_y(b).wait_send()
+            if not self.by_x:
+                self.along_y(b).wait_send()
         self.last_y().wait_send()
-        self.last_x().wait_send()
+        if not self.by_x:
+            self.last_x().wait_send()
 
     def sent(self):
         self.given()
@@ -530,10 +538,9 @@
     return [
         pltpu.VMEM((4, 128, width), BF16),
         pltpu.VMEM((4, 128, width), BF16),
-        pltpu.VMEM((2, 64, width), BF16),
-        pltpu.VMEM((2, 64, width), BF16),
-        pltpu.VMEM((2, 64, width), BF16),
-        pltpu.VMEM((2, 64, width), BF16),
+        pltpu.VMEM((2, 128, width), BF16),
+        pltpu.VMEM((128, width), BF16),
+        pltpu.VMEM((128, width), BF16),
         pltpu.VMEM((128, width), F32),
         dma(10),
         dma(10),
@@ -578,29 +585,6 @@
     def sent(self):
         for zk in range(4):
             pl.when(self.z != zk)(lambda zk=zk: self.copy(zk).wait_send())
-
-
-class DirectBoth:
-    def __init__(self, half, slot, send, recv):
-        self.half, self.slot, self.send, self.recv = half, slot, send, recv
-        self.base, self.y, self.c, self.z, self.x = here()
-
-    def copy(self, zk, a):
-        return remote(self.half(zk, a), self.slot(self.z, self.x), self.send.at[zk, a],
-                      self.recv.at[self.z, self.x], device(self.base, self.y, self.c, zk, a))
-
-    def start(self, zk):
-        self.copy(zk, 1 - self.x).start()
-        pl.when(zk != self.z)(lambda: self.copy(zk, self.x).start())
-
-    def arrive(self, zk, a):
-        ref = self.slot(zk, a)
-        remote(ref, ref, self.send.at[0, 0], self.recv.at[zk, a],
-               device(self.base, self.y, self.c, self.z, 1 - self.x)).wait_recv()
-
-    def sent(self):
-        for k in range(1, 8):
-            self.copy((self.z + k // 2) % 4, (self.x + k) % 2).wait_send()
 
 
 class RepShare:
@@ -1050,12 +1034,12 @@
     for zk in range(4):
         hand(13, zk, m["zb"], wdb, b_sems, rows_b)
     gate_b.finish()
+    gate_sum.second_hop(add)
     handed(m["zb"], wdb, b_sems, rows_b)
     for i in range(4):
         pl.when(r != i)(lambda i=i: remote(
             spread_from(i), got_a.at[i], m["ha_s"].at[i], m["ha_r"].at[i], to_c).wait_recv())
     down_sum.start()
-    gate_sum.second_hop(add)
     summed.passed()
 
     def total_in(block):
@@ -1110,7 +1094,7 @@
         cols = pl.ds(pl.multiple_of(zk * block_rows, 128), block_rows)
         left = n2[:, :, cols].reshape(8 * rows, block_rows)
         ggu[zk] = first_dims(left, dgu[:, cols_a:]).astype(BF16)
-        gu_sum.start_one(zk)
+        pl.when(i < 2)(lambda: gu_sum.start_one(zk))
         return carry
 
     lax.fori_loop(0, 2, grad_gu, 0)
@@ -1151,7 +1135,7 @@
         return carry
 
     lax.fori_loop(0, 4, down, 0)
-    mixed = SeqSum(parts, [m[n] for n in SUM_NAMES])
+    mixed = SeqSum(parts, [m[n] for n in SUM_NAMES], by_x=True)
 
     def give(i, lo, n, ss, rs):
         return remote(gdo.at[i, pl.ds(lo, n)], got.at[r, pl.ds(lo, n)], ss.at[i], rs.at[r],
@@ -1171,6 +1155,34 @@
     def give_sent(lo, n, ss, rs):
         for i in range(4):
             pl.when(r != i)(lambda i=i: give(i, lo, n, ss, rs).wait_send())
+
+    def swap(src, out, ss, rs):
+        return remote(src.at[pl.ds(own_rows * (1 - x), own_rows)], out.at[t_own], ss, rs, to_x)
+
+    def keep_own(k, src, out):
+        copy = pltpu.make_async_copy(src.at[pl.ds(own_rows * x, own_rows)], out.at[t_own],
+                                     keep.at[k])
+        copy.start()
+        return copy
+
+    def swapped(src, out, ss, rs):
+        return remote(src.at[pl.ds(own_rows * x, own_rows)], out.at[2 * r + 1 - x], ss, rs, to_x)
+
+    def pairs(out):
+        return lambda i: out.at[pl.ds(2 * i, 2)]
+
+    ga_out, gb_out, qkv_out = m["ga_g"], m["gb_g"], m["qkv_g"]
+    ga_swap = swap(gga.at[z], ga_out, m["xs_s"], m["xs_r"])
+    ga_keep = local_copy(14, gga.at[z, pl.ds(own_rows * x, own_rows)], ga_out.at[t_own])
+    da_keep = local_copy(15, got_a.at[z], m["da_g"].at[r])
+    ga_share = RepShare(pairs(ga_out), m["ra_s"], m["ra_r"])
+    da_share = RepShare(lambda i: m["da_g"].at[i], m["rc_s"], m["rc_r"])
+
+    def swap_first():
+        gate_sum.collect(total_in(gga.at[z]))
+        down_sum.collect(total_in(got_a.at[z]))
+        for copy in (ga_swap, ga_keep, da_keep):
+            copy.start()
 
     branch.forward()
     branch.arrive(2)
@@ -1178,30 +1190,8 @@
     give_all(0, quarter_d, m["he_s"], m["he_r"])
     mixed.give(0)
     mixed.give(1)
+    swap_first()
     gu_sum.first_hop(add, (1,))
-
-    def swap(src, out, ss, rs):
-        return remote(src.at[pl.ds(own_rows * (1 - x), own_rows)], out.at[t_own], ss, rs, to_x)
-
-    def keep_own(k, src, out):
-        copy = pltpu.make_async_copy(src.at[pl.ds(own_rows * x, own_rows)], out.at[t_own],
-                                     keep.at[k])
-        copy.start()
-        return copy
-
-    def swapped(src, out, ss, rs):
-        return remote(src.at[pl.ds(own_rows * x, own_rows)], out.at[2 * r + 1 - x], ss, rs, to_x)
-
-    def pairs(out):
-        return lambda i: out.at[pl.ds(2 * i, 2)]
-
-    ga_out, gb_out, qkv_out = m["ga_g"], m["gb_g"], m["qkv_g"]
-    ga_swap = swap(gga.at[z], ga_out, m["xs_s"], m["xs_r"])
-    ga_keep = local_copy(14, gga.at[z, pl.ds(own_rows * x, own_rows)], ga_out.at[t_own])
-    da_keep = local_copy(15, got_a.at[z], m["da_g"].at[r])
-    ga_share = RepShare(pairs(ga_out), m["ra_s"], m["ra_r"])
-    da_share = RepShare(lambda i: m["da_g"].at[i], m["rc_s"], m["rc_r"])
-
 
     wo, qkv, dkv = m["wo_v"], qkv_all, kv
     db, dqkv, do_v = m["db"], m["dqkv"], m["do"]
@@ -1210,12 +1200,6 @@
 
     down_rest = ChainSum(lambda zk: got.at[zk, pl.ds(0, quarter_d)],
                          lambda at: m["down_slot"].at[at], m["zd_s"], m["zd_r"])
-
-    def swap_first():
-        gate_sum.collect(total_in(gga.at[z]))
-        down_sum.collect(total_in(got_a.at[z]))
-        for copy in (ga_swap, ga_keep, da_keep):
-            copy.start()
 
     def share_first():
         ga_keep.wait()
@@ -1300,24 +1284,15 @@
         pl.when(k == 0)(lambda: gu_sum.second_hop(add))
         pl.when(k == 0)(mixed.take_far)
         pl.when(k == 0)(mixed.take_near)
-        pl.when(k == 1)(swap_first)
-        pl.when(k == 2)(mixed.middle)
-        pl.when(k == 3)(share_first)
+        pl.when(k == 1)(share_first)
+        pl.when(k == 3)(mixed.middle)
         pl.when(k == 3)(lambda: given(0, quarter_d, m["he_s"], m["he_r"]))
         return carry
 
     lax.fori_loop(0, 4, attend_back, 0)
     kv_merge(3)
+    gu_sum.start_one(farthest(2))
     down_rest.start()
-    mixed.finish()
-    branch.sent()
-    m["low"][...] = (m["mid"][...] + mixed.out[...]).astype(BF16)
-    mixed_out = loaded(17, m["low"], m["mixed"])
-    mixed.sent()
-    free = m["free"]
-    for to in (to_c, to_x, to_y):
-        pl.semaphore_signal(free, inc=1, device_id=to, device_id_type=MESH)
-
     for j in range(0, width, 512):
         cols = slice(j, j + 512)
         grad = first_dims(att[...].reshape(8 * rows, Q_COLS),
@@ -1325,14 +1300,8 @@
         for i in range(4):
             gdo[i, quarter_d:quarter_d + quarter_o, cols] = grad[quarter_o * i:quarter_o * (i + 1)]
     give_all(quarter_d, quarter_o, m["hf_s"], m["hf_r"])
-    gu_sum.collect(total_in(ggu.at[z]))
-    gb_swap = swap(ggu.at[z], gb_out, m["xg_s"], m["xg_r"])
-    gb_swap.start()
-    gb_keep = keep_own(14, ggu.at[z], gb_out)
-
-    pl.semaphore_wait(free, 3)
-
-    inputs = SeqSum(parts, [m[n] for n in SUM_NAMES])
+    mixed.given()
+    inputs = SeqSum(parts, [m[n] for n in SUM_NAMES], by_x=True)
 
     def finish_one(k, carry):
         b, e = (y + (k + 1) // 2) % 2, (c + 1 + k // 2) % 2
@@ -1352,16 +1321,12 @@
         dqkv[s, :, 256:320] = roll(total, 64)[:, 0:HEAD_DIM].astype(BF16)
         out = last_dims(dqkv[s], wq[...]).astype(BF16)
         parts[pl.ds(2 * s, 2)] = out.reshape(2, rows, width)
-        pl.when(k < 2)(lambda: inputs.give(b))
-        pl.when(k == 2)(inputs.take_far)
-        pl.when(k == 3)(inputs.take_near)
         return carry
 
     lax.fori_loop(0, 4, finish_one, 0)
-    down_rest.first_hop(add)
     gqkv = m["gqkv"]
-    qkv_sum = DirectBoth(lambda zk, a: gqkv.at[zk, pl.ds(own_rows * a, own_rows)],
-                         lambda zk, a: m["qkv_slot"].at[zk, a], m["zq_s"], m["zq_r"])
+    qkv_sum = Direct(lambda zk: gqkv.at[zk], lambda zk: m["qkv_slot"].at[zk], m["zq_s"],
+                     m["zq_r"])
 
     def grad_qkv(i, carry):
         zk = farthest(i)
@@ -1372,8 +1337,31 @@
         return carry
 
     lax.fori_loop(0, 4, grad_qkv, 0)
+    gu_sum.collect(total_in(ggu.at[z]))
+    gb_swap = swap(ggu.at[z], gb_out, m["xg_s"], m["xg_r"])
+    gb_swap.start()
+    gb_keep = keep_own(14, ggu.at[z], gb_out)
+    mixed.finish()
+    branch.sent()
+    m["low"][...] = (m["mid"][...] + mixed.out[...]).astype(BF16)
+    mixed_out = loaded(17, m["low"], m["mixed"])
+    mixed.passed()
+    free = m["free"]
+    for to in (to_c, to_x, to_y):
+        pl.semaphore_signal(free, inc=1, device_id=to, device_id_type=MESH)
+
+    pl.semaphore_wait(free, 3)
+    inputs.give(0)
+    inputs.give(1)
+    inputs.take_far()
+    inputs.take_near()
+    gb_keep.wait()
+    swapped(ggu.at[z], gb_out, m["xg_s"], m["xg_r"]).wait_recv()
+    gb_share = RepShare(pairs(gb_out), m["rg_s"], m["rg_r"])
+    gb_share.start()
+    down_rest.first_hop(add)
     inputs.middle()
-    down_rest.second_hop(add)
+    down_rest.second_hop(add, (1,))
     given(quarter_d, quarter_o, m["hf_s"], m["hf_r"])
     out_sum = Direct(lambda zk: got.at[zk, pl.ds(quarter_d, quarter_o)],
                      lambda zk: m["out_slot"].at[zk], m["zo_s"], m["zo_r"])
@@ -1406,13 +1394,23 @@
 
     for k in range(1, 8):
         gain_sum(k).start()
-    gb_keep.wait()
-    swapped(ggu.at[z], gb_out, m["xg_s"], m["xg_r"]).wait_recv()
-    gb_share = RepShare(pairs(gb_out), m["rg_s"], m["rg_r"])
-    gb_share.start()
+
+    down_rest.second_hop(add, (2,))
+
+    total = gqkv[z].astype(F32)
+    for term in qkv_sum.take():
+        total = total + term
+    gqkv[z] = total.astype(BF16)
+    qkv_swap = swap(gqkv.at[z], qkv_out, m["xq_s"], m["xq_r"])
+    qkv_swap.start()
+    qkv_keep = keep_own(16, gqkv.at[z], qkv_out)
+    qkv_share = RepShare(pairs(qkv_out), m["rq_s"], m["rq_r"])
 
     down_rest.collect(total_in(got.at[z, pl.ds(0, quarter_d)]))
     db_keep = loaded(15, got.at[z, pl.ds(0, quarter_d)], m["db_g"].at[r])
+    db_keep.wait()
+    db_share = RepShare(lambda i: m["db_g"].at[i], m["rd_s"], m["rd_r"])
+    db_share.start()
     for k in range(1, 8):
         gain_sum(k).wait_recv()
     total = gains_own[...]
@@ -1427,27 +1425,10 @@
 
     for k in range(1, 4):
         gain_z(k).start()
-    db_keep.wait()
-    db_share = RepShare(lambda i: m["db_g"].at[i], m["rd_s"], m["rd_r"])
-    db_share.start()
     gb_share.forward()
-
-    qkv_own = m["qkv_slot"].at[z]
-    total = gqkv[z, pl.ds(own_rows * x, own_rows)].astype(F32)
-    for k in (1, 3, 2):
-        qkv_sum.arrive((z + k) % 4, x)
-        total = total + m["qkv_slot"][(z + k) % 4, x].astype(F32)
-    qkv_own[x] = total.astype(BF16)
-    total = jnp.zeros((own_rows, HEAD_COLS), F32)
-    for k in (0, 1, 3, 2):
-        qkv_sum.arrive((z + k) % 4, 1 - x)
-        total = total + m["qkv_slot"][(z + k) % 4, 1 - x].astype(F32)
-    qkv_own[1 - x] = total.astype(BF16)
-    qkv_keep = loaded(16, qkv_own, pairs(qkv_out)(r))
     qkv_keep.wait()
-    qkv_share = RepShare(pairs(qkv_out), m["rq_s"], m["rq_r"])
+    swapped(gqkv.at[z], qkv_out, m["xq_s"], m["xq_r"]).wait_recv()
     qkv_share.start()
-
     out_own = got.at[z, pl.ds(quarter_d, quarter_o)]
     total = out_own[...].astype(F32)
     for term in out_sum.take():
@@ -1469,7 +1450,7 @@
 
     for share in shares:
         share.sent()
-    for copy in (ga_swap, gb_swap):
+    for copy in (ga_swap, gb_swap, qkv_swap):
         copy.wait_send()
     for k in range(1, 8):
         gain_sum(k).wait_send()
@@ -1508,7 +1489,7 @@
     hand_sent(m["zb"], wdb, b_sems, rows_b)
 
 
-SUM_NAMES = ("r1", "chip", "rx", "ry", "mine", "late", "sum_out", "sum_s", "sum_r")
+SUM_NAMES = ("r1", "chip", "rx", "mine", "late", "sum_out", "sum_s", "sum_r")
 IN = ("tok", "cot", "small", "wqkv", "wgu", "wd", "wo", "rope")
 OUT = ("mixed", "input_grad", "gains_g", "ga_g", "gb_g", "da_g", "db_g", "out_g", "qkv_g",
        "zo", "za", "zb", "gains_all")
@@ -1570,7 +1551,7 @@
         "down_slot": ((5, quarter_d, width), BF16),
         "out_slot": ((4, quarter_o, width), BF16),
         "gqkv": ((4, 2 * own_rows, HEAD_COLS), BF16),
-        "qkv_slot": ((4, 2, own_rows, HEAD_COLS), BF16),
+        "qkv_slot": ((4, 2 * own_rows, HEAD_COLS), BF16),
         "row_two": ((1, width), F32), "row_head": ((1, 128), F32),
         "z_rows": ((4, 8, width), F32),
     }
@@ -1579,7 +1560,7 @@
         "gm": (7, 7), "gz": (3, 3), "wa": (6, 4), "wb": (6, 4), "wo": (6, 4), "wx": (1, 1),
         "xa": (1, 1), "xb": (1, 1), "xs": (1, 1), "xg": (1, 1), "ca": (5, 4), "cb": (5, 4),
         "da": (5, 4), "db": (5, 4), "ys": (4, 5), "yd": (4, 5), "zg": (4, 5), "zd": (4, 5),
-        "zo": (4, 4), "zq": ((4, 2), (4, 2)), "zk": ((3, 4), (3, 4)), "kv": ((3, 4), (4, 4)),
+        "zo": (4, 4), "zq": (4, 4), "xq": (1, 1), "zk": ((3, 4), (3, 4)), "kv": ((3, 4), (4, 4)),
         "su": (3, 4), "ha": (4, 4), "hb": (4, 4), "hd": (4, 4), "he": (4, 4), "hf": (4, 4),
         "ho": (4, 4), "ra": (3, 3), "rc": (3, 3), "rd": (3, 3), "re": (3, 3), "rg": (3, 3),
         "rq": (3, 3),

time: 295 us -> 288 us (0.976); the launches traced: 293 us -> 282 us
  Pallas kernels: 287 us -> 277 us
    pallas_call x1, Pallas kernels: 278 us -> 268 us  [block_call(): pl.pallas_call(functools.partial(block_kernel, names), name='block', out_...]
where the time goes in v7:
time: 288 us; the launch traced here: 282 us
  Pallas kernels  277 us (96%)
  other arithmetic  3.21 us (1%)
    pallas_call x1, Pallas kernels, block_call(): pl.pallas_call(functools.partial(block_kernel, names), name='block', out_...  268 us
    pallas_call x1, Pallas kernels, order_call(): pl.pallas_call(functools.partial(order_kernel, names), name='final_order'...  9.32 us

profile of v7, /device:TPU:0, one launch (start us, length us, event | category | flops | bytes accessed | tf_op | source)
XLA Modules:
  0.0 282.3 jit_solution(15586082844840595307)
XLA Ops:
  0.7 0.7 convert_bitcast_fusion
  1.3 0.7 broadcast_in_dim.19
  2.0 0.7 broadcast_in_dim.21
  2.6 1.3 pad_add_fusion.refs_2_
  4.0 1.2 fusion.refs_7_
  5.2 267.6 %block.1 = (bf16[128,1536]{1,0:T(8,128)(2,1)}, f32[128,1536]{1,0:T(8,128)}, f32[8,1536]{1,0:T(8,128)}, bf16[8,192,512]{2,1,0:T(8,128)(2,1)}, bf16[8,192,640]{2,1...) custom-call(bf16[128,1536]{1,0:T(8,128)(2,1)} %refs_0_.1, ...), custom_call_target="tpu_custom_call" | custom-call | tf_op jit(solution)/shard_map/block/pallas_call | solution.py:1576
  272.8 9.3 %final_order.1 = (f32[192,9216]{1,0:T(8,128)}, f32[576,1536]{1,0:T(8,128)}, f32[192,1536]{1,0:T(8,128)}, f32[192,2560]{1,0:T(8,128)}, f32[128,1536]{1,0:T(8,128)...) custom-call(bf16[8,192,512]{2,1,0:T(8,128)(2,1)} %get-tuple-element., ...), custom_call_target="tpu_custom_call" | custom-call | tf_op jit(solution)/shard_map/final_order/pallas_call | solution.py:1709
  (4 shorter events, 0.0 us)

commit v8 on v7

--- a/solution.py
+++ b/solution.py
@@ -622,6 +622,16 @@
     gain_grad = jnp.sum(dy * u * inv, axis=0, keepdims=True)
     inner = jnp.sum(scaled * u, axis=-1, keepdims=True) * (1.0 / HEAD_DIM)
     return inv * scaled - u * (inv * inv * inv * inner), gain_grad
+
+
+def rope_table(start, rows):
+    half = HEAD_DIM // 2
+    lane = lax.broadcasted_iota(jnp.int32, (rows, 4 * half), 1)
+    freq = jnp.exp(-jnp.log(THETA) * (lane % half).astype(F32) * 2.0 / HEAD_DIM)
+    position = start + lax.broadcasted_iota(jnp.int32, (rows, 4 * half), 0)
+    angle = position.astype(F32) * freq
+    sine = jnp.sin(angle)
+    return jnp.where(lane < 2 * half, jnp.cos(angle), jnp.where(lane < 3 * half, -sine, sine))
 
 
 def block_kernel(names, *refs):
@@ -790,6 +800,7 @@
     gate_b = Chain(unit(cols_a, cols_b), m["cb_s"], m["cb_r"])
     down_a = Chain(lambda zk: m["za"].at[zk], m["da_s"], m["da_r"])
     down_b = Chain(lambda zk: m["zb"].at[zk], m["db_s"], m["db_r"])
+    m["rope"][...] = rope_table(2 * rows * z, 2 * rows)
     tok.forward()
     for copy in (cross_a, mine_a, cross_b, mine_b):
         copy.start()
@@ -1252,6 +1263,8 @@
             do_v[pl.ds(j * span, span)] = part_j
             deltas.append(jnp.sum(part_j.astype(F32) * o, axis=1, keepdims=True))
         delta = jnp.concatenate(deltas, axis=0)
+        m["q_t"][...] = jnp.transpose(q_all[s].astype(F32)).astype(BF16)
+        m["do_t"][...] = jnp.transpose(do_v[...].astype(F32)).astype(BF16)
         q_seg[...] = segment_columns(segs, z, s)
         acc[...] = jnp.zeros_like(acc)
 
@@ -1262,7 +1275,9 @@
             p = exp_scores(q, tile, q_seg[...], segment_row(segs, zk, s), diagonal)
             ds = (p * (last_dims(d_out, tile) - delta)).astype(BF16)
             acc[...] += jnp.dot(ds, tile, preferred_element_type=F32)
-            return first_dims(ds, q) + first_dims(p.astype(BF16), d_out)
+            both = jnp.dot(m["q_t"][...], ds, preferred_element_type=F32)
+            both = both + jnp.dot(m["do_t"][...], p.astype(BF16), preferred_element_type=F32)
+            return jnp.transpose(both)
 
         def step(zk, inner):
             dkv[zk, s] = block(zk, False).astype(BF16)
@@ -1293,6 +1308,41 @@
     kv_merge(3)
     gu_sum.start_one(farthest(2))
     down_rest.start()
+    inputs = SeqSum(parts, [m[n] for n in SUM_NAMES], by_x=True)
+
+    def finish_one(k, carry):
+        b, e = (y + (k + 1) // 2) % 2, (c + 1 + k // 2) % 2
+        s = 2 * b + e
+        @pl.when(z < 3)
+        def _():
+            kv_down(z, s).wait_recv()
+            own_kv[s] += kv_slot[z, s].astype(F32)
+
+        total = own_kv[s]
+        u = split_heads(qkv[s, :, 0:128], qkv[s, :, 128:256])[GROUP]
+        dy = rotated(low_half(total), cos, -sin)
+        raw, gain_part = head_back(dy, u, kg)
+        m["row_head"][...] += roll(gain_part, 64)
+        tile = dqkv[s, :, 128:256].astype(F32)
+        dqkv[s, :, 128:256] = (low_half(tile) + roll(raw, 64)).astype(BF16)
+        dqkv[s, :, 256:320] = roll(total, 64)[:, 0:HEAD_DIM].astype(BF16)
+        return carry
+
+    lax.fori_loop(0, 4, finish_one, 0)
+    gqkv = m["gqkv"]
+    qkv_sum = Direct(lambda zk: gqkv.at[zk], lambda zk: m["qkv_slot"].at[zk], m["zq_s"],
+                     m["zq_r"])
+
+    def grad_qkv(i, carry):
+        zk = farthest(i)
+        cols = pl.ds(pl.multiple_of(zk * block_rows, 128), block_rows)
+        left = normed[:, :, cols].reshape(8 * rows, block_rows)
+        gqkv[zk] = first_dims(left, dqkv[...].reshape(8 * rows, HEAD_COLS)).astype(BF16)
+        qkv_sum.start(zk)
+        return carry
+
+    lax.fori_loop(0, 4, grad_qkv, 0)
+
     for j in range(0, width, 512):
         cols = slice(j, j + 512)
         grad = first_dims(att[...].reshape(8 * rows, Q_COLS),
@@ -1301,42 +1351,13 @@
             gdo[i, quarter_d:quarter_d + quarter_o, cols] = grad[quarter_o * i:quarter_o * (i + 1)]
     give_all(quarter_d, quarter_o, m["hf_s"], m["hf_r"])
     mixed.given()
-    inputs = SeqSum(parts, [m[n] for n in SUM_NAMES], by_x=True)
-
-    def finish_one(k, carry):
-        b, e = (y + (k + 1) // 2) % 2, (c + 1 + k // 2) % 2
-        s = 2 * b + e
-        @pl.when(z < 3)
-        def _():
-            kv_down(z, s).wait_recv()
-            own_kv[s] += kv_slot[z, s].astype(F32)
-
-        total = own_kv[s]
-        u = split_heads(qkv[s, :, 0:128], qkv[s, :, 128:256])[GROUP]
-        dy = rotated(low_half(total), cos, -sin)
-        raw, gain_part = head_back(dy, u, kg)
-        m["row_head"][...] += roll(gain_part, 64)
-        tile = dqkv[s, :, 128:256].astype(F32)
-        dqkv[s, :, 128:256] = (low_half(tile) + roll(raw, 64)).astype(BF16)
-        dqkv[s, :, 256:320] = roll(total, 64)[:, 0:HEAD_DIM].astype(BF16)
+
+    def back_in(s, carry):
         out = last_dims(dqkv[s], wq[...]).astype(BF16)
         parts[pl.ds(2 * s, 2)] = out.reshape(2, rows, width)
         return carry
 
-    lax.fori_loop(0, 4, finish_one, 0)
-    gqkv = m["gqkv"]
-    qkv_sum = Direct(lambda zk: gqkv.at[zk], lambda zk: m["qkv_slot"].at[zk], m["zq_s"],
-                     m["zq_r"])
-
-    def grad_qkv(i, carry):
-        zk = farthest(i)
-        cols = pl.ds(pl.multiple_of(zk * block_rows, 128), block_rows)
-        left = normed[:, :, cols].reshape(8 * rows, block_rows)
-        gqkv[zk] = first_dims(left, dqkv[...].reshape(8 * rows, HEAD_COLS)).astype(BF16)
-        qkv_sum.start(zk)
-        return carry
-
-    lax.fori_loop(0, 4, grad_qkv, 0)
+    lax.fori_loop(0, 4, back_in, 0)
     gu_sum.collect(total_in(ggu.at[z]))
     gb_swap = swap(ggu.at[z], gb_out, m["xg_s"], m["xg_r"])
     gb_swap.start()
@@ -1490,7 +1511,7 @@
 
 
 SUM_NAMES = ("r1", "chip", "rx", "mine", "late", "sum_out", "sum_s", "sum_r")
-IN = ("tok", "cot", "small", "wqkv", "wgu", "wd", "wo", "rope")
+IN = ("tok", "cot", "small", "wqkv", "wgu", "wd", "wo")
 OUT = ("mixed", "input_grad", "gains_g", "ga_g", "gb_g", "da_g", "db_g", "out_g", "qkv_g",
        "zo", "za", "zb", "gains_all")
 
@@ -1527,7 +1548,7 @@
         "tok_all": ((8, rows, width), BF16), "cot_v": ((8, rows, width), BF16),
         "n2_v": ((8, rows, width), BF16), "db": ((8, rows, width), BF16),
         "part": ((8, rows, width), BF16),
-        "seg": (seg.shape, seg.dtype), "gains": (gains.shape, BF16),
+        "rope": ((span, 128), F32), "seg": (seg.shape, seg.dtype), "gains": (gains.shape, BF16),
         "wq": ((2, own_rows, HEAD_COLS), BF16), "wq_raw": ((own_rows, 640), BF16),
         "segs_v": ((4, 8) + seg.shape, seg.dtype), "gains_v": ((8,) + gains.shape, BF16),
         "wq_v": ((width, HEAD_COLS), BF16), "wo_v": ((Q_COLS, width), BF16),
@@ -1538,7 +1559,7 @@
         "kv_v": ((4, 4, span, 128), BF16), "kv_slot": ((3, 4, span, 128), BF16),
         "own_kv": ((4, span, 128), F32), "inv_v": ((4, span, 128), F32),
         "att_v": ((4, span, Q_COLS), BF16), "acc": ((heads, 128), F32),
-        "do": ((heads, 128), BF16), "q_seg": ((span, span), jnp.int32),
+        "do": ((heads, 128), BF16), "q_t": ((128, heads), BF16), "do_t": ((128, heads), BF16), "q_seg": ((span, span), jnp.int32),
         "dqkv": ((4, span, HEAD_COLS), BF16),
         "mid": ((rows, width), F32), "dmid": ((rows, width), F32), "low": ((rows, width), BF16),
         "g_one": ((1, width), F32), "g_two": ((1, width), F32),
@@ -1721,16 +1742,6 @@
 ORDER_IN = ("ga_g", "gb_g", "da_g", "db_g", "out_g", "qkv_g", "mixed", "input_grad")
 
 
-def rope_table(start, rows):
-    half = HEAD_DIM // 2
-    lane = lax.broadcasted_iota(jnp.int32, (rows, 4 * half), 1)
-    freq = jnp.exp(-jnp.log(THETA) * (lane % half).astype(F32) * 2.0 / HEAD_DIM)
-    position = start + lax.broadcasted_iota(jnp.int32, (rows, 4 * half), 0)
-    angle = position.astype(F32) * freq
-    sine = jnp.sin(angle)
-    return jnp.where(lane < 2 * half, jnp.cos(angle), jnp.where(lane < 3 * half, -sine, sine))
-
-
 def over_quads(array):
     reps = lax.axis_size("rep")
     if reps == 4:
@@ -1742,18 +1753,15 @@
 def local(tokens, attn_gain, w_qkv, q_gain, k_gain, w_out, ffn_gain, w_gate_up, w_down,
           cotangent, segment_ids):
     rows, width = tokens.shape
-    _, y, c, z, x = here()
-    r = 2 * y + c
-    span = 2 * rows
-    rope = rope_table(span * z, span)
     parts = (attn_gain, q_gain, ffn_gain, k_gain, segment_ids)
     total = sum(v.shape[0] for v in parts)
     small, at = 0.0, 0
     for v in parts:
         n = v.shape[0]
-        small = small + jnp.pad(v.astype(F32)[None], ((0, 0), (at, total - at - n)))
+        small = small + jnp.pad(v.astype(F32), (at, total - at - n))
         at += n
-    g = block_call(tokens, cotangent, small, w_qkv, w_gate_up, w_down, w_out, rope)
+    g = block_call(
+        tokens, cotangent, small.reshape(1, -1), w_qkv, w_gate_up, w_down, w_out)
     g = {n: over_quads(v) if n.endswith("_g") else v for n, v in g.items()}
     o = order_call(g)
     flat = lambda n: o[n].reshape(-1)

time: 288 us -> 286 us (level); the launches traced: 282 us -> 286 us
  Pallas kernels: 277 us -> 283 us
    pallas_call x1, Pallas kernels: 268 us -> 273 us  [block_call(): pl.pallas_call(functools.partial(block_kernel, names), name='block', out_...]
where the time goes in v8:
time: 286 us
  Pallas kernels  283 us (99%)
    pallas_call x1, Pallas kernels, block_call(): pl.pallas_call(functools.partial(block_kernel, names), name='block', out_...  273 us
    pallas_call x1, Pallas kernels, order_call(): pl.pallas_call(functools.partial(order_kernel, names), name='final_order'...  9.32 us

profile of v8, /device:TPU:0, one launch (start us, length us, event | category | flops | bytes accessed | tf_op | source)
XLA Modules:
  0.0 285.5 jit_solution(15436623684328943629)
XLA Ops:
  0.6 0.7 convert_element_type.10
  1.3 0.8 pad_add_fusion
  2.1 0.6 reshape.35.refs_2_
  2.7 273.3 %block.1 = (bf16[128,1536]{1,0:T(8,128)(2,1)}, f32[128,1536]{1,0:T(8,128)}, f32[8,1536]{1,0:T(8,128)}, bf16[8,192,512]{2,1,0:T(8,128)(2,1)}, bf16[8,192,640]{2,1...) custom-call(bf16[128,1536]{1,0:T(8,128)(2,1)} %refs_0_.1, ...), custom_call_target="tpu_custom_call" | custom-call | tf_op jit(solution)/shard_map/block/pallas_call | solution.py:1597
  276.0 9.3 %final_order.1 = (f32[192,9216]{1,0:T(8,128)}, f32[576,1536]{1,0:T(8,128)}, f32[192,1536]{1,0:T(8,128)}, f32[192,2560]{1,0:T(8,128)}, f32[128,1536]{1,0:T(8,128)...) custom-call(bf16[8,192,512]{2,1,0:T(8,128)(2,1)} %get-tuple-element., ...), custom_call_target="tpu_custom_call" | custom-call | tf_op jit(solution)/shard_map/final_order/pallas_call | solution.py:1730

commit v9 on v8

--- a/solution.py
+++ b/solution.py
@@ -648,6 +648,8 @@
             (q_cols + kv_cols, 2 * Q_COLS + 2 * HEAD_DIM, 2 * HEAD_DIM)))]
     for copy in raw_q:
         copy.start()
+    tok_load = pltpu.make_async_copy(m["tok"], m["tok_v"], m["keep"].at[19])
+    tok_load.start()
     small = m["small"][...].astype(F32)
     m["seg"][...] = jnp.broadcast_to(small[:, 512:640], (8, 128)).astype(jnp.int32)
     m["gains"][...] = jnp.concatenate(
@@ -722,12 +724,12 @@
     flip = Along(wq_slot(z, 1 - x), lambda zk: wq_slot(zk, 1 - x), m["wb_s"], m["wb_r"])
     over = remote(m["wq"].at[1 - x], wq_slot(z, x), m["wx_s"], m["wx_r"], to_x)
     over_in = remote(m["wq"].at[x], wq_slot(z, 1 - x), m["wx_s"], m["wx_r"], to_x)
-    for k in range(1, 8):
-        seg_copy(k).start()
     over.start()
     near.first()
     near.second()
     tok.start()
+    for k in range(1, 8):
+        seg_copy(k).start()
     local = [
         local_copy(2, m["wq"].at[x], wq_slot(z, x)),
         local_copy(3, m["gains"], m["gains_all"].at[own]),
@@ -965,7 +967,8 @@
     summed.middle()
     down_a.third()
     summed.finish()
-    mid = m["tok"][...].astype(F32) + summed.out[...]
+    tok_load.wait()
+    mid = m["tok_v"][...].astype(F32) + summed.out[...]
     m["mid"][...] = mid
     m["low"][...] = (mid * inverse_rms(mid) * m["g_two"][...]).astype(BF16)
     n2_all, cot_all = m["n2_v"], m["cot_v"]
@@ -1041,16 +1044,16 @@
         block[...] = (block[...].astype(F32) + slot[...].astype(F32)).astype(BF16)
 
     gate_sum.first_hop(add)
+    for i in range(4):
+        pl.when(r != i)(lambda i=i: remote(
+            spread_from(i), got_a.at[i], m["ha_s"].at[i], m["ha_r"].at[i], to_c).wait_recv())
+    down_sum.start()
     down_b.finish()
     for zk in range(4):
         hand(13, zk, m["zb"], wdb, b_sems, rows_b)
     gate_b.finish()
     gate_sum.second_hop(add)
     handed(m["zb"], wdb, b_sems, rows_b)
-    for i in range(4):
-        pl.when(r != i)(lambda i=i: remote(
-            spread_from(i), got_a.at[i], m["ha_s"].at[i], m["ha_r"].at[i], to_c).wait_recv())
-    down_sum.start()
     summed.passed()
 
     def total_in(block):
@@ -1396,7 +1399,7 @@
     da_share.forward()
 
     inputs.finish()
-    v = m["tok"][...].astype(F32)
+    v = m["tok_v"][...].astype(F32)
     dv, gain_grad = norm_back(inputs.out[...], v, inverse_rms(v), m["g_one"][...])
     m["dmid"][...] += dv
     grad_out = loaded(18, m["dmid"], m["input_grad"])
@@ -1548,7 +1551,7 @@
         "tok_all": ((8, rows, width), BF16), "cot_v": ((8, rows, width), BF16),
         "n2_v": ((8, rows, width), BF16), "db": ((8, rows, width), BF16),
         "part": ((8, rows, width), BF16),
-        "rope": ((span, 128), F32), "seg": (seg.shape, seg.dtype), "gains": (gains.shape, BF16),
+        "tok_v": (tok.shape, BF16), "rope": ((span, 128), F32), "seg": (seg.shape, seg.dtype), "gains": (gains.shape, BF16),
         "wq": ((2, own_rows, HEAD_COLS), BF16), "wq_raw": ((own_rows, 640), BF16),
         "segs_v": ((4, 8) + seg.shape, seg.dtype), "gains_v": ((8,) + gains.shape, BF16),
         "wq_v": ((width, HEAD_COLS), BF16), "wo_v": ((Q_COLS, width), BF16),
@@ -1598,7 +1601,7 @@
         functools.partial(block_kernel, names),
         name="block",
         out_shape=tuple(outs[n] for n in OUT),
-        in_specs=[ANY if n in ("cot", "wqkv", "wgu", "wd", "wo") else VMEM for n in IN],
+        in_specs=[ANY if n in ("tok", "cot", "wqkv", "wgu", "wd", "wo") else VMEM for n in IN],
         out_specs=tuple(VMEM if n == "gains_g" else ANY for n in OUT),
         scratch_shapes=list(scratch.values()) + list(sems.values()),
         compiler_params=params(0, 63),

time: 286 us -> 285 us (level)
  Pallas kernels: 283 us -> 280 us
where the time goes in v9:
time: 285 us; the launch traced here: 283 us
  Pallas kernels  280 us (98%)
    pallas_call x1, Pallas kernels, block_call(): pl.pallas_call(functools.partial(block_kernel, names), name='block', out_...  271 us
    pallas_call x1, Pallas kernels, order_call(): pl.pallas_call(functools.partial(order_kernel, names), name='final_order'...  9.32 us

profile of v9, /device:TPU:0, one launch (start us, length us, event | category | flops | bytes accessed | tf_op | source)
XLA Modules:
  0.0 282.8 jit_solution(9212143980836013375)
XLA Ops:
  0.6 0.7 convert_element_type.10
  1.3 0.8 pad_add_fusion
  2.1 0.6 reshape.35.refs_2_
  2.7 270.6 %block.1 = (bf16[128,1536]{1,0:T(8,128)(2,1)}, f32[128,1536]{1,0:T(8,128)}, f32[8,1536]{1,0:T(8,128)}, bf16[8,192,512]{2,1,0:T(8,128)(2,1)}, bf16[8,192,640]{2,1...) custom-call(bf16[128,1536]{1,0:T(8,128)(2,1)} %refs_0_.1, ...), custom_call_target="tpu_custom_call" | custom-call | tf_op jit(solution)/shard_map/block/pallas_call | solution.py:1600
  273.3 9.3 %final_order.1 = (f32[192,9216]{1,0:T(8,128)}, f32[576,1536]{1,0:T(8,128)}, f32[192,1536]{1,0:T(8,128)}, f32[192,2560]{1,0:T(8,128)}, f32[128,1536]{1,0:T(8,128)...) custom-call(bf16[8,192,512]{2,1,0:T(8,128)(2,1)} %get-tuple-element., ...), custom_call_target="tpu_custom_call" | custom-call | tf_op jit(solution)/shard_map/final_order/pallas_call | solution.py:1733

commit v10 on v9

--- a/solution.py
+++ b/solution.py
@@ -1314,7 +1314,7 @@
     inputs = SeqSum(parts, [m[n] for n in SUM_NAMES], by_x=True)
 
     def finish_one(k, carry):
-        b, e = (y + (k + 1) // 2) % 2, (c + 1 + k // 2) % 2
+        b, e = order_back(k)
         s = 2 * b + e
         @pl.when(z < 3)
         def _():

time: 285 us -> 286 us (level)
  no operation moved by 1% of the time
where the time goes in v10:
time: 286 us; the launch traced here: 285 us
  Pallas kernels  282 us (99%)
    pallas_call x1, Pallas kernels, block_call(): pl.pallas_call(functools.partial(block_kernel, names), name='block', out_...  272 us
    pallas_call x1, Pallas kernels, order_call(): pl.pallas_call(functools.partial(order_kernel, names), name='final_order'...  9.32 us

profile of v10, /device:TPU:0, one launch (start us, length us, event | category | flops | bytes accessed | tf_op | source)
XLA Modules:
  0.0 284.6 jit_solution(12639773301685786888)
XLA Ops:
  0.6 0.7 convert_element_type.10
  1.3 0.8 pad_add_fusion
  2.1 0.6 reshape.35.refs_2_
  2.7 272.5 %block.1 = (bf16[128,1536]{1,0:T(8,128)(2,1)}, f32[128,1536]{1,0:T(8,128)}, f32[8,1536]{1,0:T(8,128)}, bf16[8,192,512]{2,1,0:T(8,128)(2,1)}, bf16[8,192,640]{2,1...) custom-call(bf16[128,1536]{1,0:T(8,128)(2,1)} %refs_0_.1, ...), custom_call_target="tpu_custom_call" | custom-call | tf_op jit(solution)/shard_map/block/pallas_call | solution.py:1600
  275.1 9.3 %final_order.1 = (f32[192,9216]{1,0:T(8,128)}, f32[576,1536]{1,0:T(8,128)}, f32[192,1536]{1,0:T(8,128)}, f32[192,2560]{1,0:T(8,128)}, f32[128,1536]{1,0:T(8,128)...) custom-call(bf16[8,192,512]{2,1,0:T(8,128)(2,1)} %get-tuple-element., ...), custom_call_target="tpu_custom_call" | custom-call | tf_op jit(solution)/shard_map/final_order/pallas_call | solution.py:1733
